TPU v7x, 256 devices: a whole 4x4x8 slice. The times are simulated.
256 devices in a mesh: occ: 32 (over z, x_lo, core), aux: 8 (over x_hi, y).
Axes of the slice: x: 4 (x_hi: 2, x_lo: 2; x = x_hi * 2 + x_lo), y: 4, z: 8, core: 2. Of those that a mesh axis runs over, the one named last changes fastest.
Arguments:
- b_factor: bfloat16 [1024, 16, 49152], P('occ', None, 'aux'), may hold values from -0.40234375 to 0.40234375
- occ_energy: float32 [1024], P('occ'), may hold values from -3 to -0.5
- virt_energy: float32 [16], replicated, may hold values from 0.2 to 4
Outputs:
- gamma: bfloat16 [1024, 16, 49152], P('occ', None, 'aux')
All inputs are finite; a program needn't handle non-finite values.
Results may differ from a plain program's by a relative error of at most 0.022.
Values may be sent and summed in bfloat16 or wider, within the bound.
No kernel may reach another device: no remote copies, remote signals or barrier semaphores. Data moves between devices by JAX's collectives and lax.ppermute only.
A program may use at most 128 MiB of HBM per device.

v0:
```python
import jax
import jax.numpy as jnp
from jax import lax
from jax.sharding import PartitionSpec as P


def passed_along(array, axis, by):
    size = lax.axis_size(axis)
    return lax.ppermute(array, axis, [(i, (i + by) % size) for i in range(size)])


def amplitudes(integrals_flat, own_energy, partner_energy, virt_energy):
    row_count = own_energy.shape[0]
    slab_width = virt_energy.shape[0]
    integrals = integrals_flat.reshape(row_count, slab_width, partner_energy.shape[0], slab_width)
    denominator = (
        own_energy[:, None, None, None]
        + partner_energy[None, None, :, None]
        - virt_energy[None, :, None, None]
        - virt_energy[None, None, None, :]
    )
    amplitude = (2.0 * integrals - integrals.transpose(0, 3, 2, 1)) / denominator
    return amplitude.astype(jnp.bfloat16).reshape(
        row_count * slab_width, partner_energy.shape[0] * slab_width
    )


def per_device(b_factor, occ_energy, virt_energy):
    occ_rows, slab_width, aux_cols = b_factor.shape
    own_rows = b_factor.reshape(occ_rows * slab_width, aux_cols)
    near_block = (
        passed_along(b_factor, "occ", 1),
        passed_along(occ_energy.astype(jnp.bfloat16), "occ", 1).astype(occ_energy.dtype),
    )
    far_block = (
        passed_along(near_block[0], "occ", 1),
        passed_along(near_block[1].astype(jnp.bfloat16), "occ", 1).astype(jnp.float32),
    )
    gamma_sum = jnp.zeros((occ_rows * slab_width, aux_cols), jnp.float32)
    for partner in (near_block, far_block):
        partner_rows = partner[0].reshape(occ_rows * slab_width, aux_cols)
        partial_value = lax.dot_general(
            own_rows, partner_rows, (((1,), (1,)), ((), ())), preferred_element_type=jnp.float32
        )
        summed = lax.psum(partial_value.astype(jnp.bfloat16), "aux").astype(jnp.float32)
        amplitude = amplitudes(summed, occ_energy, partner[1], virt_energy)
        gamma_sum = gamma_sum + jnp.dot(amplitude, partner_rows, preferred_element_type=jnp.float32)
    return gamma_sum.astype(jnp.bfloat16).reshape(occ_rows, slab_width, aux_cols)


def solution(mesh):
    placed = (P("occ", None, "aux"), P("occ"), P())
    return jax.shard_map(
        per_device, mesh=mesh, in_specs=placed, out_specs=P("occ", None, "aux"), check_vma=False
    )
```

profile of v0, /device:TPU:2, one launch (start us, length us, event | category | flops | bytes accessed | tf_op | source)
XLA Modules:
  0.0 341.6 jit_solution(15911453921908334909)
XLA Ops:
  6.5 70.7 %collective-permute-done = bf16[32,16,6144]{2,1,0:T(8,128)(2,1)} collective-permute-done((bf16[32,16,6144]{2,1,0:T(8,128)(2,1)}, bf16[32,16,6144]{2,1,0:T(8,128)(2,1)}, u32[]{:S(2)}, u32[]{:S(2)}) %collective-permute-start) | collective-permute-done | bytes 6291488 | tf_op jit(solution)/shard_map/ppermute | solution.py:9
  77.3 8.0 %convolution_convert_fusion.1 = bf16[512,512]{1,0:T(8,128)(2,1)S(1)} fusion(bf16[512,6144]{1,0:T(8,128)(2,1)} %bitcast.26, bf16[512,6144]{1,0:T(8,128)(2,1)} %bitcast.1), kind=kOutput, calls=%fused_computation.11 | convolution fusion | flops 3221487616 | bytes 13107200 | tf_op jit(solution)/shard_map/dot_general | solution.py:42
  85.3 4.5 %reshape.102 = bf16[32,16,32,16]{3,2,1,0:T(8,128)(2,1)} reshape(bf16[512,512]{1,0:T(8,128)(2,1)S(1)} %convolution_convert_fusion.1) | data formatting | bytes 1048576 | tf_op jit(solution)/shard_map/reshape | solution.py:15
  89.8 5.0 %copy.10 = bf16[32,16,32,16]{2,1,3,0:T(8,128)(2,1)} copy(bf16[32,16,32,16]{3,2,1,0:T(8,128)(2,1)} %reshape.102) | data formatting | bytes 1048576 | tf_op jit(solution)/shard_map/reshape | solution.py:15
  94.8 53.2 %collective-permute-done.2 = bf16[32,16,6144]{2,1,0:T(8,128)(2,1)} collective-permute-done((bf16[32,16,6144]{2,1,0:T(8,128)(2,1)}, bf16[32,16,6144]{2,1,0:T(8,128)(2,1)}, u32[]{:S(2)}, u32[]{:S(2)}) %collective-permute-start.2) | collective-permute-done | bytes 6291488 | tf_op jit(solution)/shard_map/ppermute | solution.py:9
  148.0 8.0 %convolution_convert_fusion = bf16[512,512]{1,0:T(8,128)(2,1)S(1)} fusion(bf16[512,6144]{1,0:T(8,128)(2,1)} %bitcast.27, bf16[512,6144]{1,0:T(8,128)(2,1)} %bitcast.3), kind=kOutput, calls=%fused_computation.10 | convolution fusion | flops 3221487616 | bytes 13107200 | tf_op jit(solution)/shard_map/dot_general | solution.py:42
  156.0 4.5 %reshape.106 = bf16[32,16,32,16]{3,2,1,0:T(8,128)(2,1)} reshape(bf16[512,512]{1,0:T(8,128)(2,1)S(1)} %convolution_convert_fusion) | data formatting | bytes 1048576 | tf_op jit(solution)/shard_map/reshape | solution.py:15
  160.5 4.8 %copy.13 = bf16[32,16,32,16]{2,3,1,0:T(8,128)(2,1)} copy(bf16[32,16,32,16]{3,2,1,0:T(8,128)(2,1)} %reshape.106) | data formatting | bytes 1048576 | tf_op jit(solution)/shard_map/reshape | solution.py:15
  165.3 0.5 collective-permute-start.1
  165.8 2.5 collective-permute-done.1
  168.4 1.6 collective-permute-start.3
  169.9 4.6 %collective-permute-done.3 = bf16[32]{0:T(256)(128)(2,1)S(1)} collective-permute-done((bf16[32]{0:T(256)(128)(2,1)S(1)}, bf16[32]{0:T(256)(128)(2,1)S(1)}, u32[]{:S(2)}, u32[]{:S(2)}) %collective-permute-start.3) | collective-permute-done | bytes 96 | tf_op jit(solution)/shard_map/ppermute | solution.py:9
  174.5 0.1 broadcast_add_fusion
  174.6 0.1 broadcast_subtract_fusion
  174.7 112.2 %all-reduce.3.cloned.1.call-done = (bf16[32,16,32,16]{2,1,3,0:T(8,128)(2,1)}, bf16[32,16,32,16]{2,3,1,0:T(8,128)(2,1)}) async-done(((bf16[32,16,32,16]{2,1,3,0:T(8,128)(2,1)}, bf16[32,16,32,16]{2,3,1,0:T(8,128)(2,1)}), (bf16[32,16,32,16]{2,1,3,0:T(8,128)(2,1)}, bf16[32,16,32,16]{2,3,1,0:T(8,128)(2,1)})) %all-reduce.3.cloned.1.call-update) | async-done | bytes 1048592 | tf_op jit(solution)/shard_map/psum | solution.py:45
  286.9 2.2 reshape.107
  289.1 2.4 convert_multiply_fusion
  291.5 5.8 %fusion.3 = (bf16[32,16,32,16]{2,3,1,0:T(8,128)(2,1)}, bf16[32,16,32,16]{2,3,1,0:T(8,128)(2,1)S(1)}) fusion(f32[32,16,32,16]{2,1,3,0:T(8,128)S(1)} %get-tuple-element.14, f32[32,16,32]{2,1,0:T(8,128)S(1)} %get-tuple-element.9, f32[16]{0:T(128)S(1)} %copy-done.1, f32[32,16,32]{2,1,0:T(8,128)S(1)} %get-tuple-element.10, ...), kind=kLoop, calls=%fused_computation.8 | loop fusion | flops 2097152 | bytes 3801152 | tf_op jit(solution)/shard_map/convert_element_type | solution.py:23
  297.3 4.8 %copy.16 = bf16[32,16,32,16]{3,2,1,0:T(8,128)(2,1)} copy(bf16[32,16,32,16]{2,3,1,0:T(8,128)(2,1)} %get-tuple-element.7) | data formatting | bytes 1048576 | tf_op jit(solution)/shard_map/convert_element_type | solution.py:23
  302.1 7.8 %reshape.108 = bf16[512,512]{1,0:T(8,128)(2,1)S(1)} reshape(bf16[32,16,32,16]{3,2,1,0:T(8,128)(2,1)} %copy.16) | data formatting | bytes 1048576 | tf_op jit(solution)/shard_map/reshape | solution.py:23
  309.9 3.2 copy.12
  313.1 7.8 %reshape.104 = bf16[512,512]{1,0:T(8,128)(2,1)S(1)} reshape(bf16[32,16,32,16]{3,2,1,0:T(8,128)(2,1)} %copy.12) | data formatting | bytes 1048576 | tf_op jit(solution)/shard_map/reshape | solution.py:23
  320.8 5.5 %fusion.4 = f32[512,6144]{1,0:T(8,128)S(1)} fusion(bf16[512,512]{1,0:T(8,128)(2,1)S(1)} %reshape.104, bf16[512,6144]{1,0:T(8,128)(2,1)} %bitcast.1), kind=kOutput, calls=%fused_computation.16 | convolution fusion | flops 3221225472 | bytes 19398656 | tf_op jit(solution)/shard_map/dot_general | solution.py:47
  326.4 8.4 %add_convert_fusion = bf16[512,6144]{1,0:T(8,128)(2,1)} fusion(f32[512,6144]{1,0:T(8,128)S(1)} %fusion.4, bf16[512,512]{1,0:T(8,128)(2,1)S(1)} %reshape.108, bf16[512,6144]{1,0:T(8,128)(2,1)} %bitcast.3), kind=kOutput, calls=%fused_computation | convolution fusion | flops 3227516928 | bytes 25690112 | tf_op jit(solution)/shard_map/dot_general | solution.py:47
  (13 shorter events, 0.0 us)
Async XLA Ops:
  6.5 280.3 %all-reduce.3.cloned.1.call-start = ((), (), s32[]{:S(2)}) async-start(), calls=%async_computation | async-start | bytes 8388608 | tf_op jit(solution)/shard_map/psum | solution.py:45
  6.5 70.7 %collective-permute-start = (bf16[32,16,6144]{2,1,0:T(8,128)(2,1)}, bf16[32,16,6144]{2,1,0:T(8,128)(2,1)}, u32[]{:S(2)}, u32[]{:S(2)}) collective-permute-start(bf16[32,16,6144]{2,1,0:T(8,128)(2,1)} %param.3), channel_id=1, source_target_pairs={{0,8},{8,16},{16,24},{24,32},{32,40},{40,48},{48,56},{56,64},{64,7... | collective-permute-start | bytes 18874376 | tf_op jit(solution)/shard_map/ppermute | solution.py:9
  77.3 70.7 %collective-permute-start.2 = (bf16[32,16,6144]{2,1,0:T(8,128)(2,1)}, bf16[32,16,6144]{2,1,0:T(8,128)(2,1)}, u32[]{:S(2)}, u32[]{:S(2)}) collective-permute-start(bf16[32,16,6144]{2,1,0:T(8,128)(2,1)} %collective-permute-done), channel_id=1, source_target_pairs={{0,8},{8,16},{16,24},{24,32},{32,40},{40,48},{48,56},{56,64},{64,7... | collective-permute-start | bytes 18874376 | tf_op jit(solution)/shard_map/ppermute | solution.py:9
  160.5 4.8 %copy-start.2 = (f32[32]{0:T(128)S(1)}, f32[32]{0:T(128)}, u32[]{:S(2)}) copy-start(f32[32]{0:T(128)} %param.4) | copy-start | bytes 388
  160.5 14.1 %copy-start.1 = (f32[16]{0:T(128)S(1)}, f32[16]{0:T(128)}, u32[]{:S(2)}) copy-start(f32[16]{0:T(128)} %param.5) | copy-start | bytes 196
  165.3 3.0 collective-permute-start.1
  168.4 6.1 %collective-permute-start.3 = (bf16[32]{0:T(256)(128)(2,1)S(1)}, bf16[32]{0:T(256)(128)(2,1)S(1)}, u32[]{:S(2)}, u32[]{:S(2)}) collective-permute-start(bf16[32]{0:T(256)(128)(2,1)S(1)} %collective-permute-done.1), channel_id=1, source_target_pairs={{0,8},{8,16},{16,24},{24,32},{32,40},{40,48},{48,56},{56,64},{64,7... | collective-permute-start | bytes 200 | tf_op jit(solution)/shard_map/ppermute | solution.py:9
  286.8 2.3 copy-start
Sparse Core Ops, SparseCore 0:
  165.4 121.3 all-reduce.2
where the time goes:
time: 344 us; the launch traced here: 342 us
  waiting for transfers between devices  243 us (71%)
  local copies, waits for them, and re-layouts  42.3 us (12%)
  matrix products  30 us (9%)
  between operations  13.5 us (4%)
  other arithmetic  10.6 us (3%)
    ppermute x4, waiting for transfers between devices, passed_along(): lax.ppermute(array, axis, [(i, (i + by) % size) for i in range(size)])  131 us
    psum x1, waiting for transfers between devices, per_device(): lax.psum(partial_value.astype(jnp.bfloat16), 'aux').astype(jnp.float32)  112 us
    reshape x4, local copies, waits for them, and re-layouts, amplitudes(): integrals_flat.reshape(row_count, slab_width, partner_energy.shape[0], sl...  18.7 us
    dot_general x2, matrix products, per_device(): lax.dot_general(own_rows, partner_rows, (((1,), (1,)), ((), ())), preferr...  16.1 us
    reshape x2, local copies, waits for them, and re-layouts, amplitudes(): amplitude.astype(jnp.bfloat16)  15.5 us
    dot_general x2, matrix products, per_device(): jnp.dot(amplitude, partner_rows, preferred_element_type=jnp.float32)  13.9 us
    convert_element_type x2, local copies, waits for them, and re-layouts, amplitudes(): amplitude.astype(jnp.bfloat16)  7.99 us
  transfers between devices with their start and end apart: 5, of which 5 were waited for; matrix products, arithmetic and copies ran while one was open for 5% of the time, Pallas kernels for 0%

commit v1 on v0

v1 whole, which is shorter than its diff:
```python
import functools

import jax
import jax.numpy as jnp
from jax import lax
from jax.experimental import pallas as pl
from jax.experimental.pallas import tpu as pltpu
from jax.sharding import PartitionSpec as P

VMEM_BYTES = 40 * 1024 * 1024


def after(value, *earlier):
    return lax.optimization_barrier((value,) + earlier)[0]


def stacked(refs):
    blocks = [ref[...] for ref in refs]
    return blocks[0] if len(blocks) == 1 else jnp.concatenate(blocks, axis=0)


def product_kernel(n_left, n_right, at_ref, *refs):
    left, right = refs[:n_left], refs[n_left:n_left + n_right]
    out_ref, total = refs[n_left + n_right:]
    step = pl.program_id(0)
    term = lax.dot_general(
        stacked(left), stacked(right), (((1,), (1,)), ((), ())), preferred_element_type=jnp.float32
    )

    @pl.when(step == 0)
    def _():
        total[...] = term

    @pl.when(step > 0)
    def _():
        total[...] += term

    @pl.when(step == pl.num_programs(0) - 1)
    def _():
        out_ref[...] = total[...].astype(out_ref.dtype)


def products(left, right, left_at, right_at, depth, tile):
    rows = sum(array.shape[0] for array in left)
    cols = sum(array.shape[0] for array in right)
    offsets = jnp.stack([jnp.asarray(left_at, jnp.int32), jnp.asarray(right_at, jnp.int32)])
    return pl.pallas_call(
        functools.partial(product_kernel, len(left), len(right)),
        out_shape=jax.ShapeDtypeStruct((rows, cols), jnp.bfloat16),
        grid_spec=pltpu.PrefetchScalarGridSpec(
            num_scalar_prefetch=1,
            grid=(depth // tile,),
            in_specs=[pl.BlockSpec((a.shape[0], tile), lambda c, at: (0, at[0] + c)) for a in left]
            + [pl.BlockSpec((a.shape[0], tile), lambda c, at: (0, at[1] + c)) for a in right],
            out_specs=pl.BlockSpec((rows, cols), lambda c, at: (0, 0)),
            scratch_shapes=[pltpu.VMEM((rows, cols), jnp.float32)],
        ),
        compiler_params=pltpu.CompilerParams(vmem_limit_bytes=VMEM_BYTES),
        cost_estimate=pl.CostEstimate(
            flops=2 * rows * cols * depth, bytes_accessed=2 * (rows + cols) * depth, transcendentals=0
        ),
        name="products",
    )(offsets, *left, *right)


def swapped(x, width):
    rows, cols = x.shape
    r = lax.broadcasted_iota(jnp.int32, x.shape, 0)
    c = lax.broadcasted_iota(jnp.int32, x.shape, 1)
    s = 1
    while s < width:
        below = pltpu.roll(pltpu.roll(x, rows - s, 0), s, 1)
        above = pltpu.roll(pltpu.roll(x, s, 0), cols - s, 1)
        r_bit, c_bit = (r & s) != 0, (c & s) != 0
        x = jnp.where(r_bit == c_bit, x, jnp.where(c_bit, below, above))
        s *= 2
    return x


def amplitude_kernel(width, parts_ref, other_ref, row_ref, col_ref, out_ref):
    x = other_ref[...]
    for part in range(parts_ref.shape[0]):
        x = x + parts_ref[part].astype(jnp.float32)
    out_ref[...] = ((2.0 * x - swapped(x, width)) / (row_ref[...] + col_ref[...])).astype(out_ref.dtype)


def amplitudes(parts, other, row, col, width):
    return pl.pallas_call(
        functools.partial(amplitude_kernel, width),
        out_shape=jax.ShapeDtypeStruct(other.shape, jnp.bfloat16),
        compiler_params=pltpu.CompilerParams(vmem_limit_bytes=VMEM_BYTES),
        cost_estimate=pl.CostEstimate(flops=60 * other.size, bytes_accessed=2 * parts.size, transcendentals=0),
        name="amplitudes",
    )(parts, other, row, col)


def density_kernel(n_late, at_ref, amp_early, amp_late, early, *refs):
    late, out_ref = refs[:n_late], refs[-1]
    total = jnp.dot(amp_early[...], early[...], preferred_element_type=jnp.float32)
    total = total + jnp.dot(amp_late[...], stacked(late), preferred_element_type=jnp.float32)
    out_ref[...] = total.astype(out_ref.dtype)


def density(out, amp_early, amp_late, early, late, at, tile):
    rows, width = early.shape
    cols = late[0].shape[1]
    in_specs = [
        pl.BlockSpec(amp_early.shape, lambda c, at: (0, 0)),
        pl.BlockSpec(amp_late.shape, lambda c, at: (0, 0)),
        pl.BlockSpec((rows, tile), lambda c, at: (0, c)),
    ] + [pl.BlockSpec((a.shape[0], tile), lambda c, at: (0, at[0] + c)) for a in late]
    operands = [jnp.reshape(at, (1,)).astype(jnp.int32), amp_early, amp_late, early, *late]
    aliases = {}
    if out is not None:
        in_specs.append(pl.BlockSpec(memory_space=pl.ANY))
        aliases = {len(operands): 0}
        operands.append(out)
    return pl.pallas_call(
        functools.partial(density_kernel, len(late)),
        out_shape=jax.ShapeDtypeStruct((amp_early.shape[0], cols), jnp.bfloat16),
        grid_spec=pltpu.PrefetchScalarGridSpec(
            num_scalar_prefetch=1,
            grid=(width // tile,),
            in_specs=in_specs,
            out_specs=pl.BlockSpec((amp_early.shape[0], tile), lambda c, at: (0, at[0] + c)),
        ),
        input_output_aliases=aliases,
        compiler_params=pltpu.CompilerParams(vmem_limit_bytes=VMEM_BYTES),
        cost_estimate=pl.CostEstimate(
            flops=4 * rows * rows * width, bytes_accessed=6 * rows * width, transcendentals=0
        ),
        name="density",
    )(*operands)


def per_device(b_factor, occ_energy, virt_energy):
    occ_rows, slab, cols = b_factor.shape
    rows, half = occ_rows * slab, cols // 2
    n_occ, n_aux = lax.axis_size("occ"), lax.axis_size("aux")
    p, q = lax.axis_index("occ"), lax.axis_index("aux")
    core, parity = p % 2, (p // 2) % 2
    own_rows = rows // n_aux
    depth_tile, out_tile = cols // 6, cols // 24
    n_o, n_e = 4, 2

    ring = [(i, (i + 1) % n_occ) for i in range(n_occ)]
    in_chip = [(i, i + 1) for i in range(0, n_occ, 2)]
    to_next_chip = [(i, (i + 1) % n_occ) for i in range(1, n_occ, 2)]
    chip_before_last = [(i, (i - 4) % n_occ) for i in range(0, n_occ, 2)]
    evens_to_next = [(i, (i + 2) % n_occ) for i in range(0, n_occ, 2)]

    def send(value, pairs):
        return lax.ppermute(value, "occ", pairs)

    own = b_factor.reshape(rows, cols)
    energy_near = send(occ_energy, ring)
    energy_far = send(occ_energy, [(i, (i + 2) % n_occ) for i in range(n_occ)])

    even = send(own, in_chip)
    first = core == 0
    even_source = jnp.where(first, own, even)
    early_half = (parity + core + 1) % 2
    o_rows, e_rows = rows // n_o, rows // n_e

    def odd_part(part, *earlier):
        return send(after(own[part * o_rows:(part + 1) * o_rows], *earlier), to_next_chip)

    def early_part(part, *earlier):
        block = lax.dynamic_slice(even_source, (part * e_rows, parity * half), (e_rows, half))
        return send(after(block, *earlier), ring)

    def last_part(start, size, *earlier):
        block = lax.dynamic_slice(even_source, (0, (1 - parity) * half + start), (rows, size))
        return send(after(block, *earlier), ring)

    odd = [odd_part(0)]
    early = [early_part(0), early_part(1, odd[0])]
    odd.append(odd_part(1, early[0]))
    odd.append(odd_part(2, early[1]))
    odd.append(odd_part(3, odd[1]))
    sizes = (half // 2, half // 4, half // 4)
    last = [last_part(0, sizes[0], odd[2])]
    last.append(last_part(sizes[0], sizes[1], odd[3]))
    last.append(last_part(sizes[0] + sizes[1], sizes[2], last[0]))

    back = [send(part, chip_before_last) for part in early]
    partner = [jnp.where(first, part, send(part, in_chip)) for part in odd]

    half_tiles = half // depth_tile
    near_half = products([own], early, early_half * half_tiles, 0, half, depth_tile)
    far_half = lax.cond(
        first,
        lambda: products(back, [own], 0, early_half * half_tiles, half, depth_tile),
        lambda: products(
            [own], [even], (1 - early_half) * half_tiles, (1 - early_half) * half_tiles, half, depth_tile
        ),
    )

    def spread(value):
        return lax.all_to_all(value.reshape(n_aux, own_rows, rows), "aux", 0, 0)

    near_parts = spread(near_half)
    far_sum = spread(far_half).astype(jnp.float32).sum(0)
    other = jnp.where(first, send(far_sum, evens_to_next), far_sum)

    row = (occ_energy[:, None] - virt_energy[None, :]).reshape(rows, 1)
    row = lax.dynamic_slice(row, (q * own_rows, 0), (own_rows, 1))

    def partner_energy(near):
        energy = jnp.where(near, energy_near, energy_far)
        return (energy[:, None] - virt_energy[None, :]).reshape(1, rows)

    amp_even = amplitudes(near_parts, other, row, partner_energy(core == 1), slab)
    amp_even = lax.all_gather(amp_even, "aux", axis=0, tiled=True)

    odd_products = jnp.concatenate(
        [products([own], partner[:2], 0, 0, cols, depth_tile), products([own], partner[2:], 0, 0, cols, depth_tile)],
        axis=1,
    )
    amp_odd = amplitudes(
        spread(odd_products), jnp.zeros((own_rows, rows), jnp.float32), row, partner_energy(first), slab
    )
    amp_odd = lax.all_gather(amp_odd, "aux", axis=0, tiled=True)

    tiles = half // out_tile
    early_block = jnp.concatenate(early, axis=0)
    gamma = density(None, amp_even, amp_odd, early_block, partner, early_half * tiles, out_tile)
    start = 0
    for block, size in zip(last, sizes):
        at = (1 - early_half) * tiles + start // out_tile
        gamma = density(gamma, amp_even, amp_odd, block, partner, at, out_tile)
        start += size
    return gamma.reshape(occ_rows, slab, cols)


def solution(mesh):
    placed = (P("occ", None, "aux"), P("occ"), P())
    return jax.shard_map(
        per_device, mesh=mesh, in_specs=placed, out_specs=P("occ", None, "aux"), check_vma=False
    )
```

time: 344 us -> 311 us (0.904)
  waiting for transfers between devices: 243 us -> 66.8 us
  blocking collectives: 0 us -> 88.7 us
  starting transfers between devices: 2.07 us -> 70.2 us
  Pallas kernels: 0 us -> 46.5 us
  matrix products: 30 us -> 0 us
  local copies, waits for them, and re-layouts: 42.3 us -> 20.3 us
  between operations: 13.5 us -> 0.46 us
  other arithmetic: 10.6 us -> 16.2 us
    psum x1 -> x0, waiting for transfers between devices: 112 us -> none  [per_device(): lax.psum(partial_value.astype(jnp.bfloat16), 'aux').astype(jnp.float32)]
    all_gather x0 -> x2, blocking collectives: none -> 88.7 us  [the longest x1 53.5 us: per_device(): amp_even = lax.all_gather(amp_even, 'aux', axis=0, tiled=True)]
    ppermute x4 -> x19, waiting for transfers between devices: 131 us -> 66.5 us  [send(): return lax.ppermute(value, 'occ', pairs)]
    ppermute x4 -> x19, starting transfers between devices: 2.07 us -> 51.3 us  [send(): return lax.ppermute(value, 'occ', pairs)]
    pallas_call x0 -> x10, Pallas kernels: none -> 46.5 us  [the longest x4 22.3 us: products(): pl.pallas_call(functools.partial(product_kernel, len(left), len(right)),...]
    reshape x6 -> x0, local copies, waits for them, and re-layouts: 34.3 us -> none  [the longest x4 18.7 us: amplitudes(): integrals_flat.reshape(row_count, slab_width, partner_energy.shape[0], sl...]
    dot_general x4 -> x0, matrix products: 30 us -> none  [the longest x2 16.1 us: per_device(): lax.dot_general(own_rows, partner_rows, (((1,), (1,)), ((), ())), preferr...]
    all_to_all x0 -> x3, starting transfers between devices: none -> 18.9 us  [spread(): return lax.all_to_all(value.reshape(n_aux, own_rows, rows), 'aux', 0, 0)]
  transfers between devices with their start and end apart: 5 -> 22, of which waited for: 5 -> 6; matrix products, arithmetic and copies ran while one was open for 5% -> 9% of each run, Pallas kernels for 0% -> 14%
where the time goes in v1:
time: 311 us; the launch traced here: 309 us
  blocking collectives  88.7 us (29%)
  starting transfers between devices  70.2 us (23%)
  waiting for transfers between devices  66.8 us (21%)
  Pallas kernels  46.5 us (15%)
  local copies, waits for them, and re-layouts  20.3 us (7%)
  other arithmetic  16.2 us (5%)
    ppermute x19, waiting for transfers between devices, send(): return lax.ppermute(value, 'occ', pairs)  66.5 us
    all_gather x1, blocking collectives, per_device(): amp_even = lax.all_gather(amp_even, 'aux', axis=0, tiled=True)  53.5 us
    ppermute x19, starting transfers between devices, send(): return lax.ppermute(value, 'occ', pairs)  51.3 us
    all_gather x1, blocking collectives, per_device(): amp_odd = lax.all_gather(amp_odd, 'aux', axis=0, tiled=True)  35.2 us
    pallas_call x4, Pallas kernels, products(): pl.pallas_call(functools.partial(product_kernel, len(left), len(right)),...  22.3 us
    pallas_call x4, Pallas kernels, density(): pl.pallas_call(functools.partial(density_kernel, len(late)), out_shape=ja...  20.9 us
    all_to_all x3, starting transfers between devices, spread(): return lax.all_to_all(value.reshape(n_aux, own_rows, rows), 'aux', 0, 0)  18.9 us
    unnamed x26, local copies, waits for them, and re-layouts  7.41 us
  transfers between devices with their start and end apart: 22, of which 6 were waited for; matrix products, arithmetic and copies ran while one was open for 9% of the time, Pallas kernels for 14%

profile of v1, /device:TPU:2, one launch (start us, length us, event | category | flops | bytes accessed | tf_op | source)
XLA Modules:
  0.0 309.3 jit_solution(6311410469590040758)
XLA Ops:
  0.0 4.4 %collective-permute-start = (bf16[512,6144]{1,0:T(8,128)(2,1)}, bf16[512,6144]{1,0:T(8,128)(2,1)}, u32[]{:S(2)}, u32[]{:S(2)}) collective-permute-start(bf16[512,6144]{1,0:T(8,128)(2,1)} %bitcast.18), channel_id=1, source_target_pairs={{0,8},{16,24},{32,40},{48,56},{64,72},{80,88},{96,104},{112,120},{... | collective-permute-start | bytes 18874376 | tf_op jit(solution)/shard_map/ppermute | solution.py:153
  4.4 5.7 %fusion = (bf16[8,16,6144]{2,1,0:T(8,128)(2,1)}, bf16[8,16,6144]{2,1,0:T(8,128)(2,1)}, bf16[8,16,6144]{2,1,0:T(8,128)(2,1)}, bf16[8,16,6144]{2,1,0:T(8,128)(2,1)}) fusion(bf16[32,16,6144]{2,1,0:T(8,128)(2,1)} %param.5), kind=kLoop, calls=%fused_computation.23 | loop fusion | bytes 12582912 | tf_op jit(solution)/shard_map/slice | solution.py:166
  18.5 5.1 %collective-permute-start.1 = (bf16[256,3072]{1,0:T(8,128)(2,1)S(1)}, bf16[256,3072]{1,0:T(8,128)(2,1)S(1)}, u32[]{:S(2)}, u32[]{:S(2)}) collective-permute-start(bf16[256,3072]{1,0:T(8,128)(2,1)S(1)} %get-tuple-element.50), channel_id=1, source_target_pairs={{0,8},{8,16},{16,24},{24,32},{32,40},{40,48},{48,56},{56,64},{64,7... | collective-permute-start | bytes 4718600 | tf_op jit(solution)/shard_map/ppermute | solution.py:153
  23.6 8.6 %collective-permute-done.2 = bf16[128,6144]{1,0:T(8,128)(2,1)} collective-permute-done((bf16[128,6144]{1,0:T(8,128)(2,1)}, bf16[128,6144]{1,0:T(8,128)(2,1)}, u32[]{:S(2)}, u32[]{:S(2)}) %collective-permute-start.2) | collective-permute-done | bytes 1572896 | tf_op jit(solution)/shard_map/ppermute | solution.py:153
  32.1 16.7 %collective-permute-done.1.refs_1_ = bf16[256,3072]{1,0:T(8,128)(2,1)S(1)} collective-permute-done((bf16[256,3072]{1,0:T(8,128)(2,1)S(1)}, bf16[256,3072]{1,0:T(8,128)(2,1)S(1)}, u32[]{:S(2)}, u32[]{:S(2)}) %collective-permute-start.1) | collective-permute-done | bytes 1572896 | tf_op jit(solution)/shard_map/ppermute | solution.py:153
  50.2 6.7 %collective-permute-start.9 = (bf16[128,6144]{1,0:T(8,128)(2,1)}, bf16[128,6144]{1,0:T(8,128)(2,1)S(1)}, u32[]{:S(2)}, u32[]{:S(2)}) collective-permute-start(bf16[128,6144]{1,0:T(8,128)(2,1)} %collective-permute-done.2), channel_id=1, source_target_pairs={{0,8},{16,24},{32,40},{48,56},{64,72},{80,88},{96,104},{112,120},{... | collective-permute-start | bytes 4718600 | tf_op jit(solution)/shard_map/ppermute | solution.py:153
  57.7 25.0 %collective-permute-done.7 = f32[32]{0:T(128)S(1)} collective-permute-done((f32[32]{0:T(128)S(1)}, f32[32]{0:T(128)S(1)}, u32[]{:S(2)}, u32[]{:S(2)}) %collective-permute-start.7) | collective-permute-done | bytes 160 | tf_op jit(solution)/shard_map/ppermute | solution.py:153
  84.5 7.8 %collective-permute-start.4 = (bf16[256,3072]{1,0:T(8,128)(2,1)S(1)}, bf16[256,3072]{1,0:T(8,128)(2,1)}, u32[]{:S(2)}, u32[]{:S(2)}) collective-permute-start(bf16[256,3072]{1,0:T(8,128)(2,1)S(1)} %collective-permute-done.1.refs_1_), channel_id=1, source_target_pairs={{0,224},{16,240},{32,0},{48,16},{64,32},{80,48},{96,64},{112,80},{... | collective-permute-start | bytes 4718600 | tf_op jit(solution)/shard_map/ppermute | solution.py:153
  97.6 6.9 %collective-permute-start.11 = (bf16[128,6144]{1,0:T(8,128)(2,1)}, bf16[128,6144]{1,0:T(8,128)(2,1)}, u32[]{:S(2)}, u32[]{:S(2)}) collective-permute-start(bf16[128,6144]{1,0:T(8,128)(2,1)} %collective-permute-done.10), channel_id=1, source_target_pairs={{0,8},{16,24},{32,40},{48,56},{64,72},{80,88},{96,104},{112,120},{... | collective-permute-start | bytes 4718600 | tf_op jit(solution)/shard_map/ppermute | solution.py:153
  111.3 15.8 %collective-permute-done.5 = bf16[256,3072]{1,0:T(8,128)(2,1)} collective-permute-done((bf16[256,3072]{1,0:T(8,128)(2,1)}, bf16[256,3072]{1,0:T(8,128)(2,1)}, u32[]{:S(2)}, u32[]{:S(2)}) %collective-permute-start.5) | collective-permute-done | bytes 1572896 | tf_op jit(solution)/shard_map/ppermute | solution.py:153
  127.1 6.2 %conditional.1 = (bf16[512,512]{1,0:T(8,128)(2,1)}) conditional(s32[]{:T(128)} %convert_element_type.6, (s32[]{:T(128)}, bf16[512,6144]{1,0:T(8,128)(2,1)}, bf16[512,6144]{1,0:T(8,128)(2,1)}) %tuple.37, (s32[]{:T(128)}, bf16[256,3072]{1,0:T(8,128)(2,1)}, bf16[256,3072]{1,0:T(8,128)(2,1)}, bf16[512,6144]{1,0:T(8,128)(2,1)}) %tuple.38), branch_computations={%region_0.1_spmd, %region_1.2_spmd} | conditional | flops 1610612736 | bytes 6291500 | solution.py:191
  127.2 6.1 %products.6 = bf16[512,512]{1,0:T(8,128)(2,1)} custom-call(s32[2]{0:T(128)S(1)} %pad_add_fusion.1.at_ref, bf16[256,3072]{1,0:T(8,128)(2,1)} %get-tuple-element.26.refs_0_, bf16[256,3072]{1,0:T(8,128)(2,1)} %get-tuple-element.27.refs_1_, bf16[512,6144]{1,0:T(8,128)(2,1)} %get-tuple-element.28.refs_2_), custom_call_target="tpu_custom_call" | custom-call | flops 1610612736 | bytes 6291456 | tf_op jit(solution)/shard_map/cond/branch_1_fun/products/pallas_call | solution.py:47
  133.3 6.0 %all-to-all-start.1 = ((bf16[8,64,512]{2,1,0:T(8,128)(2,1)}), bf16[8,64,512]{2,1,0:T(8,128)(2,1)}, u32[]{:S(2)}, u32[]{:S(2)}) async-start(bf16[8,64,512]{2,1,0:T(8,128)(2,1)} %bitcast.26), calls=%async_computation.1 | async-start | bytes 1048576 | tf_op jit(solution)/shard_map/all_to_all | solution.py:200
  139.3 5.0 %products.7 = bf16[512,512]{1,0:T(8,128)(2,1)S(1)} custom-call(s32[2]{0:T(128)S(1)} %pad_add_fusion.2.at_ref, bf16[512,6144]{1,0:T(8,128)(2,1)} %bitcast.21, bf16[256,3072]{1,0:T(8,128)(2,1)S(1)} %collective-permute-done.1.refs_1_, bf16[256,3072]{1,0:T(8,128)(2,1)} %collective-permute-done.3.refs_2_), custom_call_target="tpu_custom_call" | custom-call | flops 1610612736 | bytes 6291456 | tf_op jit(solution)/shard_map/products/pallas_call | solution.py:47
  151.4 6.6 %all-to-all-start = ((bf16[8,64,512]{2,1,0:T(8,128)(2,1)}), bf16[8,64,512]{2,1,0:T(8,128)(2,1)}, u32[]{:S(2)}, u32[]{:S(2)}) async-start(bf16[8,64,512]{2,1,0:T(8,128)(2,1)} %bitcast.17), calls=%async_computation | async-start | bytes 1048576 | tf_op jit(solution)/shard_map/all_to_all | solution.py:200
  165.2 6.7 %products.8 = bf16[512,256]{1,0:T(8,128)(2,1)S(1)} custom-call(s32[2]{0:T(128)S(1)} %broadcast_1_at_ref.2.at_ref, bf16[512,6144]{1,0:T(8,128)(2,1)} %bitcast.22, bf16[128,6144]{1,0:T(8,128)(2,1)S(1)} %broadcast_select_fusion.4.refs_1_.refs_0_, bf16[128,6144]{1,0:T(8,128)(2,1)S(1)} %broadcast_select_fusion.3.refs_2_.refs_1_), custom_call_target="tpu_custom_call" | custom-call | flops 1610612736 | bytes 9437184 | tf_op jit(solution)/shard_map/products/pallas_call | solution.py:47
  175.7 4.5 %products.9 = bf16[512,256]{1,0:T(8,128)(2,1)S(1)} custom-call(s32[2]{0:T(128)S(1)} %broadcast_1_at_ref.2.at_ref, bf16[512,6144]{1,0:T(8,128)(2,1)S(1)} %bitcast.25, bf16[128,6144]{1,0:T(8,128)(2,1)S(1)} %broadcast_select_fusion.2.refs_1_.refs_2_, bf16[128,6144]{1,0:T(8,128)(2,1)S(1)} %broadcast_select_fusion.1.refs_2_.refs_3_), custom_call_target="tpu_custom_call" | custom-call | flops 1610612736 | bytes 9437184 | tf_op jit(solution)/shard_map/products/pallas_call | solution.py:47
  181.4 6.3 %all-to-all-start.2 = ((bf16[8,64,512]{2,1,0:T(8,128)(2,1)}), bf16[8,64,512]{2,1,0:T(8,128)(2,1)}, u32[]{:S(2)}, u32[]{:S(2)}) async-start(bf16[8,64,512]{2,1,0:T(8,128)(2,1)} %bitcast.27), calls=%async_computation.2 | async-start | bytes 1048576 | tf_op jit(solution)/shard_map/all_to_all | solution.py:200
  189.5 3.8 %collective-permute-start.18 = (bf16[512,768]{1,0:T(8,128)(2,1)}, bf16[512,768]{1,0:T(8,128)(2,1)}, u32[]{:S(2)}, u32[]{:S(2)}) collective-permute-start(bf16[512,768]{1,0:T(8,128)(2,1)} %get-tuple-element.42), channel_id=1, source_target_pairs={{0,8},{8,16},{16,24},{24,32},{32,40},{40,48},{48,56},{56,64},{64,7... | collective-permute-start | bytes 2359304 | tf_op jit(solution)/shard_map/ppermute | solution.py:153
  193.2 53.5 %all_gather.6.amp_early = bf16[512,512]{1,0:T(8,128)(2,1)} all-gather(bf16[64,512]{1,0:T(8,128)(2,1)S(1)} %amplitudes.2), channel_id=1, replica_groups=mesh['occ'=32,'aux'=8] {'aux'}, dimensions={0}, use_global_device_ids=true | all-gather | bytes 589824 | tf_op jit(solution)/shard_map/all_gather | solution.py:214
  248.4 35.2 %all_gather.7.amp_late = bf16[512,512]{1,0:T(8,128)(2,1)S(1)} all-gather(bf16[64,512]{1,0:T(8,128)(2,1)S(1)} %amplitudes.3), channel_id=1, replica_groups=mesh['occ'=32,'aux'=8] {'aux'}, dimensions={0}, use_global_device_ids=true | all-gather | bytes 589824 | tf_op jit(solution)/shard_map/all_gather | solution.py:223
  288.4 8.0 %density.4.refs_4_ = bf16[512,6144]{1,0:T(8,128)(2,1)} custom-call(s32[1]{0:T(128)} %bitcast.14.at_ref, bf16[512,512]{1,0:T(8,128)(2,1)S(1)} %copy-done.4, bf16[512,512]{1,0:T(8,128)(2,1)S(1)} %all_gather.7.amp_late, bf16[512,3072]{1,0:T(8,128)(2,1)S(1)} %copy-done.5, bf16[128,6144]{1,0:T(8,128)(2,1)S(1)} %broadcast_select_fusion.4.refs_1_.refs_0_, ...), custom_call_target="tpu_custom_call" | custom-call | flops 3221225472 | bytes 9437184 | tf_op jit(solution)/shard_map/density/pallas_call | solution.py:118
  296.4 5.7 %density.5.refs_4_ = bf16[512,6144]{1,0:T(8,128)(2,1)} custom-call(s32[1]{0:T(128)} %bitcast.13.at_ref, bf16[512,512]{1,0:T(8,128)(2,1)S(1)} %copy-done.4, bf16[512,512]{1,0:T(8,128)(2,1)S(1)} %all_gather.7.amp_late, bf16[512,1536]{1,0:T(8,128)(2,1)} %collective-permute-done.16.early, ...), custom_call_target="tpu_custom_call", output_to_operand_aliasing={{}: (8, {})} | custom-call | flops 1610612736 | bytes 4718592 | tf_op jit(solution)/shard_map/density/pallas_call | solution.py:118
  302.1 3.6 %density.6.refs_4_ = bf16[512,6144]{1,0:T(8,128)(2,1)} custom-call(s32[1]{0:T(128)} %bitcast.12.at_ref, bf16[512,512]{1,0:T(8,128)(2,1)S(1)} %copy-done.4, bf16[512,512]{1,0:T(8,128)(2,1)S(1)} %all_gather.7.amp_late, bf16[512,768]{1,0:T(8,128)(2,1)} %collective-permute-done.18.early, ...), custom_call_target="tpu_custom_call", output_to_operand_aliasing={{}: (8, {})} | custom-call | flops 805306368 | bytes 2359296 | tf_op jit(solution)/shard_map/density/pallas_call | solution.py:118
  (83 shorter events, 55.1 us)
Async XLA Ops:
  0.0 11.8 %collective-permute-start = (bf16[512,6144]{1,0:T(8,128)(2,1)}, bf16[512,6144]{1,0:T(8,128)(2,1)}, u32[]{:S(2)}, u32[]{:S(2)}) collective-permute-start(bf16[512,6144]{1,0:T(8,128)(2,1)} %bitcast.18), channel_id=1, source_target_pairs={{0,8},{16,24},{32,40},{48,56},{64,72},{80,88},{96,104},{112,120},{... | collective-permute-start | bytes 18874376 | tf_op jit(solution)/shard_map/ppermute | solution.py:153
  10.1 22.0 %collective-permute-start.2 = (bf16[128,6144]{1,0:T(8,128)(2,1)}, bf16[128,6144]{1,0:T(8,128)(2,1)}, u32[]{:S(2)}, u32[]{:S(2)}) collective-permute-start(bf16[128,6144]{1,0:T(8,128)(2,1)} %bitcast.5), channel_id=1, source_target_pairs={{8,16},{24,32},{40,48},{56,64},{72,80},{88,96},{104,112},{120,128}... | collective-permute-start | bytes 4718600 | tf_op jit(solution)/shard_map/ppermute | solution.py:153
  15.3 41.6 %copy-start.9 = (f32[32]{0:T(128)S(1)}, f32[32]{0:T(128)}, u32[]{:S(2)}) copy-start(f32[32]{0:T(128)} %param.6) | copy-start | bytes 388
  15.3 67.4 %copy-start.10 = (f32[16]{0:T(128)S(1)}, f32[16]{0:T(128)}, u32[]{:S(2)}) copy-start(f32[16]{0:T(128)} %param.7) | copy-start | bytes 196
  18.5 30.4 %collective-permute-start.1 = (bf16[256,3072]{1,0:T(8,128)(2,1)S(1)}, bf16[256,3072]{1,0:T(8,128)(2,1)S(1)}, u32[]{:S(2)}, u32[]{:S(2)}) collective-permute-start(bf16[256,3072]{1,0:T(8,128)(2,1)S(1)} %get-tuple-element.50), channel_id=1, source_target_pairs={{0,8},{8,16},{16,24},{24,32},{32,40},{40,48},{48,56},{56,64},{64,7... | collective-permute-start | bytes 4718600 | tf_op jit(solution)/shard_map/ppermute | solution.py:153
  32.1 51.0 %collective-permute-start.3 = (bf16[256,3072]{1,0:T(8,128)(2,1)}, bf16[256,3072]{1,0:T(8,128)(2,1)}, u32[]{:S(2)}, u32[]{:S(2)}) collective-permute-start(bf16[256,3072]{1,0:T(8,128)(2,1)} %get-tuple-element.36), channel_id=1, source_target_pairs={{0,8},{8,16},{16,24},{24,32},{32,40},{40,48},{48,56},{56,64},{64,7... | collective-permute-start | bytes 4718600 | tf_op jit(solution)/shard_map/ppermute | solution.py:153
  48.9 46.3 %collective-permute-start.10 = (bf16[128,6144]{1,0:T(8,128)(2,1)}, bf16[128,6144]{1,0:T(8,128)(2,1)}, u32[]{:S(2)}, u32[]{:S(2)}) collective-permute-start(bf16[128,6144]{1,0:T(8,128)(2,1)} %bitcast.8), channel_id=1, source_target_pairs={{8,16},{24,32},{40,48},{56,64},{72,80},{88,96},{104,112},{120,128}... | collective-permute-start | bytes 4718600 | tf_op jit(solution)/shard_map/ppermute | solution.py:153
  50.2 46.3 %collective-permute-start.9 = (bf16[128,6144]{1,0:T(8,128)(2,1)}, bf16[128,6144]{1,0:T(8,128)(2,1)S(1)}, u32[]{:S(2)}, u32[]{:S(2)}) collective-permute-start(bf16[128,6144]{1,0:T(8,128)(2,1)} %collective-permute-done.2), channel_id=1, source_target_pairs={{0,8},{16,24},{32,40},{48,56},{64,72},{80,88},{96,104},{112,120},{... | collective-permute-start | bytes 4718600 | tf_op jit(solution)/shard_map/ppermute | solution.py:153
  56.9 25.8 %collective-permute-start.7 = (f32[32]{0:T(128)S(1)}, f32[32]{0:T(128)S(1)}, u32[]{:S(2)}, u32[]{:S(2)}) collective-permute-start(f32[32]{0:T(128)S(1)} %copy-done.9), channel_id=1, source_target_pairs={{0,8},{8,16},{16,24},{24,32},{32,40},{40,48},{48,56},{56,64},{64,7... | collective-permute-start | bytes 392 | tf_op jit(solution)/shard_map/ppermute | solution.py:153
  57.0 25.7 %collective-permute-start.8 = (f32[32]{0:T(128)S(1)}, f32[32]{0:T(128)S(1)}, u32[]{:S(2)}, u32[]{:S(2)}) collective-permute-start(f32[32]{0:T(128)S(1)} %copy-done.9), channel_id=1, source_target_pairs={{0,16},{8,24},{16,32},{24,40},{32,48},{40,56},{48,64},{56,72},{64,... | collective-permute-start | bytes 392 | tf_op jit(solution)/shard_map/ppermute | solution.py:153
  83.2 64.7 %collective-permute-start.12 = (bf16[128,6144]{1,0:T(8,128)(2,1)}, bf16[128,6144]{1,0:T(8,128)(2,1)}, u32[]{:S(2)}, u32[]{:S(2)}) collective-permute-start(bf16[128,6144]{1,0:T(8,128)(2,1)} %bitcast.29), channel_id=1, source_target_pairs={{8,16},{24,32},{40,48},{56,64},{72,80},{88,96},{104,112},{120,128}... | collective-permute-start | bytes 4718600 | tf_op jit(solution)/shard_map/ppermute | solution.py:153
  84.5 26.9 %collective-permute-start.4 = (bf16[256,3072]{1,0:T(8,128)(2,1)S(1)}, bf16[256,3072]{1,0:T(8,128)(2,1)}, u32[]{:S(2)}, u32[]{:S(2)}) collective-permute-start(bf16[256,3072]{1,0:T(8,128)(2,1)S(1)} %collective-permute-done.1.refs_1_), channel_id=1, source_target_pairs={{0,224},{16,240},{32,0},{48,16},{64,32},{80,48},{96,64},{112,80},{... | collective-permute-start | bytes 4718600 | tf_op jit(solution)/shard_map/ppermute | solution.py:153
  92.2 34.9 %collective-permute-start.5 = (bf16[256,3072]{1,0:T(8,128)(2,1)}, bf16[256,3072]{1,0:T(8,128)(2,1)}, u32[]{:S(2)}, u32[]{:S(2)}) collective-permute-start(bf16[256,3072]{1,0:T(8,128)(2,1)} %collective-permute-done.3.refs_2_), channel_id=1, source_target_pairs={{0,224},{16,240},{32,0},{48,16},{64,32},{80,48},{96,64},{112,80},{... | collective-permute-start | bytes 4718600 | tf_op jit(solution)/shard_map/ppermute | solution.py:153
  95.2 66.8 %collective-permute-start.14 = (bf16[128,6144]{1,0:T(8,128)(2,1)}, bf16[128,6144]{1,0:T(8,128)(2,1)}, u32[]{:S(2)}, u32[]{:S(2)}) collective-permute-start(bf16[128,6144]{1,0:T(8,128)(2,1)} %bitcast.28), channel_id=1, source_target_pairs={{8,16},{24,32},{40,48},{56,64},{72,80},{88,96},{104,112},{120,128}... | collective-permute-start | bytes 4718600 | tf_op jit(solution)/shard_map/ppermute | solution.py:153
  97.6 65.7 %collective-permute-start.11 = (bf16[128,6144]{1,0:T(8,128)(2,1)}, bf16[128,6144]{1,0:T(8,128)(2,1)}, u32[]{:S(2)}, u32[]{:S(2)}) collective-permute-start(bf16[128,6144]{1,0:T(8,128)(2,1)} %collective-permute-done.10), channel_id=1, source_target_pairs={{0,8},{16,24},{32,40},{48,56},{64,72},{80,88},{96,104},{112,120},{... | collective-permute-start | bytes 4718600 | tf_op jit(solution)/shard_map/ppermute | solution.py:153
  133.3 18.1 %all-to-all-start.1 = ((bf16[8,64,512]{2,1,0:T(8,128)(2,1)}), bf16[8,64,512]{2,1,0:T(8,128)(2,1)}, u32[]{:S(2)}, u32[]{:S(2)}) async-start(bf16[8,64,512]{2,1,0:T(8,128)(2,1)} %bitcast.26), calls=%async_computation.1 | async-start | bytes 1048576 | tf_op jit(solution)/shard_map/all_to_all | solution.py:200
  147.9 41.5 %collective-permute-start.16 = (bf16[512,1536]{1,0:T(8,128)(2,1)}, bf16[512,1536]{1,0:T(8,128)(2,1)}, u32[]{:S(2)}, u32[]{:S(2)}) collective-permute-start(bf16[512,1536]{1,0:T(8,128)(2,1)} %constant_dynamic-slice_fusion.1), channel_id=1, source_target_pairs={{0,8},{8,16},{16,24},{24,32},{32,40},{40,48},{48,56},{56,64},{64,7... | collective-permute-start | bytes 4718600 | tf_op jit(solution)/shard_map/ppermute | solution.py:153
  147.9 24.0 %collective-permute-start.13 = (bf16[128,6144]{1,0:T(8,128)(2,1)}, bf16[128,6144]{1,0:T(8,128)(2,1)}, u32[]{:S(2)}, u32[]{:S(2)}) collective-permute-start(bf16[128,6144]{1,0:T(8,128)(2,1)} %collective-permute-done.12), channel_id=1, source_target_pairs={{0,8},{16,24},{32,40},{48,56},{64,72},{80,88},{96,104},{112,120},{... | collective-permute-start | bytes 4718600 | tf_op jit(solution)/shard_map/ppermute | solution.py:153
  151.4 30.0 %all-to-all-start = ((bf16[8,64,512]{2,1,0:T(8,128)(2,1)}), bf16[8,64,512]{2,1,0:T(8,128)(2,1)}, u32[]{:S(2)}, u32[]{:S(2)}) async-start(bf16[8,64,512]{2,1,0:T(8,128)(2,1)} %bitcast.17), calls=%async_computation | async-start | bytes 1048576 | tf_op jit(solution)/shard_map/all_to_all | solution.py:200
  159.1 28.6 %collective-permute-start.6 = (f32[64,512]{1,0:T(8,128)S(1)}, f32[64,512]{1,0:T(8,128)S(1)}, u32[]{:S(2)}, u32[]{:S(2)}) collective-permute-start(f32[64,512]{1,0:T(8,128)S(1)} %convert_reduce_fusion), channel_id=1, source_target_pairs={{0,16},{16,32},{32,48},{48,64},{64,80},{80,96},{96,112},{112,128},... | collective-permute-start | bytes 393224 | tf_op jit(solution)/shard_map/ppermute | solution.py:153
  162.0 11.5 %collective-permute-start.15 = (bf16[128,6144]{1,0:T(8,128)(2,1)}, bf16[128,6144]{1,0:T(8,128)(2,1)S(1)}, u32[]{:S(2)}, u32[]{:S(2)}) collective-permute-start(bf16[128,6144]{1,0:T(8,128)(2,1)} %collective-permute-done.14), channel_id=1, source_target_pairs={{0,8},{16,24},{32,40},{48,56},{64,72},{80,88},{96,104},{112,120},{... | collective-permute-start | bytes 4718600 | tf_op jit(solution)/shard_map/ppermute | solution.py:153
  181.4 65.3 %all-to-all-start.2 = ((bf16[8,64,512]{2,1,0:T(8,128)(2,1)}), bf16[8,64,512]{2,1,0:T(8,128)(2,1)}, u32[]{:S(2)}, u32[]{:S(2)}) async-start(bf16[8,64,512]{2,1,0:T(8,128)(2,1)} %bitcast.27), calls=%async_computation.2 | async-start | bytes 1048576 | tf_op jit(solution)/shard_map/all_to_all | solution.py:200
  189.4 116.3 %collective-permute-start.17 = (bf16[512,768]{1,0:T(8,128)(2,1)}, bf16[512,768]{1,0:T(8,128)(2,1)}, u32[]{:S(2)}, u32[]{:S(2)}) collective-permute-start(bf16[512,768]{1,0:T(8,128)(2,1)} %get-tuple-element.41), channel_id=1, source_target_pairs={{0,8},{8,16},{16,24},{24,32},{32,40},{40,48},{48,56},{56,64},{64,7... | collective-permute-start | bytes 2359304 | tf_op jit(solution)/shard_map/ppermute | solution.py:153
  189.5 112.6 %collective-permute-start.18 = (bf16[512,768]{1,0:T(8,128)(2,1)}, bf16[512,768]{1,0:T(8,128)(2,1)}, u32[]{:S(2)}, u32[]{:S(2)}) collective-permute-start(bf16[512,768]{1,0:T(8,128)(2,1)} %get-tuple-element.42), channel_id=1, source_target_pairs={{0,8},{8,16},{16,24},{24,32},{32,40},{40,48},{48,56},{56,64},{64,7... | collective-permute-start | bytes 2359304 | tf_op jit(solution)/shard_map/ppermute | solution.py:153
  (11 other events, 78.9 us)

commit v2 on v1

v2 whole, which is shorter than its diff:
```python
import functools

import jax
import jax.numpy as jnp
from jax import lax
from jax.experimental import pallas as pl
from jax.experimental.pallas import tpu as pltpu
from jax.sharding import PartitionSpec as P

VMEM_BYTES = 40 * 1024 * 1024


def after(value, *earlier):
    return lax.optimization_barrier((value,) + earlier)[0]


def stacked(refs):
    blocks = [ref[...] for ref in refs]
    return blocks[0] if len(blocks) == 1 else jnp.concatenate(blocks, axis=0)


def product_kernel(n_left, n_right, at_ref, *refs):
    left, right = refs[:n_left], refs[n_left:n_left + n_right]
    out_ref, total = refs[n_left + n_right:]
    step = pl.program_id(0)
    term = lax.dot_general(
        stacked(left), stacked(right), (((1,), (1,)), ((), ())), preferred_element_type=jnp.float32
    )

    @pl.when(step == 0)
    def _():
        total[...] = term

    @pl.when(step > 0)
    def _():
        total[...] += term

    @pl.when(step == pl.num_programs(0) - 1)
    def _():
        out_ref[...] = total[...].astype(out_ref.dtype)


def products(left, right, left_at, right_at, depth, tile):
    rows = sum(array.shape[0] for array in left)
    cols = sum(array.shape[0] for array in right)
    offsets = jnp.stack([jnp.asarray(left_at, jnp.int32), jnp.asarray(right_at, jnp.int32)])
    return pl.pallas_call(
        functools.partial(product_kernel, len(left), len(right)),
        out_shape=jax.ShapeDtypeStruct((rows, cols), jnp.bfloat16),
        grid_spec=pltpu.PrefetchScalarGridSpec(
            num_scalar_prefetch=1,
            grid=(depth // tile,),
            in_specs=[pl.BlockSpec((a.shape[0], tile), lambda c, at: (0, at[0] + c)) for a in left]
            + [pl.BlockSpec((a.shape[0], tile), lambda c, at: (0, at[1] + c)) for a in right],
            out_specs=pl.BlockSpec((rows, cols), lambda c, at: (0, 0)),
            scratch_shapes=[pltpu.VMEM((rows, cols), jnp.float32)],
        ),
        compiler_params=pltpu.CompilerParams(vmem_limit_bytes=VMEM_BYTES),
        cost_estimate=pl.CostEstimate(
            flops=2 * rows * cols * depth, bytes_accessed=2 * (rows + cols) * depth, transcendentals=0
        ),
        name="products",
    )(offsets, *left, *right)


def swapped(x, width):
    rows, cols = x.shape
    r = lax.broadcasted_iota(jnp.int32, x.shape, 0)
    c = lax.broadcasted_iota(jnp.int32, x.shape, 1)
    s = 1
    while s < width:
        below = pltpu.roll(pltpu.roll(x, rows - s, 0), s, 1)
        above = pltpu.roll(pltpu.roll(x, s, 0), cols - s, 1)
        r_bit, c_bit = (r & s) != 0, (c & s) != 0
        x = jnp.where(r_bit == c_bit, x, jnp.where(c_bit, below, above))
        s *= 2
    return x


def amplitude_kernel(width, sum_ref, other_ref, row_ref, col_ref, out_ref):
    x = sum_ref[...] + other_ref[...].astype(jnp.float32)
    out_ref[...] = ((2.0 * x - swapped(x, width)) / (row_ref[...] + col_ref[...])).astype(out_ref.dtype)


def amplitudes(partial_sum, other, row, col, width):
    return pl.pallas_call(
        functools.partial(amplitude_kernel, width),
        out_shape=jax.ShapeDtypeStruct(other.shape, jnp.bfloat16),
        compiler_params=pltpu.CompilerParams(vmem_limit_bytes=VMEM_BYTES),
        cost_estimate=pl.CostEstimate(flops=60 * other.size, bytes_accessed=8 * other.size, transcendentals=0),
        name="amplitudes",
    )(partial_sum, other, row, col)


def density_kernel(n_early, n_late, at_ref, amp_early, amp_late, *refs):
    early, late, out_ref = refs[:n_early], refs[n_early:n_early + n_late], refs[-1]
    total = jnp.dot(amp_early[...], stacked(early), preferred_element_type=jnp.float32)
    total = total + jnp.dot(amp_late[...], stacked(late), preferred_element_type=jnp.float32)
    out_ref[...] = total.astype(out_ref.dtype)


def density(out, amp_early, amp_late, early, late, at, tile):
    rows, width, cols = amp_early.shape[0], early[0].shape[1], late[0].shape[1]
    in_specs = (
        [pl.BlockSpec(amp_early.shape, lambda c, at: (0, 0)), pl.BlockSpec(amp_late.shape, lambda c, at: (0, 0))]
        + [pl.BlockSpec((a.shape[0], tile), lambda c, at: (0, c)) for a in early]
        + [pl.BlockSpec((a.shape[0], tile), lambda c, at: (0, at[0] + c)) for a in late]
    )
    operands = [jnp.reshape(at, (1,)).astype(jnp.int32), amp_early, amp_late, *early, *late]
    aliases = {}
    if out is not None:
        in_specs.append(pl.BlockSpec(memory_space=pl.ANY))
        aliases = {len(operands): 0}
        operands.append(out)
    return pl.pallas_call(
        functools.partial(density_kernel, len(early), len(late)),
        out_shape=jax.ShapeDtypeStruct((rows, cols), jnp.bfloat16),
        grid_spec=pltpu.PrefetchScalarGridSpec(
            num_scalar_prefetch=1,
            grid=(width // tile,),
            in_specs=in_specs,
            out_specs=pl.BlockSpec((rows, tile), lambda c, at: (0, at[0] + c)),
        ),
        input_output_aliases=aliases,
        compiler_params=pltpu.CompilerParams(vmem_limit_bytes=VMEM_BYTES),
        cost_estimate=pl.CostEstimate(
            flops=4 * rows * rows * width, bytes_accessed=6 * rows * width, transcendentals=0
        ),
        name="density",
    )(*operands)


def per_device(b_factor, occ_energy, virt_energy):
    occ_rows, slab, cols = b_factor.shape
    rows, half = occ_rows * slab, cols // 2
    n_occ, n_aux = lax.axis_size("occ"), lax.axis_size("aux")
    p, q = lax.axis_index("occ"), lax.axis_index("aux")
    core, parity = p % 2, (p // 2) % 2
    first = core == 0
    n_y = n_aux // 2
    y_groups = [list(range(n_y)), list(range(n_y, n_aux))]
    own_rows = rows // n_y
    depth_tile, wide_tile, tile = cols // 6, cols // 8, cols // 16

    ring = [(i, (i + 1) % n_occ) for i in range(n_occ)]
    two_on = [(i, (i + 2) % n_occ) for i in range(n_occ)]
    in_chip = [(i, i + 1) for i in range(0, n_occ, 2)]
    to_next_chip = [(i, (i + 1) % n_occ) for i in range(1, n_occ, 2)]
    two_chips_back = [(i, (i - 4) % n_occ) for i in range(0, n_occ, 2)]
    evens_to_next = [(i, (i + 2) % n_occ) for i in range(0, n_occ, 2)]
    other_x = [(i, (i + n_y) % n_aux) for i in range(n_aux)]

    def send(value, pairs):
        return lax.ppermute(value, "occ", pairs)

    own = b_factor.reshape(rows, cols)
    energy_near, energy_far = send(occ_energy, ring), send(occ_energy, two_on)
    ready_own = after(own, energy_near, energy_far)

    o_starts = [0, 3 * rows // 16, 3 * rows // 4]
    o_sizes = [3 * rows // 16, 9 * rows // 16, rows // 4]
    odd = [send(ready_own[:o_sizes[0]], to_next_chip)]
    even = send(ready_own, in_chip)
    later_own = after(own, even)
    early_half = (parity + core + 1) % 2
    l_cols = half // 4

    def odd_part(part, *earlier):
        start = o_starts[part]
        return send(after(later_own[start:start + o_sizes[part]], *earlier), to_next_chip)

    def even_block(start, size):
        return jnp.where(
            first, lax.dynamic_slice(later_own, start, size), lax.dynamic_slice(even, start, size)
        )

    last_blocks = [even_block((0, (1 - parity) * half + part * l_cols), (rows, l_cols)) for part in range(4)]

    def last_part(part, *earlier):
        return send(after(last_blocks[part], *earlier), ring)

    def partner_part(part):
        return jnp.where(first, part, send(part, in_chip))

    partner = [partner_part(odd[0])]
    e_rows = rows // 2
    early = [send(after(even_block((0, parity * half), (e_rows, half)), odd[0]), ring)]
    early.append(send(after(even_block((e_rows, parity * half), (e_rows, half)), early[0]), ring))
    back = [send(part, two_chips_back) for part in early]
    odd.append(odd_part(1, early[1]))
    def spread_sum(value):
        parts = lax.all_to_all(value.reshape(n_y, own_rows, rows), "aux", 0, 0, axis_index_groups=y_groups)
        return parts.astype(jnp.float32).sum(0)

    def collected(value):
        parts = jnp.broadcast_to(value, (n_y, own_rows, rows))
        return lax.all_to_all(parts, "aux", 0, 0, axis_index_groups=y_groups).reshape(rows, rows)

    def slab_amplitudes(partial_sum, energy):
        other = lax.ppermute(partial_sum.astype(jnp.bfloat16), "aux", other_x)
        col = (energy[:, None] - virt_energy[None, :]).reshape(1, rows)
        return amplitudes(partial_sum, other, row, col, slab)

    row = (occ_energy[:, None] - virt_energy[None, :]).reshape(rows, 1)
    row = lax.dynamic_slice(row, ((q % n_y) * own_rows, 0), (own_rows, 1))
    even_energy = jnp.where(first, energy_far, energy_near)
    odd_energy = jnp.where(first, energy_near, energy_far)

    half_tiles = half // depth_tile
    near_half = products([own], [after(part, *last_blocks) for part in early], early_half * half_tiles, 0, half, depth_tile)
    near_sum = spread_sum(near_half)
    back = [after(part, near_sum) for part in back]
    far_half = lax.cond(
        first,
        lambda: products(back, [own], 0, early_half * half_tiles, half, depth_tile),
        lambda: products(
            [own], [even], (1 - early_half) * half_tiles, (1 - early_half) * half_tiles, half, depth_tile
        ),
    )
    odd.append(odd_part(2, odd[1], far_half))
    last = [last_part(0, odd[2])]
    last.append(last_part(1, odd[2]))
    far_sum = spread_sum(far_half)
    far_sum = jnp.where(
        first, send(far_sum.astype(jnp.bfloat16), evens_to_next).astype(jnp.float32), far_sum
    )
    even_sum = after(near_sum + far_sum, odd[1])
    even_slab = slab_amplitudes(even_sum, even_energy)

    partner.append(partner_part(after(odd[1], even_sum)))
    odd_products = [products([own], [after(part, even_slab) for part in partner], 0, 0, cols, depth_tile)]
    amp_even = collected(after(even_slab, odd_products[0]))
    partner.append(partner_part(after(odd[2], even_slab)))
    odd_products.append(products([own], partner[2:], 0, 0, cols, depth_tile))
    last.append(last_part(2, last[0], *odd_products))
    odd_products = after(jnp.concatenate(odd_products, axis=1), amp_even, last[0])
    odd_sum = after(spread_sum(odd_products), last[1])
    last.append(last_part(3, odd_sum))
    amp_odd = collected(after(slab_amplitudes(odd_sum, odd_energy), last[2]))

    gamma = density(None, amp_even, amp_odd, early, partner, early_half * (half // wide_tile), wide_tile)
    for part, block in enumerate(last):
        at = (1 - early_half) * (half // tile) + part * (l_cols // tile)
        gamma = density(gamma, amp_even, amp_odd, [block], partner, at, tile)
    return gamma.reshape(occ_rows, slab, cols)


def solution(mesh):
    placed = (P("occ", None, "aux"), P("occ"), P())
    return jax.shard_map(
        per_device, mesh=mesh, in_specs=placed, out_specs=P("occ", None, "aux"), check_vma=False
    )
```

time: 311 us -> 276 us (0.89); the launches traced: 309 us -> 270 us
  blocking collectives: 88.7 us -> 26.2 us
  waiting for transfers between devices: 66.8 us -> 99.5 us
  starting transfers between devices: 70.2 us -> 62.7 us
    all_gather x2 -> x0, blocking collectives: 88.7 us -> none  [the longest x1 53.5 us: per_device(): amp_even = lax.all_gather(amp_even, 'aux', axis=0, tiled=True)]
    all_to_all x0 -> x2, blocking collectives: none -> 26.2 us  [spread_sum(): lax.all_to_all(value.reshape(n_y, own_rows, rows), 'aux', 0, 0, axis_inde...]
    all_to_all x3, waiting for transfers between devices: 0.3 us -> 18.9 us  [the longest x1 10.8 us: spread_sum(): lax.all_to_all(value.reshape(n_y, own_rows, rows), 'aux', 0, 0, axis_inde...]
    ppermute x0 -> x2, waiting for transfers between devices: none -> 8.08 us  [slab_amplitudes(): other = lax.ppermute(partial_sum.astype(jnp.bfloat16), 'aux', other_x)]
    dynamic_slice x4 -> x1, local copies, waits for them, and re-layouts: 6.91 us -> 0.01 us  [per_device(): row = lax.dynamic_slice(row, (q % n_y * own_rows, 0), (own_rows, 1))]
    all_to_all x3, starting transfers between devices: 18.9 us -> 12.7 us  [the longest x2 8.29 us: collected(): lax.all_to_all(parts, 'aux', 0, 0, axis_index_groups=y_groups)]
    ppermute x19 -> x18, waiting for transfers between devices: 66.5 us -> 72.6 us  [send(): return lax.ppermute(value, 'occ', pairs)]
    ppermute x19 -> x18, starting transfers between devices: 51.3 us -> 45.6 us  [send(): return lax.ppermute(value, 'occ', pairs)]
  transfers between devices with their start and end apart: 22 -> 23, of which waited for: 6 -> 13; matrix products, arithmetic and copies ran while one was open for 9% -> 9% of each run, Pallas kernels for 14% -> 16%
where the time goes in v2:
time: 276 us; the launch traced here: 270 us
  waiting for transfers between devices  99.5 us (36%)
  starting transfers between devices  62.7 us (23%)
  Pallas kernels  46 us (17%)
  blocking collectives  26.2 us (9%)
  local copies, waits for them, and re-layouts  18.4 us (7%)
  other arithmetic  16.9 us (6%)
    ppermute x18, waiting for transfers between devices, send(): return lax.ppermute(value, 'occ', pairs)  72.6 us
    ppermute x18, starting transfers between devices, send(): return lax.ppermute(value, 'occ', pairs)  45.6 us
    all_to_all x2, blocking collectives, spread_sum(): lax.all_to_all(value.reshape(n_y, own_rows, rows), 'aux', 0, 0, axis_inde...  26.2 us
    pallas_call x4, Pallas kernels, products(): pl.pallas_call(functools.partial(product_kernel, len(left), len(right)),...  22.9 us
    pallas_call x5, Pallas kernels, density(): pl.pallas_call(functools.partial(density_kernel, len(early), len(late)),...  20.8 us
    all_to_all x1, waiting for transfers between devices, spread_sum(): lax.all_to_all(value.reshape(n_y, own_rows, rows), 'aux', 0, 0, axis_inde...  10.8 us
    unnamed x44, local copies, waits for them, and re-layouts  10.6 us
    select_n x2, other arithmetic, even_block(): jnp.where(first, lax.dynamic_slice(later_own, start, size), lax.dynamic_s...  9.07 us
  transfers between devices with their start and end apart: 23, of which 13 were waited for; matrix products, arithmetic and copies ran while one was open for 9% of the time, Pallas kernels for 16%

profile of v2, /device:TPU:2, one launch (start us, length us, event | category | flops | bytes accessed | tf_op | source)
XLA Modules:
  0.0 270.3 jit_solution(7632482347955806873)
XLA Ops:
  3.9 5.2 %collective-permute-start.2 = (bf16[512,6144]{1,0:T(8,128)(2,1)}, bf16[512,6144]{1,0:T(8,128)(2,1)}, u32[]{:S(2)}, u32[]{:S(2)}) collective-permute-start(bf16[512,6144]{1,0:T(8,128)(2,1)} %bitcast.16), channel_id=1, source_target_pairs={{0,8},{16,24},{32,40},{48,56},{64,72},{80,88},{96,104},{112,120},{... | collective-permute-start | bytes 18874376 | tf_op jit(solution)/shard_map/ppermute | solution.py:154
  11.8 4.7 %collective-permute-done.2 = bf16[512,6144]{1,0:T(8,128)(2,1)} collective-permute-done((bf16[512,6144]{1,0:T(8,128)(2,1)}, bf16[512,6144]{1,0:T(8,128)(2,1)}, u32[]{:S(2)}, u32[]{:S(2)}) %collective-permute-start.2) | collective-permute-done | bytes 6291488 | tf_op jit(solution)/shard_map/ppermute | solution.py:154
  20.7 7.3 %collective-permute-done.3 = bf16[96,6144]{1,0:T(8,128)(2,1)S(1)} collective-permute-done((bf16[96,6144]{1,0:T(8,128)(2,1)S(1)}, bf16[96,6144]{1,0:T(8,128)(2,1)S(1)}, u32[]{:S(2)}, u32[]{:S(2)}) %collective-permute-start.3) | collective-permute-done | bytes 1179680 | tf_op jit(solution)/shard_map/ppermute | solution.py:154
  29.0 19.8 %collective-permute-done.4.refs_1_.refs_0_ = bf16[256,3072]{1,0:T(8,128)(2,1)S(1)} collective-permute-done((bf16[256,3072]{1,0:T(8,128)(2,1)S(1)}, bf16[256,3072]{1,0:T(8,128)(2,1)S(1)}, u32[]{:S(2)}, u32[]{:S(2)}) %collective-permute-start.4) | collective-permute-done | bytes 1572896 | tf_op jit(solution)/shard_map/ppermute | solution.py:154
  52.0 16.7 %collective-permute-done.5.refs_2_.refs_1_ = bf16[256,3072]{1,0:T(8,128)(2,1)S(1)} collective-permute-done((bf16[256,3072]{1,0:T(8,128)(2,1)S(1)}, bf16[256,3072]{1,0:T(8,128)(2,1)S(1)}, u32[]{:S(2)}, u32[]{:S(2)}) %collective-permute-start.5) | collective-permute-done | bytes 1572896 | tf_op jit(solution)/shard_map/ppermute | solution.py:154
  70.0 6.3 %collective-permute-start.6 = (bf16[256,3072]{1,0:T(8,128)(2,1)S(1)}, bf16[256,3072]{1,0:T(8,128)(2,1)}, u32[]{:S(2)}, u32[]{:S(2)}) collective-permute-start(bf16[256,3072]{1,0:T(8,128)(2,1)S(1)} %collective-permute-done.4.refs_1_.refs_0_), channel_id=1, source_target_pairs={{0,224},{16,240},{32,0},{48,16},{64,32},{80,48},{96,64},{112,80},{... | collective-permute-start | bytes 4718600 | tf_op jit(solution)/shard_map/ppermute | solution.py:154
  79.9 5.0 %dynamic-slice_select_fusion.2 = (bf16[512,768]{1,0:T(8,128)(2,1)}, bf16[512,768]{1,0:T(8,128)(2,1)}, bf16[512,768]{1,0:T(8,128)(2,1)}, bf16[512,768]{1,0:T(8,128)(2,1)}) fusion(bf16[512,6144]{1,0:T(8,128)(2,1)} %collective-permute-done.2, s32[]{:T(128)S(6)} %select_n.138, bf16[512,6144]{1,0:T(8,128)(2,1)} %bitcast.19, pred[]{:T(512)S(6)} %eq.8, ...), kind=kLoop, calls=%fused_computation.10 | loop fusion | flops 1572864 | bytes 9437201 | tf_op jit(solution)/shard_map/jit(_where)/select_n | solution.py:173
  84.9 4.7 %products.7 = bf16[512,512]{1,0:T(8,128)(2,1)S(1)} custom-call(s32[2]{0:T(128)S(1)} %pad_add_fusion.2.at_ref, bf16[512,6144]{1,0:T(8,128)(2,1)} %bitcast.20, bf16[256,3072]{1,0:T(8,128)(2,1)S(1)} %collective-permute-done.4.refs_1_.refs_0_, bf16[256,3072]{1,0:T(8,128)(2,1)S(1)} %collective-permute-done.5.refs_2_.refs_1_), custom_call_target="tpu_custom_call" | custom-call | flops 1610612736 | bytes 6291456 | tf_op jit(solution)/shard_map/products/pallas_call | solution.py:47
  90.4 4.5 %all-to-all-start = ((bf16[4,128,512]{2,1,0:T(8,128)(2,1)}), bf16[4,128,512]{2,1,0:T(8,128)(2,1)}, u32[]{:S(2)}, u32[]{:S(2)}) async-start(bf16[4,128,512]{2,1,0:T(8,128)(2,1)} %bitcast.15), calls=%async_computation | async-start | bytes 1048576 | tf_op jit(solution)/shard_map/all_to_all | solution.py:192
  94.9 10.8 %all-to-all-done = bf16[4,128,512]{2,1,0:T(8,128)(2,1)} async-done(((bf16[4,128,512]{2,1,0:T(8,128)(2,1)}), bf16[4,128,512]{2,1,0:T(8,128)(2,1)}, u32[]{:S(2)}, u32[]{:S(2)}) %all-to-all-start) | async-done | bytes 524320 | tf_op jit(solution)/shard_map/all_to_all | solution.py:192
  106.9 4.2 %collective-permute-done.7 = bf16[256,3072]{1,0:T(8,128)(2,1)} collective-permute-done((bf16[256,3072]{1,0:T(8,128)(2,1)S(1)}, bf16[256,3072]{1,0:T(8,128)(2,1)}, u32[]{:S(2)}, u32[]{:S(2)}) %collective-permute-start.7) | collective-permute-done | bytes 1572896 | tf_op jit(solution)/shard_map/ppermute | solution.py:154
  111.1 5.5 %conditional.1 = (bf16[512,512]{1,0:T(8,128)(2,1)S(1)}) conditional(s32[]{:T(128)} %convert_element_type.25, (s32[]{:T(128)}, bf16[512,6144]{1,0:T(8,128)(2,1)}, bf16[512,6144]{1,0:T(8,128)(2,1)}) %tuple.68, (s32[]{:T(128)}, bf16[256,3072]{1,0:T(8,128)(2,1)}, bf16[256,3072]{1,0:T(8,128)(2,1)}, bf16[512,6144]{1,0:T(8,128)(2,1)}) %tuple.69), branch_computations={%region_1.2_spmd, %region_2.3_spmd} | conditional | flops 1610612736 | bytes 6291500 | solution.py:213
  111.2 5.4 %products.6 = bf16[512,512]{1,0:T(8,128)(2,1)S(1)} custom-call(s32[2]{0:T(128)S(1)} %pad_add_fusion.1.at_ref, bf16[256,3072]{1,0:T(8,128)(2,1)} %get-tuple-element.26.refs_0_, bf16[256,3072]{1,0:T(8,128)(2,1)} %get-tuple-element.27.refs_1_, bf16[512,6144]{1,0:T(8,128)(2,1)} %get-tuple-element.28.refs_2_), custom_call_target="tpu_custom_call" | custom-call | flops 1610612736 | bytes 6291456 | tf_op jit(solution)/shard_map/cond/branch_1_fun/products/pallas_call | solution.py:47
  116.6 12.5 %all_to_all.25 = bf16[4,128,512]{2,1,0:T(8,128)(2,1)S(1)} all-to-all(bf16[4,128,512]{2,1,0:T(8,128)(2,1)S(1)} %bitcast.29), channel_id=1, replica_groups={{0,1,2,3},{4,5,6,7},{8,9,10,11},{12,13,14,15},{16,17,18,19},{20,21,22,2..., dimensions={0} | all-to-all | bytes 1048576 | tf_op jit(solution)/shard_map/all_to_all | solution.py:192
  129.2 9.1 %collective-permute-start.8 = (bf16[128,512]{1,0:T(8,128)(2,1)S(1)}, bf16[128,512]{1,0:T(8,128)(2,1)S(1)}, u32[]{:S(2)}, u32[]{:S(2)}) collective-permute-start(bf16[128,512]{1,0:T(8,128)(2,1)S(1)} %convert_element_type.27), channel_id=1, source_target_pairs={{0,16},{16,32},{32,48},{48,64},{64,80},{80,96},{96,112},{112,128},... | collective-permute-start | bytes 393224 | tf_op jit(solution)/shard_map/ppermute | solution.py:154
  153.9 4.2 %collective-permute-done.10.other_ref = bf16[128,512]{1,0:T(8,128)(2,1)S(1)} collective-permute-done((bf16[128,512]{1,0:T(8,128)(2,1)S(1)}, bf16[128,512]{1,0:T(8,128)(2,1)S(1)}, u32[]{:S(2)}, u32[]{:S(2)}) %collective-permute-start.10) | collective-permute-done | bytes 131104 | tf_op jit(solution)/shard_map/ppermute | solution.py:200
  158.9 13.6 %collective-permute-done.13 = bf16[128,6144]{1,0:T(8,128)(2,1)} collective-permute-done((bf16[128,6144]{1,0:T(8,128)(2,1)S(1)}, bf16[128,6144]{1,0:T(8,128)(2,1)}, u32[]{:S(2)}, u32[]{:S(2)}) %collective-permute-start.13) | collective-permute-done | bytes 1572896 | tf_op jit(solution)/shard_map/ppermute | solution.py:154
  172.5 5.8 %collective-permute-start.15 = (bf16[512,768]{1,0:T(8,128)(2,1)}, bf16[512,768]{1,0:T(8,128)(2,1)}, u32[]{:S(2)}, u32[]{:S(2)}) collective-permute-start(bf16[512,768]{1,0:T(8,128)(2,1)} %get-tuple-element.68), channel_id=1, source_target_pairs={{0,8},{8,16},{16,24},{24,32},{32,40},{40,48},{48,56},{56,64},{64,7... | collective-permute-start | bytes 2359304 | tf_op jit(solution)/shard_map/ppermute | solution.py:154
  184.3 6.3 %products.8 = bf16[512,384]{1,0:T(8,128)(2,1)S(1)} custom-call(s32[2]{0:T(128)S(1)} %broadcast_1_at_ref.2.at_ref, bf16[512,6144]{1,0:T(8,128)(2,1)S(1)} %bitcast.28, bf16[96,6144]{1,0:T(8,128)(2,1)S(1)} %broadcast_select_fusion.2.refs_1_.refs_2_, bf16[288,6144]{1,0:T(8,128)(2,1)S(1)} %broadcast_select_fusion.refs_2_.refs_3_), custom_call_target="tpu_custom_call" | custom-call | flops 2415919104 | bytes 11010048 | tf_op jit(solution)/shard_map/products/pallas_call | solution.py:47
  192.3 4.2 %all-to-all-start.2 = ((bf16[4,128,512]{2,1,0:T(8,128)(2,1)}), bf16[4,128,512]{2,1,0:T(8,128)(2,1)}, u32[]{:S(2)}, u32[]{:S(2)}) async-start(bf16[4,128,512]{2,1,0:T(8,128)(2,1)} %broadcast_in_dim.4), calls=%async_computation.2 | async-start | bytes 1048576 | tf_op jit(solution)/shard_map/all_to_all | solution.py:197
  198.0 6.4 %products.9 = bf16[512,128]{1,0:T(8,128)(2,1)S(1)} custom-call(s32[2]{0:T(128)S(1)} %broadcast_1_at_ref.2.at_ref, bf16[512,6144]{1,0:T(8,128)(2,1)} %bitcast.24, bf16[128,6144]{1,0:T(8,128)(2,1)S(1)} %broadcast_select_fusion.1.refs_1_.refs_4_.refs_3_), custom_call_target="tpu_custom_call" | custom-call | flops 805306368 | bytes 7864320 | tf_op jit(solution)/shard_map/products/pallas_call | solution.py:47
  205.4 13.8 %all_to_all.26 = bf16[4,128,512]{2,1,0:T(8,128)(2,1)S(1)} all-to-all(bf16[4,128,512]{2,1,0:T(8,128)(2,1)} %bitcast.30), channel_id=1, replica_groups={{0,1,2,3},{4,5,6,7},{8,9,10,11},{12,13,14,15},{16,17,18,19},{20,21,22,2..., dimensions={0} | all-to-all | bytes 1048576 | tf_op jit(solution)/shard_map/all_to_all | solution.py:192
  236.0 8.0 %all-to-all-done.4 = bf16[4,128,512]{2,1,0:T(8,128)(2,1)} async-done(((bf16[4,128,512]{2,1,0:T(8,128)(2,1)}), bf16[4,128,512]{2,1,0:T(8,128)(2,1)}, u32[]{:S(2)}, u32[]{:S(2)}) %all-to-all-start.4) | async-done | bytes 524320 | tf_op jit(solution)/shard_map/all_to_all | solution.py:197
  249.5 6.5 %density.5.refs_4_ = bf16[512,6144]{1,0:T(8,128)(2,1)} custom-call(s32[1]{0:T(128)} %bitcast.13.at_ref, bf16[512,512]{1,0:T(8,128)(2,1)} %bitcast.7.amp_early, bf16[512,512]{1,0:T(8,128)(2,1)} %bitcast.9.amp_late, bf16[256,3072]{1,0:T(8,128)(2,1)S(1)} %copy-done.5, bf16[256,3072]{1,0:T(8,128)(2,1)S(1)} %copy-done.7, bf16[96,6144]{1,0:T(8,128)(2,1)S(1)} %copy-done.3, ...), custom_call_target="tpu_custom_call" | custom-call | flops 3221225472 | bytes 9437184 | tf_op jit(solution)/shard_map/density/pallas_call | solution.py:115
  (108 shorter events, 84.5 us)
Async XLA Ops:
  0.0 3.1 %collective-permute-start = (f32[32]{0:T(128)}, f32[32]{0:T(128)S(1)}, u32[]{:S(2)}, u32[]{:S(2)}) collective-permute-start(f32[32]{0:T(128)} %param.6), channel_id=1, source_target_pairs={{0,8},{8,16},{16,24},{24,32},{32,40},{40,48},{48,56},{56,64},{64,7... | collective-permute-start | bytes 392 | tf_op jit(solution)/shard_map/ppermute | solution.py:154
  0.0 3.9 %collective-permute-start.1 = (f32[32]{0:T(128)}, f32[32]{0:T(128)S(1)}, u32[]{:S(2)}, u32[]{:S(2)}) collective-permute-start(f32[32]{0:T(128)} %param.6), channel_id=1, source_target_pairs={{0,16},{8,24},{16,32},{24,40},{32,48},{40,56},{48,64},{56,72},{64,... | collective-permute-start | bytes 392 | tf_op jit(solution)/shard_map/ppermute | solution.py:154
  3.9 12.6 %collective-permute-start.2 = (bf16[512,6144]{1,0:T(8,128)(2,1)}, bf16[512,6144]{1,0:T(8,128)(2,1)}, u32[]{:S(2)}, u32[]{:S(2)}) collective-permute-start(bf16[512,6144]{1,0:T(8,128)(2,1)} %bitcast.16), channel_id=1, source_target_pairs={{0,8},{16,24},{32,40},{48,56},{64,72},{80,88},{96,104},{112,120},{... | collective-permute-start | bytes 18874376 | tf_op jit(solution)/shard_map/ppermute | solution.py:154
  10.5 17.5 %collective-permute-start.3 = (bf16[96,6144]{1,0:T(8,128)(2,1)S(1)}, bf16[96,6144]{1,0:T(8,128)(2,1)S(1)}, u32[]{:S(2)}, u32[]{:S(2)}) collective-permute-start(bf16[96,6144]{1,0:T(8,128)(2,1)S(1)} %slice.9), channel_id=1, source_target_pairs={{8,16},{24,32},{40,48},{56,64},{72,80},{88,96},{104,112},{120,128}... | collective-permute-start | bytes 3538952 | tf_op jit(solution)/shard_map/ppermute | solution.py:154
  29.0 19.8 %collective-permute-start.4 = (bf16[256,3072]{1,0:T(8,128)(2,1)S(1)}, bf16[256,3072]{1,0:T(8,128)(2,1)S(1)}, u32[]{:S(2)}, u32[]{:S(2)}) collective-permute-start(bf16[256,3072]{1,0:T(8,128)(2,1)S(1)} %get-tuple-element.54), channel_id=1, source_target_pairs={{0,8},{8,16},{16,24},{24,32},{32,40},{40,48},{48,56},{56,64},{64,7... | collective-permute-start | bytes 4718600 | tf_op jit(solution)/shard_map/ppermute | solution.py:154
  48.9 36.0 %copy-start.4 = (bf16[256,3072]{1,0:T(8,128)(2,1)}, bf16[256,3072]{1,0:T(8,128)(2,1)S(1)}, u32[]{:S(2)}) copy-start(bf16[256,3072]{1,0:T(8,128)(2,1)S(1)} %collective-permute-done.4.refs_1_.refs_0_) | copy-start | bytes 4718596
  48.9 19.8 %collective-permute-start.5 = (bf16[256,3072]{1,0:T(8,128)(2,1)S(1)}, bf16[256,3072]{1,0:T(8,128)(2,1)S(1)}, u32[]{:S(2)}, u32[]{:S(2)}) collective-permute-start(bf16[256,3072]{1,0:T(8,128)(2,1)S(1)} %get-tuple-element.56), channel_id=1, source_target_pairs={{0,8},{8,16},{16,24},{24,32},{32,40},{40,48},{48,56},{56,64},{64,7... | collective-permute-start | bytes 4718600 | tf_op jit(solution)/shard_map/ppermute | solution.py:154
  68.7 73.7 %collective-permute-start.9 = (bf16[288,6144]{1,0:T(8,128)(2,1)}, bf16[288,6144]{1,0:T(8,128)(2,1)}, u32[]{:S(2)}, u32[]{:S(2)}) collective-permute-start(bf16[288,6144]{1,0:T(8,128)(2,1)} %slice.10), channel_id=1, source_target_pairs={{8,16},{24,32},{40,48},{56,64},{72,80},{88,96},{104,112},{120,128}... | collective-permute-start | bytes 10616840 | tf_op jit(solution)/shard_map/ppermute | solution.py:154
  70.0 36.9 %collective-permute-start.6 = (bf16[256,3072]{1,0:T(8,128)(2,1)S(1)}, bf16[256,3072]{1,0:T(8,128)(2,1)}, u32[]{:S(2)}, u32[]{:S(2)}) collective-permute-start(bf16[256,3072]{1,0:T(8,128)(2,1)S(1)} %collective-permute-done.4.refs_1_.refs_0_), channel_id=1, source_target_pairs={{0,224},{16,240},{32,0},{48,16},{64,32},{80,48},{96,64},{112,80},{... | collective-permute-start | bytes 4718600 | tf_op jit(solution)/shard_map/ppermute | solution.py:154
  76.3 34.8 %collective-permute-start.7 = (bf16[256,3072]{1,0:T(8,128)(2,1)S(1)}, bf16[256,3072]{1,0:T(8,128)(2,1)}, u32[]{:S(2)}, u32[]{:S(2)}) collective-permute-start(bf16[256,3072]{1,0:T(8,128)(2,1)S(1)} %collective-permute-done.5.refs_2_.refs_1_), channel_id=1, source_target_pairs={{0,224},{16,240},{32,0},{48,16},{64,32},{80,48},{96,64},{112,80},{... | collective-permute-start | bytes 4718600 | tf_op jit(solution)/shard_map/ppermute | solution.py:154
  90.4 15.3 %all-to-all-start = ((bf16[4,128,512]{2,1,0:T(8,128)(2,1)}), bf16[4,128,512]{2,1,0:T(8,128)(2,1)}, u32[]{:S(2)}, u32[]{:S(2)}) async-start(bf16[4,128,512]{2,1,0:T(8,128)(2,1)} %bitcast.15), calls=%async_computation | async-start | bytes 1048576 | tf_op jit(solution)/shard_map/all_to_all | solution.py:192
  129.2 13.2 %collective-permute-start.8 = (bf16[128,512]{1,0:T(8,128)(2,1)S(1)}, bf16[128,512]{1,0:T(8,128)(2,1)S(1)}, u32[]{:S(2)}, u32[]{:S(2)}) collective-permute-start(bf16[128,512]{1,0:T(8,128)(2,1)S(1)} %convert_element_type.27), channel_id=1, source_target_pairs={{0,16},{16,32},{32,48},{48,64},{64,80},{80,96},{96,112},{112,128},... | collective-permute-start | bytes 393224 | tf_op jit(solution)/shard_map/ppermute | solution.py:154
  142.4 39.5 %collective-permute-start.12 = (bf16[288,6144]{1,0:T(8,128)(2,1)}, bf16[288,6144]{1,0:T(8,128)(2,1)}, u32[]{:S(2)}, u32[]{:S(2)}) collective-permute-start(bf16[288,6144]{1,0:T(8,128)(2,1)} %collective-permute-done.9), channel_id=1, source_target_pairs={{0,8},{16,24},{32,40},{48,56},{64,72},{80,88},{96,104},{112,120},{... | collective-permute-start | bytes 10616840 | tf_op jit(solution)/shard_map/ppermute | solution.py:154
  145.4 8.4 %collective-permute-start.11 = (bf16[96,6144]{1,0:T(8,128)(2,1)S(1)}, bf16[96,6144]{1,0:T(8,128)(2,1)}, u32[]{:S(2)}, u32[]{:S(2)}) collective-permute-start(bf16[96,6144]{1,0:T(8,128)(2,1)S(1)} %copy-done.17), channel_id=1, source_target_pairs={{0,8},{16,24},{32,40},{48,56},{64,72},{80,88},{96,104},{112,120},{... | collective-permute-start | bytes 3538952 | tf_op jit(solution)/shard_map/ppermute | solution.py:154
  149.3 23.2 %collective-permute-start.13 = (bf16[128,6144]{1,0:T(8,128)(2,1)S(1)}, bf16[128,6144]{1,0:T(8,128)(2,1)}, u32[]{:S(2)}, u32[]{:S(2)}) collective-permute-start(bf16[128,6144]{1,0:T(8,128)(2,1)S(1)} %slice.11), channel_id=1, source_target_pairs={{8,16},{24,32},{40,48},{56,64},{72,80},{88,96},{104,112},{120,128}... | collective-permute-start | bytes 4718600 | tf_op jit(solution)/shard_map/ppermute | solution.py:154
  151.6 6.6 %collective-permute-start.10 = (bf16[128,512]{1,0:T(8,128)(2,1)S(1)}, bf16[128,512]{1,0:T(8,128)(2,1)S(1)}, u32[]{:S(2)}, u32[]{:S(2)}) collective-permute-start(bf16[128,512]{1,0:T(8,128)(2,1)S(1)} %convert_element_type.29), channel_id=1, source_target_pairs={{0,4},{1,5},{2,6},{3,7},{4,0},{5,1},{6,2},{7,3},{8,12},{9,13},{10,... | collective-permute-start | bytes 393224 | tf_op jit(solution)/shard_map/ppermute | solution.py:200
  172.5 31.9 %collective-permute-start.15 = (bf16[512,768]{1,0:T(8,128)(2,1)}, bf16[512,768]{1,0:T(8,128)(2,1)}, u32[]{:S(2)}, u32[]{:S(2)}) collective-permute-start(bf16[512,768]{1,0:T(8,128)(2,1)} %get-tuple-element.68), channel_id=1, source_target_pairs={{0,8},{8,16},{16,24},{24,32},{32,40},{40,48},{48,56},{56,64},{64,7... | collective-permute-start | bytes 2359304 | tf_op jit(solution)/shard_map/ppermute | solution.py:154
  178.4 40.9 %collective-permute-start.16 = (bf16[512,768]{1,0:T(8,128)(2,1)}, bf16[512,768]{1,0:T(8,128)(2,1)}, u32[]{:S(2)}, u32[]{:S(2)}) collective-permute-start(bf16[512,768]{1,0:T(8,128)(2,1)} %get-tuple-element.70), channel_id=1, source_target_pairs={{0,8},{8,16},{16,24},{24,32},{32,40},{40,48},{48,56},{56,64},{64,7... | collective-permute-start | bytes 2359304 | tf_op jit(solution)/shard_map/ppermute | solution.py:154
  178.6 17.8 %collective-permute-start.14 = (bf16[128,6144]{1,0:T(8,128)(2,1)}, bf16[128,6144]{1,0:T(8,128)(2,1)}, u32[]{:S(2)}, u32[]{:S(2)}) collective-permute-start(bf16[128,6144]{1,0:T(8,128)(2,1)} %collective-permute-done.13), channel_id=1, source_target_pairs={{0,8},{16,24},{32,40},{48,56},{64,72},{80,88},{96,104},{112,120},{... | collective-permute-start | bytes 4718600 | tf_op jit(solution)/shard_map/ppermute | solution.py:154
  192.3 13.2 %all-to-all-start.2 = ((bf16[4,128,512]{2,1,0:T(8,128)(2,1)}), bf16[4,128,512]{2,1,0:T(8,128)(2,1)}, u32[]{:S(2)}, u32[]{:S(2)}) async-start(bf16[4,128,512]{2,1,0:T(8,128)(2,1)} %broadcast_in_dim.4), calls=%async_computation.2 | async-start | bytes 1048576 | tf_op jit(solution)/shard_map/all_to_all | solution.py:197
  204.5 26.4 %collective-permute-start.18 = (bf16[512,768]{1,0:T(8,128)(2,1)}, bf16[512,768]{1,0:T(8,128)(2,1)}, u32[]{:S(2)}, u32[]{:S(2)}) collective-permute-start(bf16[512,768]{1,0:T(8,128)(2,1)} %get-tuple-element.72), channel_id=1, source_target_pairs={{0,8},{8,16},{16,24},{24,32},{32,40},{40,48},{48,56},{56,64},{64,7... | collective-permute-start | bytes 2359304 | tf_op jit(solution)/shard_map/ppermute | solution.py:154
  220.7 6.8 %collective-permute-start.17 = (bf16[128,512]{1,0:T(8,128)(2,1)}, bf16[128,512]{1,0:T(8,128)(2,1)}, u32[]{:S(2)}, u32[]{:S(2)}) collective-permute-start(bf16[128,512]{1,0:T(8,128)(2,1)} %convert_element_type.31), channel_id=1, source_target_pairs={{0,4},{1,5},{2,6},{3,7},{4,0},{5,1},{6,2},{7,3},{8,12},{9,13},{10,... | collective-permute-start | bytes 393224 | tf_op jit(solution)/shard_map/ppermute | solution.py:200
  231.7 12.3 %all-to-all-start.4 = ((bf16[4,128,512]{2,1,0:T(8,128)(2,1)}), bf16[4,128,512]{2,1,0:T(8,128)(2,1)}, u32[]{:S(2)}, u32[]{:S(2)}) async-start(bf16[4,128,512]{2,1,0:T(8,128)(2,1)} %broadcast_in_dim.5), calls=%async_computation.4 | async-start | bytes 1048576 | tf_op jit(solution)/shard_map/all_to_all | solution.py:197
  235.9 30.8 %collective-permute-start.19 = (bf16[512,768]{1,0:T(8,128)(2,1)}, bf16[512,768]{1,0:T(8,128)(2,1)}, u32[]{:S(2)}, u32[]{:S(2)}) collective-permute-start(bf16[512,768]{1,0:T(8,128)(2,1)} %get-tuple-element.74), channel_id=1, source_target_pairs={{0,8},{8,16},{16,24},{24,32},{32,40},{40,48},{48,56},{56,64},{64,7... | collective-permute-start | bytes 2359304 | tf_op jit(solution)/shard_map/ppermute | solution.py:154
  (21 other events, 200.3 us)

commit v3 on v0

v3 whole, which is shorter than its diff:
```python
import functools

import jax
import jax.numpy as jnp
from jax import lax
from jax.experimental import pallas as pl
from jax.experimental.pallas import tpu as pltpu
from jax.sharding import PartitionSpec as P

VMEM_BYTES = 24 * 1024 * 1024


def after(value, *earlier):
    return lax.optimization_barrier((value,) + earlier)[0]


IN_VMEM = pl.BlockSpec(memory_space=pltpu.VMEM)


def part(ref, step, size):
    return ref[:, pl.ds(pl.multiple_of(step * size, size), size)]


def joined(arrays, dim):
    return arrays[0] if len(arrays) == 1 else jnp.concatenate(arrays, axis=dim)


def product_kernel(tile, left_ref, *refs):
    right, out_ref, total = refs[:-2], refs[-2], refs[-1]
    total[...] = jnp.zeros_like(total)

    def body(step, carry):
        total[...] += lax.dot_general(
            part(left_ref, step, tile),
            joined([part(ref, step, tile) for ref in right], 0),
            (((1,), (1,)), ((), ())),
            preferred_element_type=jnp.float32,
        )
        return carry

    lax.fori_loop(0, left_ref.shape[1] // tile, body, 0)
    out_ref[...] = total[...].astype(out_ref.dtype)


def products(left, right, tile):
    rows, depth = left.shape
    cols = sum(array.shape[0] for array in right)
    return pl.pallas_call(
        functools.partial(product_kernel, tile),
        out_shape=jax.ShapeDtypeStruct((rows, cols), jnp.bfloat16),
        in_specs=[IN_VMEM] * (1 + len(right)),
        out_specs=IN_VMEM,
        scratch_shapes=[pltpu.VMEM((rows, cols), jnp.float32)],
        compiler_params=pltpu.CompilerParams(vmem_limit_bytes=VMEM_BYTES),
        cost_estimate=pl.CostEstimate(
            flops=2 * rows * cols * depth, bytes_accessed=2 * (rows + cols) * depth, transcendentals=0
        ),
        name="products",
    )(left, *right)


def swapped(x, width):
    rows, cols = x.shape
    r = lax.broadcasted_iota(jnp.int32, x.shape, 0)
    c = lax.broadcasted_iota(jnp.int32, x.shape, 1)
    s = 1
    while s < width:
        below = pltpu.roll(pltpu.roll(x, rows - s, 0), s, 1)
        above = pltpu.roll(pltpu.roll(x, s, 0), cols - s, 1)
        r_bit, c_bit = (r & s) != 0, (c & s) != 0
        x = jnp.where(r_bit == c_bit, x, jnp.where(c_bit, below, above))
        s *= 2
    return x


def amplitude_kernel(width, row_ref, col_ref, *refs):
    x = refs[0][...].astype(jnp.float32)
    for ref in refs[1:-1]:
        x = x + ref[...].astype(jnp.float32)
    refs[-1][...] = ((2.0 * x - swapped(x, width)) / (row_ref[...] + col_ref[...])).astype(refs[-1].dtype)


def amplitudes(terms, row, col, width):
    rows, cols = terms[0].shape
    block = min(rows, 128)
    return pl.pallas_call(
        functools.partial(amplitude_kernel, width),
        out_shape=jax.ShapeDtypeStruct((rows, cols), jnp.bfloat16),
        grid=(rows // block,),
        in_specs=[pl.BlockSpec((block, 1), lambda r: (r, 0)), pl.BlockSpec((1, cols), lambda r: (0, 0))]
        + [pl.BlockSpec((block, cols), lambda r: (r, 0)) for _ in terms],
        out_specs=pl.BlockSpec((block, cols), lambda r: (r, 0)),
        compiler_params=pltpu.CompilerParams(vmem_limit_bytes=VMEM_BYTES),
        cost_estimate=pl.CostEstimate(flops=60 * rows * cols, bytes_accessed=8 * rows * cols, transcendentals=0),
        name="amplitudes",
    )(row, col, *terms)


def tile_density(amp, blocks, step, tile):
    block = joined([part(ref, step, tile) for ref in blocks], 0)
    return jnp.dot(amp, block, preferred_element_type=jnp.float32)


def first_density_kernel(tile, amp_ref, *refs):
    blocks, out_ref = refs[:-1], refs[-1]

    def body(step, carry):
        total = tile_density(amp_ref[...], blocks, step, tile)
        out_ref[:, pl.ds(pl.multiple_of(step * tile, tile), tile)] = total.astype(out_ref.dtype)
        return carry

    lax.fori_loop(0, out_ref.shape[1] // tile, body, 0)


def first_density(amp, blocks, tile):
    rows, cols = amp.shape[0], blocks[0].shape[1]
    return pl.pallas_call(
        functools.partial(first_density_kernel, tile),
        out_shape=jax.ShapeDtypeStruct((rows, cols), jnp.bfloat16),
        in_specs=[IN_VMEM] * (1 + len(blocks)),
        out_specs=IN_VMEM,
        compiler_params=pltpu.CompilerParams(vmem_limit_bytes=VMEM_BYTES),
        cost_estimate=pl.CostEstimate(
            flops=2 * rows * rows * cols, bytes_accessed=4 * rows * cols, transcendentals=0
        ),
        name="first_density",
    )(amp, *blocks)


def last_density_kernel(tile, n_parts, *refs):
    amps, blocks = refs[:n_parts], refs[n_parts:2 * n_parts]
    start_ref, out_ref, amp, buffers, sems = refs[2 * n_parts:]
    amp[...] = joined([ref[...] for ref in amps], 1)
    steps = start_ref.shape[1] // tile

    def copy_out(slot, step):
        columns = pl.ds(pl.multiple_of(step * tile, tile), tile)
        return pltpu.make_async_copy(buffers.at[slot], out_ref.at[:, columns], sems.at[slot])

    for step in range(steps):
        slot = step % 2
        if step >= 2:
            copy_out(slot, step - 2).wait()
        total = tile_density(amp[...], blocks, step, tile) + part(start_ref, step, tile).astype(jnp.float32)
        buffers[slot] = total.astype(buffers.dtype)
        copy_out(slot, step).start()
    for step in range(max(steps - 2, 0), steps):
        copy_out(step % 2, step).wait()


def last_density(amps, blocks, start, tile):
    rows, cols = start.shape
    return pl.pallas_call(
        functools.partial(last_density_kernel, tile, len(amps)),
        out_shape=jax.ShapeDtypeStruct((rows, cols), jnp.bfloat16),
        in_specs=[IN_VMEM] * (2 * len(amps) + 1),
        out_specs=pl.BlockSpec(memory_space=pl.ANY),
        scratch_shapes=[
            pltpu.VMEM((rows, rows), jnp.bfloat16),
            pltpu.VMEM((2, rows, tile), jnp.bfloat16),
            pltpu.SemaphoreType.DMA((2,)),
        ],
        compiler_params=pltpu.CompilerParams(vmem_limit_bytes=VMEM_BYTES),
        cost_estimate=pl.CostEstimate(
            flops=2 * rows * rows * cols, bytes_accessed=6 * rows * cols, transcendentals=0
        ),
        name="last_density",
    )(*amps, *blocks, start)


def per_device(b_factor, occ_energy, virt_energy):
    occ_rows, slab, cols = b_factor.shape
    rows = occ_rows * slab
    n_occ, n_aux = lax.axis_size("occ"), lax.axis_size("aux")
    q = lax.axis_index("aux")
    n_y = n_aux // 2
    y_groups = [list(range(n_y)), list(range(n_y, n_aux))]
    own_rows = rows // n_y
    depth_tile, tile = cols // 6, cols // 8
    large = 3 * rows // 4

    ring = [(i, (i + 1) % n_occ) for i in range(n_occ)]
    two_on = [(i, (i + 2) % n_occ) for i in range(n_occ)]
    other_x = [(i, (i + n_y) % n_aux) for i in range(n_aux)]

    def send(value, pairs=ring):
        return lax.ppermute(value, "occ", pairs)

    def across(value):
        return lax.ppermute(value.astype(jnp.bfloat16), "aux", other_x)

    own = b_factor.reshape(rows, cols)
    near_large, near_small = send(own[:large]), send(own[large:])
    energy = after(occ_energy, near_small)
    energy_near, energy_far = send(energy), send(energy, two_on)
    far_large = send(after(near_large, energy_near, energy_far))

    energy_near, energy_far, own_energy, _ = lax.optimization_barrier(
        (energy_near, energy_far, occ_energy, near_large)
    )
    row = (own_energy[:, None] - virt_energy[None, :]).reshape(rows, 1)
    own_row = lax.dynamic_slice(row, ((q % n_y) * own_rows, 0), (own_rows, 1))
    near_col = (energy_near[:, None] - virt_energy[None, :]).reshape(1, rows)
    far_col = (energy_far[:, None] - virt_energy[None, :]).reshape(1, rows)

    near_products = products(own, [near_large, near_small], depth_tile)
    far_small = send(after(near_small, far_large, near_products))
    amp_near = amplitudes([lax.psum(near_products, "aux")], row, near_col, slab)
    near_density = first_density(amp_near, [near_large, near_small], tile)

    large_parts = lax.all_to_all(
        products(own, [far_large], depth_tile).reshape(n_y, own_rows, large), "aux", 0, 0, axis_index_groups=y_groups
    )
    large_sum = large_parts.astype(jnp.float32).sum(0)
    large_slab = amplitudes([large_sum, across(large_sum)], own_row, far_col[:, :large], slab)
    amp_large = lax.all_to_all(
        jnp.broadcast_to(large_slab, (n_y, own_rows, large)), "aux", 0, 0, axis_index_groups=y_groups
    ).reshape(rows, large)

    small_products = products(own, [after(far_small, near_density)], depth_tile)
    small_parts = lax.all_to_all(
        jnp.broadcast_to(small_products, (n_y, rows, rows - large)), "aux", 0, 0, axis_index_groups=y_groups
    )
    small_sum = small_parts.astype(jnp.float32).sum(0)
    amp_small = amplitudes([small_sum, across(small_sum)], row, far_col[:, large:], slab)

    gamma = last_density([amp_large, amp_small], [far_large, far_small], near_density, tile)
    return gamma.reshape(occ_rows, slab, cols)


def solution(mesh):
    placed = (P("occ", None, "aux"), P("occ"), P())
    return jax.shard_map(
        per_device, mesh=mesh, in_specs=placed, out_specs=P("occ", None, "aux"), check_vma=False
    )
```

time: 344 us -> 308 us (0.90)
  Pallas kernels: 0 us -> 38.7 us
  matrix products: 30 us -> 0 us
  waiting for transfers between devices: 243 us -> 216 us
  local copies, waits for them, and re-layouts: 42.3 us -> 17.1 us
  starting transfers between devices: 2.07 us -> 19.6 us
  other arithmetic: 10.6 us -> 1.25 us
    pallas_call x0 -> x8, Pallas kernels: none -> 38.7 us  [the longest x3 16.4 us: products(): pl.pallas_call(functools.partial(product_kernel, tile), out_shape=jax.Sha...]
    reshape x6 -> x0, local copies, waits for them, and re-layouts: 34.3 us -> none  [the longest x4 18.7 us: amplitudes(): integrals_flat.reshape(row_count, slab_width, partner_energy.shape[0], sl...]
    dot_general x4 -> x0, matrix products: 30 us -> none  [the longest x2 16.1 us: per_device(): lax.dot_general(own_rows, partner_rows, (((1,), (1,)), ((), ())), preferr...]
    psum x1, waiting for transfers between devices: 112 us -> 88.2 us  [per_device(): amp_near = amplitudes([lax.psum(near_products, 'aux')], row, near_col, slab)]
    all_to_all x0 -> x3, starting transfers between devices: none -> 12.7 us  [the longest x1 4.74 us: per_device(): lax.all_to_all(jnp.broadcast_to(large_slab, (n_y, own_rows, large)), 'aux...]
    unnamed x6 -> x22, local copies, waits for them, and re-layouts: 0.01 us -> 12.2 us
    convert_element_type x2 -> x0, local copies, waits for them, and re-layouts: 7.99 us -> none  [amplitudes(): amplitude.astype(jnp.bfloat16)]
    convert_element_type x4 -> x2, other arithmetic: 5.81 us -> 0.03 us  [across(): return lax.ppermute(value.astype(jnp.bfloat16), 'aux', other_x)]
  transfers between devices with their start and end apart: 5 -> 12, of which waited for: 5 -> 6; matrix products, arithmetic and copies ran while one was open for 5% -> 1% of each run, Pallas kernels for 0% -> 10%
where the time goes in v3:
time: 308 us; the launch traced here: 306 us
  waiting for transfers between devices  216 us (70%)
  Pallas kernels  38.7 us (13%)
  starting transfers between devices  19.6 us (6%)
  local copies, waits for them, and re-layouts  17.1 us (6%)
  between operations  13.7 us (4%)
    ppermute x6, waiting for transfers between devices, send(): return lax.ppermute(value, 'occ', pairs)  118 us
    psum x1, waiting for transfers between devices, per_device(): amp_near = amplitudes([lax.psum(near_products, 'aux')], row, near_col, slab)  88.2 us
    pallas_call x3, Pallas kernels, products(): pl.pallas_call(functools.partial(product_kernel, tile), out_shape=jax.Sha...  16.4 us
    unnamed x22, local copies, waits for them, and re-layouts  12.2 us
    ppermute x2, waiting for transfers between devices, across(): return lax.ppermute(value.astype(jnp.bfloat16), 'aux', other_x)  9.68 us
    pallas_call x1, Pallas kernels, last_density(): pl.pallas_call(functools.partial(last_density_kernel, tile, len(amps)), o...  9.38 us
    pallas_call x1, Pallas kernels, first_density(): pl.pallas_call(functools.partial(first_density_kernel, tile), out_shape=j...  7.2 us
  transfers between devices with their start and end apart: 12, of which 6 were waited for; matrix products, arithmetic and copies ran while one was open for 1% of the time, Pallas kernels for 10%

profile of v3, /device:TPU:2, one launch (start us, length us, event | category | flops | bytes accessed | tf_op | source)
XLA Modules:
  0.0 306.2 jit_solution(857112711960661709)
XLA Ops:
  6.5 2.8 slice.20
  9.4 1.3 copy-done
  11.6 68.2 %collective-permute-done.refs_1_ = bf16[128,6144]{1,0:T(8,128)(2,1)S(1)} collective-permute-done((bf16[128,6144]{1,0:T(8,128)(2,1)S(1)}, bf16[128,6144]{1,0:T(8,128)(2,1)S(1)}, u32[]{:S(2)}, u32[]{:S(2)}) %collective-permute-start) | collective-permute-done | bytes 1572896 | tf_op jit(solution)/shard_map/ppermute | solution.py:187
  79.8 2.8 collective-permute-start.2
  82.6 3.7 %collective-permute-done.2 = f32[32]{0:T(128)S(1)} collective-permute-done((f32[32]{0:T(128)S(1)}, f32[32]{0:T(128)S(1)}, u32[]{:S(2)}, u32[]{:S(2)}) %collective-permute-start.2) | collective-permute-done | bytes 160 | tf_op jit(solution)/shard_map/ppermute | solution.py:187
  86.4 6.9 %products.4 = bf16[512,512]{1,0:T(8,128)(2,1)S(1)} custom-call(bf16[512,6144]{1,0:T(8,128)(2,1)S(1)} %bitcast.6, bf16[384,6144]{1,0:T(8,128)(2,1)} %collective-permute-done.3.refs_0_, bf16[128,6144]{1,0:T(8,128)(2,1)S(1)} %collective-permute-done.refs_1_), custom_call_target="tpu_custom_call" | custom-call | flops 3221225472 | bytes 12582912 | tf_op jit(solution)/shard_map/products/pallas_call | solution.py:48
  94.1 46.1 %collective-permute-done.4.refs_0_.refs_2_ = bf16[384,6144]{1,0:T(8,128)(2,1)} collective-permute-done((bf16[384,6144]{1,0:T(8,128)(2,1)}, bf16[384,6144]{1,0:T(8,128)(2,1)}, u32[]{:S(2)}, u32[]{:S(2)}) %collective-permute-start.4) | collective-permute-done | bytes 4718624 | tf_op jit(solution)/shard_map/ppermute | solution.py:187
  140.6 2.8 copy-done.1
  143.4 6.8 %products.3 = bf16[512,384]{1,0:T(8,128)(2,1)S(1)} custom-call(bf16[512,6144]{1,0:T(8,128)(2,1)S(1)} %bitcast.7, bf16[384,6144]{1,0:T(8,128)(2,1)} %collective-permute-done.4.refs_0_.refs_2_), custom_call_target="tpu_custom_call" | custom-call | flops 2415919104 | bytes 11010048 | tf_op jit(solution)/shard_map/products/pallas_call | solution.py:48
  151.0 4.5 %all-to-all-start = ((bf16[4,128,384]{2,1,0:T(8,128)(2,1)}), bf16[4,128,384]{2,1,0:T(8,128)(2,1)}, u32[]{:S(2)}, u32[]{:S(2)}) async-start(bf16[4,128,384]{2,1,0:T(8,128)(2,1)} %bitcast.11), calls=%async_computation | async-start | bytes 786432 | tf_op jit(solution)/shard_map/all_to_all | solution.py:211
  155.4 88.2 %all-reduce.2.cloned.1.call-done.refs_0_ = bf16[512,512]{1,0:T(8,128)(2,1)} async-done(((bf16[512,512]{1,0:T(8,128)(2,1)}), bf16[512,512]{1,0:T(8,128)(2,1)}) %all-reduce.2.cloned.1.call-update) | async-done | bytes 524304 | tf_op jit(solution)/shard_map/psum | solution.py:208
  244.7 3.4 %amplitudes.4.amp_ref = bf16[512,512]{1,0:T(8,128)(2,1)S(1)} custom-call(f32[512,1]{1,0:T(8,128)S(1)} %sub.75.row_ref, f32[1,512]{1,0:T(1,128)S(1)} %sub.74.col_ref, bf16[512,512]{1,0:T(8,128)(2,1)S(1)} %copy-done.6), custom_call_target="tpu_custom_call" | custom-call | flops 15728640 | bytes 2097152 | tf_op jit(solution)/shard_map/amplitudes/pallas_call | solution.py:86
  248.1 7.2 %first_density.1.refs_4_ = bf16[512,6144]{1,0:T(8,128)(2,1)S(1)} custom-call(bf16[512,512]{1,0:T(8,128)(2,1)S(1)} %amplitudes.4.amp_ref, bf16[384,6144]{1,0:T(8,128)(2,1)} %collective-permute-done.3.refs_0_, bf16[128,6144]{1,0:T(8,128)(2,1)S(1)} %collective-permute-done.refs_1_), custom_call_target="tpu_custom_call" | custom-call | flops 3221225472 | bytes 12582912 | tf_op jit(solution)/shard_map/first_density/pallas_call | solution.py:117
  255.3 2.7 copy-done.2
  258.1 2.7 products.5
  261.6 3.5 %all-to-all-start.2 = ((bf16[4,512,128]{2,1,0:T(8,128)(2,1)}), bf16[4,512,128]{2,1,0:T(8,128)(2,1)S(1)}, u32[]{:S(2)}, u32[]{:S(2)}) async-start(bf16[4,512,128]{2,1,0:T(8,128)(2,1)} %broadcast_in_dim.5), calls=%async_computation.2 | async-start | bytes 1048576 | tf_op jit(solution)/shard_map/all_to_all | solution.py:221
  266.3 1.5 collective-permute-start.5
  267.8 4.7 %collective-permute-done.5.refs_1_ = bf16[128,384]{1,0:T(8,128)(2,1)S(1)} collective-permute-done((bf16[128,384]{1,0:T(8,128)(2,1)S(1)}, bf16[128,384]{1,0:T(8,128)(2,1)S(1)}, u32[]{:S(2)}, u32[]{:S(2)}) %collective-permute-start.5) | collective-permute-done | bytes 98336 | tf_op jit(solution)/shard_map/ppermute | solution.py:190
  274.1 4.7 %all-to-all-start.1 = ((bf16[4,128,384]{2,1,0:T(8,128)(2,1)}), bf16[4,128,384]{2,1,0:T(8,128)(2,1)S(1)}, u32[]{:S(2)}, u32[]{:S(2)}) async-start(bf16[4,128,384]{2,1,0:T(8,128)(2,1)} %broadcast_in_dim.4), calls=%async_computation.1 | async-start | bytes 786432 | tf_op jit(solution)/shard_map/all_to_all | solution.py:216
  278.9 1.7 collective-permute-start.7
  280.6 5.0 %collective-permute-done.7.refs_1_ = bf16[512,128]{1,0:T(8,128)(2,1)S(1)} collective-permute-done((bf16[512,128]{1,0:T(8,128)(2,1)S(1)}, bf16[512,128]{1,0:T(8,128)(2,1)S(1)}, u32[]{:S(2)}, u32[]{:S(2)}) %collective-permute-start.7) | collective-permute-done | bytes 131104 | tf_op jit(solution)/shard_map/ppermute | solution.py:190
  285.6 1.5 amplitudes.5.refs_1_
  287.2 2.8 copy-done.3
  290.0 9.4 %last_density.1 = bf16[512,6144]{1,0:T(8,128)(2,1)} custom-call(bf16[512,384]{1,0:T(8,128)(2,1)S(1)} %bitcast.12, bf16[512,128]{1,0:T(8,128)(2,1)S(1)} %amplitudes.5.refs_1_, bf16[384,6144]{1,0:T(8,128)(2,1)} %collective-permute-done.4.refs_0_.refs_2_, bf16[128,6144]{1,0:T(8,128)(2,1)S(1)} %collective-permute-done.6.refs_0_.refs_3_, ...), custom_call_target="tpu_custom_call" | custom-call | flops 3221225472 | bytes 18874368 | tf_op jit(solution)/shard_map/last_density/pallas_call | solution.py:153
  (47 shorter events, 7.6 us)
Async XLA Ops:
  6.5 73.3 %copy-start.7 = (f32[32]{0:T(128)S(1)}, f32[32]{0:T(128)}, u32[]{:S(2)}) copy-start(f32[32]{0:T(128)} %param.4) | copy-start | bytes 388
  6.5 237.1 %all-reduce.2.cloned.1.call-start = ((), (), s32[]{:S(2)}) async-start(), calls=%async_computation.3 | async-start | bytes 1048576 | tf_op jit(solution)/shard_map/psum | solution.py:208
  6.5 4.2 %copy-start = (bf16[32,16,6144]{2,1,0:T(8,128)(2,1)S(1)}, bf16[32,16,6144]{2,1,0:T(8,128)(2,1)}, u32[]{:S(2)}) copy-start(bf16[32,16,6144]{2,1,0:T(8,128)(2,1)} %param.3) | copy-start | bytes 18874372
  9.3 77.0 %collective-permute-start.3 = (bf16[384,6144]{1,0:T(8,128)(2,1)S(1)}, bf16[384,6144]{1,0:T(8,128)(2,1)}, u32[]{:S(2)}, u32[]{:S(2)}) collective-permute-start(bf16[384,6144]{1,0:T(8,128)(2,1)S(1)} %bitcast.13), channel_id=1, source_target_pairs={{0,8},{8,16},{16,24},{24,32},{32,40},{40,48},{48,56},{56,64},{64,7... | collective-permute-start | bytes 14155784 | tf_op jit(solution)/shard_map/ppermute | solution.py:187
  10.9 68.9 %collective-permute-start = (bf16[128,6144]{1,0:T(8,128)(2,1)S(1)}, bf16[128,6144]{1,0:T(8,128)(2,1)S(1)}, u32[]{:S(2)}, u32[]{:S(2)}) collective-permute-start(bf16[128,6144]{1,0:T(8,128)(2,1)S(1)} %bitcast.14), channel_id=1, source_target_pairs={{0,8},{8,16},{16,24},{24,32},{32,40},{40,48},{48,56},{56,64},{64,7... | collective-permute-start | bytes 4718600 | tf_op jit(solution)/shard_map/ppermute | solution.py:187
  79.8 6.5 %collective-permute-start.2 = (f32[32]{0:T(128)S(1)}, f32[32]{0:T(128)S(1)}, u32[]{:S(2)}, u32[]{:S(2)}) collective-permute-start(f32[32]{0:T(128)S(1)} %copy-done.7), channel_id=1, source_target_pairs={{0,16},{8,24},{16,32},{24,40},{32,48},{40,56},{48,64},{56,72},{64,... | collective-permute-start | bytes 392 | tf_op jit(solution)/shard_map/ppermute | solution.py:187
  82.6 3.8 %collective-permute-start.1 = (f32[32]{0:T(128)S(1)}, f32[32]{0:T(128)S(1)}, u32[]{:S(2)}, u32[]{:S(2)}) collective-permute-start(f32[32]{0:T(128)S(1)} %copy-done.7), channel_id=1, source_target_pairs={{0,8},{8,16},{16,24},{24,32},{32,40},{40,48},{48,56},{56,64},{64,7... | collective-permute-start | bytes 392 | tf_op jit(solution)/shard_map/ppermute | solution.py:187
  86.4 53.9 %collective-permute-start.4 = (bf16[384,6144]{1,0:T(8,128)(2,1)}, bf16[384,6144]{1,0:T(8,128)(2,1)}, u32[]{:S(2)}, u32[]{:S(2)}) collective-permute-start(bf16[384,6144]{1,0:T(8,128)(2,1)} %collective-permute-done.3.refs_0_), channel_id=1, source_target_pairs={{0,8},{8,16},{16,24},{24,32},{32,40},{40,48},{48,56},{56,64},{64,7... | collective-permute-start | bytes 14155784 | tf_op jit(solution)/shard_map/ppermute | solution.py:187
  86.4 53.9 %copy-start.8 = (f32[16]{0:T(128)S(1)}, f32[16]{0:T(128)}, u32[]{:S(2)}) copy-start(f32[16]{0:T(128)} %param.5) | copy-start | bytes 196
  93.3 0.8 copy-start.4
  140.2 117.8 %collective-permute-start.6 = (bf16[128,6144]{1,0:T(8,128)(2,1)S(1)}, bf16[128,6144]{1,0:T(8,128)(2,1)S(1)}, u32[]{:S(2)}, u32[]{:S(2)}) collective-permute-start(bf16[128,6144]{1,0:T(8,128)(2,1)S(1)} %collective-permute-done.refs_1_), channel_id=1, source_target_pairs={{0,8},{8,16},{16,24},{24,32},{32,40},{40,48},{48,56},{56,64},{64,7... | collective-permute-start | bytes 4718600 | tf_op jit(solution)/shard_map/ppermute | solution.py:187
  140.6 2.8 copy-start.1
  150.2 0.8 copy-start.5
  151.0 109.7 %all-to-all-start = ((bf16[4,128,384]{2,1,0:T(8,128)(2,1)}), bf16[4,128,384]{2,1,0:T(8,128)(2,1)}, u32[]{:S(2)}, u32[]{:S(2)}) async-start(bf16[4,128,384]{2,1,0:T(8,128)(2,1)} %bitcast.11), calls=%async_computation | async-start | bytes 786432 | tf_op jit(solution)/shard_map/all_to_all | solution.py:211
  243.6 1.0 copy-start.6
  244.7 13.4 %slice-start = ((s8[6291456]{0:T(1024)(128)(4,1)}), s8[4194304]{0:T(1024)(128)(4,1)S(1)}, s32[]{:S(2)}) async-start(s8[6291456]{0:T(1024)(128)(4,1)} %bitcast.8), calls=%async_computation.4 | async-start | bytes 8388608
  248.1 9.9 %slice-start.1 = ((s8[6291456]{0:T(1024)(128)(4,1)}), s8[2097152]{0:T(1024)(128)(4,1)S(1)}, s32[]{:S(2)}) async-start(s8[6291456]{0:T(1024)(128)(4,1)} %bitcast.8), calls=%async_computation.5 | async-start | bytes 4194304
  255.3 2.7 copy-start.2
  261.6 11.7 %all-to-all-start.2 = ((bf16[4,512,128]{2,1,0:T(8,128)(2,1)}), bf16[4,512,128]{2,1,0:T(8,128)(2,1)S(1)}, u32[]{:S(2)}, u32[]{:S(2)}) async-start(bf16[4,512,128]{2,1,0:T(8,128)(2,1)} %broadcast_in_dim.5), calls=%async_computation.2 | async-start | bytes 1048576 | tf_op jit(solution)/shard_map/all_to_all | solution.py:221
  266.3 6.2 %collective-permute-start.5 = (bf16[128,384]{1,0:T(8,128)(2,1)S(1)}, bf16[128,384]{1,0:T(8,128)(2,1)S(1)}, u32[]{:S(2)}, u32[]{:S(2)}) collective-permute-start(bf16[128,384]{1,0:T(8,128)(2,1)S(1)} %convert_element_type.13), channel_id=1, source_target_pairs={{0,4},{1,5},{2,6},{3,7},{4,0},{5,1},{6,2},{7,3},{8,12},{9,13},{10,... | collective-permute-start | bytes 294920 | tf_op jit(solution)/shard_map/ppermute | solution.py:190
  274.1 13.1 %all-to-all-start.1 = ((bf16[4,128,384]{2,1,0:T(8,128)(2,1)}), bf16[4,128,384]{2,1,0:T(8,128)(2,1)S(1)}, u32[]{:S(2)}, u32[]{:S(2)}) async-start(bf16[4,128,384]{2,1,0:T(8,128)(2,1)} %broadcast_in_dim.4), calls=%async_computation.1 | async-start | bytes 786432 | tf_op jit(solution)/shard_map/all_to_all | solution.py:216
  278.9 6.7 %collective-permute-start.7 = (bf16[512,128]{1,0:T(8,128)(2,1)S(1)}, bf16[512,128]{1,0:T(8,128)(2,1)S(1)}, u32[]{:S(2)}, u32[]{:S(2)}) collective-permute-start(bf16[512,128]{1,0:T(8,128)(2,1)S(1)} %convert_element_type.15), channel_id=1, source_target_pairs={{0,4},{1,5},{2,6},{3,7},{4,0},{5,1},{6,2},{7,3},{8,12},{9,13},{10,... | collective-permute-start | bytes 393224 | tf_op jit(solution)/shard_map/ppermute | solution.py:190
  287.2 2.8 copy-start.3
Sparse Core Ops, SparseCore 0:
  140.4 103.2 all-reduce.1

commit v4 on v3

v4 whole, which is shorter than its diff:
```python
import functools

import jax
import jax.numpy as jnp
from jax import lax
from jax.experimental import pallas as pl
from jax.experimental.pallas import tpu as pltpu
from jax.sharding import PartitionSpec as P

VMEM_BYTES = 8 * 1024 * 1024


def after(value, *earlier):
    return lax.optimization_barrier((value,) + earlier)[0]


IN_VMEM = pl.BlockSpec(memory_space=pltpu.VMEM)


def part(ref, step, size):
    return ref[:, pl.ds(pl.multiple_of(step * size, size), size)]


def joined(arrays, dim):
    return arrays[0] if len(arrays) == 1 else jnp.concatenate(arrays, axis=dim)


def product_kernel(tile, left_ref, *refs):
    right, out_ref, total = refs[:-2], refs[-2], refs[-1]
    total[...] = jnp.zeros_like(total)

    def body(step, carry):
        total[...] += lax.dot_general(
            part(left_ref, step, tile),
            joined([part(ref, step, tile) for ref in right], 0),
            (((1,), (1,)), ((), ())),
            preferred_element_type=jnp.float32,
        )
        return carry

    lax.fori_loop(0, left_ref.shape[1] // tile, body, 0)
    out_ref[...] = total[...].astype(out_ref.dtype)


def products(left, right, tile):
    rows, depth = left.shape
    cols = sum(array.shape[0] for array in right)
    return pl.pallas_call(
        functools.partial(product_kernel, tile),
        out_shape=jax.ShapeDtypeStruct((rows, cols), jnp.bfloat16),
        in_specs=[IN_VMEM] * (1 + len(right)),
        out_specs=IN_VMEM,
        scratch_shapes=[pltpu.VMEM((rows, cols), jnp.float32)],
        compiler_params=pltpu.CompilerParams(vmem_limit_bytes=VMEM_BYTES),
        cost_estimate=pl.CostEstimate(
            flops=2 * rows * cols * depth, bytes_accessed=2 * (rows + cols) * depth, transcendentals=0
        ),
        name="products",
    )(left, *right)


def swapped(x, width):
    rows, cols = x.shape
    r = lax.broadcasted_iota(jnp.int32, x.shape, 0)
    c = lax.broadcasted_iota(jnp.int32, x.shape, 1)
    s = 1
    while s < width:
        below = pltpu.roll(pltpu.roll(x, rows - s, 0), s, 1)
        above = pltpu.roll(pltpu.roll(x, s, 0), cols - s, 1)
        r_bit, c_bit = (r & s) != 0, (c & s) != 0
        x = jnp.where(r_bit == c_bit, x, jnp.where(c_bit, below, above))
        s *= 2
    return x


def amplitude_kernel(width, parts_ref, row_ref, col_ref, out_ref):
    x = parts_ref[0].astype(jnp.float32)
    for part_at in range(1, parts_ref.shape[0]):
        x = x + parts_ref[part_at].astype(jnp.float32)
    result = ((2.0 * x - swapped(x, width)) / (row_ref[...] + col_ref[...])).astype(out_ref.dtype)
    for copy_at in range(out_ref.shape[0]):
        out_ref[copy_at] = result


def amplitudes(parts, row, col, width, copies):
    _, rows, cols = parts.shape
    return pl.pallas_call(
        functools.partial(amplitude_kernel, width),
        out_shape=jax.ShapeDtypeStruct((copies, rows, cols), jnp.bfloat16),
        in_specs=[IN_VMEM] * 3,
        out_specs=IN_VMEM,
        compiler_params=pltpu.CompilerParams(vmem_limit_bytes=VMEM_BYTES),
        cost_estimate=pl.CostEstimate(
            flops=60 * rows * cols, bytes_accessed=2 * parts.size, transcendentals=0
        ),
        name="amplitudes",
    )(parts, row, col)


def tile_density(amp, blocks, step, tile):
    block = joined([part(ref, step, tile) for ref in blocks], 0)
    return jnp.dot(amp, block, preferred_element_type=jnp.float32)


def first_density_kernel(tile, amp_ref, *refs):
    blocks, out_ref = refs[:-1], refs[-1]

    def body(step, carry):
        total = tile_density(amp_ref[...], blocks, step, tile)
        out_ref[:, pl.ds(pl.multiple_of(step * tile, tile), tile)] = total.astype(out_ref.dtype)
        return carry

    lax.fori_loop(0, out_ref.shape[1] // tile, body, 0)


def first_density(amp, blocks, tile):
    rows, cols = amp.shape[0], blocks[0].shape[1]
    return pl.pallas_call(
        functools.partial(first_density_kernel, tile),
        out_shape=jax.ShapeDtypeStruct((rows, cols), jnp.bfloat16),
        in_specs=[IN_VMEM] * (1 + len(blocks)),
        out_specs=IN_VMEM,
        compiler_params=pltpu.CompilerParams(vmem_limit_bytes=VMEM_BYTES),
        cost_estimate=pl.CostEstimate(
            flops=2 * rows * rows * cols, bytes_accessed=4 * rows * cols, transcendentals=0
        ),
        name="first_density",
    )(amp, *blocks)


def last_density_kernel(tile, n_blocks, amp_ref, *refs):
    blocks = refs[:n_blocks]
    start_ref, out_ref, buffers, sems = refs[n_blocks:]
    steps = start_ref.shape[1] // tile

    def copy_out(slot, step):
        columns = pl.ds(step * tile, tile)
        return pltpu.make_async_copy(buffers.at[slot], out_ref.at[:, columns], sems.at[slot])

    for step in range(steps):
        slot = step % 2
        if step >= 2:
            copy_out(slot, step - 2).wait()
        total = tile_density(amp_ref[...], blocks, step, tile) + part(start_ref, step, tile).astype(jnp.float32)
        buffers[slot] = total.astype(buffers.dtype)
        copy_out(slot, step).start()
    for step in range(max(steps - 2, 0), steps):
        copy_out(step % 2, step).wait()


def last_density(amp, blocks, start, tile):
    rows, cols = start.shape
    return pl.pallas_call(
        functools.partial(last_density_kernel, tile, len(blocks)),
        out_shape=jax.ShapeDtypeStruct((rows, cols), jnp.bfloat16),
        in_specs=[IN_VMEM] * (2 + len(blocks)),
        out_specs=pl.BlockSpec(memory_space=pl.ANY),
        scratch_shapes=[pltpu.VMEM((2, rows, tile), jnp.bfloat16), pltpu.SemaphoreType.DMA((2,))],
        compiler_params=pltpu.CompilerParams(vmem_limit_bytes=VMEM_BYTES),
        cost_estimate=pl.CostEstimate(
            flops=2 * rows * rows * cols, bytes_accessed=6 * rows * cols, transcendentals=0
        ),
        name="last_density",
    )(amp, *blocks, start)


def per_device(b_factor, occ_energy, virt_energy):
    occ_rows, slab, cols = b_factor.shape
    rows = occ_rows * slab
    n_occ, n_aux = lax.axis_size("occ"), lax.axis_size("aux")
    q = lax.axis_index("aux")
    n_y = n_aux // 2
    y_groups = [list(range(n_y)), list(range(n_y, n_aux))]
    x_groups = [[i, i + n_y] for i in range(n_y)]
    depth_tile, tile = cols // 6, cols // 8
    large = 3 * rows // 4

    def send(value, by=1):
        return lax.ppermute(value, "occ", [(i, (i + by) % n_occ) for i in range(n_occ)])

    def exchanged(value, groups):
        return lax.all_to_all(value, "aux", 0, 0, axis_index_groups=groups)

    def repeated(value, groups):
        return exchanged(jnp.broadcast_to(value, (len(groups[0]),) + value.shape), groups)

    def total(parts):
        return parts.astype(jnp.float32).sum(0).astype(jnp.bfloat16)

    own = b_factor.reshape(rows, cols)
    energy_near, energy_far = send(occ_energy), send(occ_energy, 2)
    near = send(own)
    ready = after(near, energy_near, energy_far)
    large_rows = ready[:large]
    far_large = send(large_rows)
    far_small = send(after(ready, large_rows)[large:])

    row = (occ_energy[:, None] - virt_energy[None, :]).reshape(rows, 1)
    near_col = (energy_near[:, None] - virt_energy[None, :]).reshape(1, rows)
    far_col = (energy_far[:, None] - virt_energy[None, :]).reshape(1, rows)

    def share(index, size):
        return lax.dynamic_slice(row, (index * size, 0), (size, 1))

    near_products = products(own, [near], depth_tile)
    y_sum = total(exchanged(near_products.reshape(n_y, rows // n_y, rows), y_groups))
    near_parts = repeated(y_sum, x_groups)
    near_slab = amplitudes(near_parts, share(q % n_y, rows // n_y), near_col, slab, n_y)
    amp_near = exchanged(near_slab, y_groups).reshape(rows, rows)
    near_density = first_density(amp_near, [near], tile)

    large_products = products(own, [after(far_large, near_density)], depth_tile)
    small_products = products(own, [after(far_small, large_products)], depth_tile)
    far_products = jnp.concatenate([large_products, small_products], axis=1)
    far_parts = lax.all_to_all(far_products.reshape(n_aux, rows // n_aux, rows), "aux", 0, 0)
    far_slab = amplitudes(far_parts, share(q, rows // n_aux), far_col, slab, n_aux)
    amp_far = lax.all_to_all(far_slab, "aux", 0, 0).reshape(rows, rows)
    gamma = last_density(amp_far, [far_large, far_small], near_density, tile)
    return gamma.reshape(occ_rows, slab, cols)


def solution(mesh):
    placed = (P("occ", None, "aux"), P("occ"), P())
    return jax.shard_map(
        per_device, mesh=mesh, in_specs=placed, out_specs=P("occ", None, "aux"), check_vma=False
    )
```

time: 308 us -> 231 us (0.75)
  waiting for transfers between devices: 216 us -> 138 us
  blocking collectives: 0 us -> 28.1 us
  between operations: 13.7 us -> 0.31 us
  Pallas kernels: 38.7 us -> 30.2 us
    psum x1 -> x0, waiting for transfers between devices: 88.2 us -> none  [per_device(): amp_near = amplitudes([lax.psum(near_products, 'aux')], row, near_col, slab)]
    all_to_all x3, waiting for transfers between devices: 0.01 us -> 71 us  [the longest x2 60.9 us: exchanged(): return lax.all_to_all(value, 'aux', 0, 0, axis_index_groups=groups)]
    ppermute x8 -> x5, waiting for transfers between devices: 128 us -> 67.2 us  [send(): lax.ppermute(value, 'occ', [(i, (i + by) % n_occ) for i in range(n_occ)])]
    all_to_all x0 -> x2, blocking collectives: none -> 28.1 us  [the longest x1 14.2 us: exchanged(): return lax.all_to_all(value, 'aux', 0, 0, axis_index_groups=groups)]
    pallas_call x3 -> x2, Pallas kernels: 5.72 us -> 1.3 us  [amplitudes(): pl.pallas_call(functools.partial(amplitude_kernel, width), out_shape=jax....]
    unnamed x22 -> x18, local copies, waits for them, and re-layouts: 12.2 us -> 8.29 us
    ppermute x8 -> x5, starting transfers between devices: 6.89 us -> 6.13 us  [send(): lax.ppermute(value, 'occ', [(i, (i + by) % n_occ) for i in range(n_occ)])]
  transfers between devices with their start and end apart: 12 -> 8, of which waited for: 6 -> 4; matrix products, arithmetic and copies ran while one was open for 1% -> 2% of each run, Pallas kernels for 10% -> 8%
where the time goes in v4:
time: 231 us; the launch traced here: 230 us
  waiting for transfers between devices  138 us (60%)
  Pallas kernels  30.2 us (13%)
  blocking collectives  28.1 us (12%)
  starting transfers between devices  17.5 us (8%)
  local copies, waits for them, and re-layouts  14.8 us (6%)
    ppermute x5, waiting for transfers between devices, send(): lax.ppermute(value, 'occ', [(i, (i + by) % n_occ) for i in range(n_occ)])  67.2 us
    all_to_all x2, waiting for transfers between devices, exchanged(): return lax.all_to_all(value, 'aux', 0, 0, axis_index_groups=groups)  60.9 us
    pallas_call x3, Pallas kernels, products(): pl.pallas_call(functools.partial(product_kernel, tile), out_shape=jax.Sha...  14.8 us
    all_to_all x1, blocking collectives, exchanged(): return lax.all_to_all(value, 'aux', 0, 0, axis_index_groups=groups)  14.2 us
    all_to_all x1, blocking collectives, per_device(): amp_far = lax.all_to_all(far_slab, 'aux', 0, 0).reshape(rows, rows)  13.9 us
    all_to_all x1, waiting for transfers between devices, per_device(): lax.all_to_all(far_products.reshape(n_aux, rows // n_aux, rows), 'aux', 0...  10.2 us
    pallas_call x1, Pallas kernels, last_density(): pl.pallas_call(functools.partial(last_density_kernel, tile, len(blocks)),...  9.38 us
    unnamed x18, local copies, waits for them, and re-layouts  8.29 us
  transfers between devices with their start and end apart: 8, of which 4 were waited for; matrix products, arithmetic and copies ran while one was open for 2% of the time, Pallas kernels for 8%

profile of v4, /device:TPU:2, one launch (start us, length us, event | category | flops | bytes accessed | tf_op | source)
XLA Modules:
  0.0 230.2 jit_solution(13852505117955152973)
XLA Ops:
  0.0 2.0 collective-permute-start.1
  2.0 1.5 collective-permute-start.2
  3.5 67.2 %collective-permute-done.1 = f32[32]{0:T(128)S(1)} collective-permute-done((f32[32]{0:T(128)}, f32[32]{0:T(128)S(1)}, u32[]{:S(2)}, u32[]{:S(2)}) %collective-permute-start.1) | collective-permute-done | bytes 160 | tf_op jit(solution)/shard_map/ppermute | solution.py:179
  70.7 2.7 %slice.6 = bf16[384,6144]{1,0:T(8,128)(2,1)} slice(bf16[512,6144]{1,0:T(8,128)(2,1)S(1)} %collective-permute-done.refs_0_), slice={[0:384], [0:6144]} | slice | bytes 9437184 | tf_op jit(solution)/shard_map/slice | solution.py:194
  73.5 5.4 %products.3 = bf16[512,512]{1,0:T(8,128)(2,1)} custom-call(bf16[512,6144]{1,0:T(8,128)(2,1)S(1)} %bitcast.7, bf16[512,6144]{1,0:T(8,128)(2,1)S(1)} %collective-permute-done.refs_0_), custom_call_target="tpu_custom_call" | custom-call | flops 3221225472 | bytes 12582912 | tf_op jit(solution)/shard_map/products/pallas_call | solution.py:48
  78.8 4.5 %all-to-all-start = ((bf16[4,128,512]{2,1,0:T(8,128)(2,1)}), bf16[4,128,512]{2,1,0:T(8,128)(2,1)S(1)}, u32[]{:S(2)}, u32[]{:S(2)}) async-start(bf16[4,128,512]{2,1,0:T(8,128)(2,1)} %bitcast.1), calls=%async_computation | async-start | bytes 1048576 | tf_op jit(solution)/shard_map/all_to_all | solution.py:182
  83.3 2.7 %slice.7 = bf16[128,6144]{1,0:T(8,128)(2,1)} slice(bf16[512,6144]{1,0:T(8,128)(2,1)} %copy-done.1), slice={[384:512], [0:6144]} | slice | bytes 3145728 | tf_op jit(solution)/shard_map/slice | solution.py:196
  86.0 2.6 %collective-permute-start.4 = (bf16[128,6144]{1,0:T(8,128)(2,1)}, bf16[128,6144]{1,0:T(8,128)(2,1)S(1)}, u32[]{:S(2)}, u32[]{:S(2)}) collective-permute-start(bf16[128,6144]{1,0:T(8,128)(2,1)} %slice.7), channel_id=1, source_target_pairs={{0,8},{8,16},{16,24},{24,32},{32,40},{40,48},{48,56},{56,64},{64,7... | collective-permute-start | bytes 4718600 | tf_op jit(solution)/shard_map/ppermute | solution.py:179
  88.6 3.9 %all-to-all-done = bf16[4,128,512]{2,1,0:T(8,128)(2,1)S(1)} async-done(((bf16[4,128,512]{2,1,0:T(8,128)(2,1)}), bf16[4,128,512]{2,1,0:T(8,128)(2,1)S(1)}, u32[]{:S(2)}, u32[]{:S(2)}) %all-to-all-start) | async-done | bytes 524320 | tf_op jit(solution)/shard_map/all_to_all | solution.py:182
  93.3 3.4 %all-to-all-start.1 = ((bf16[2,128,512]{2,1,0:T(8,128)(2,1)}), bf16[2,128,512]{2,1,0:T(8,128)(2,1)S(1)}, u32[]{:S(2)}, u32[]{:S(2)}) async-start(bf16[2,128,512]{2,1,0:T(8,128)(2,1)} %broadcast_in_dim.2), calls=%async_computation.1 | async-start | bytes 524288 | tf_op jit(solution)/shard_map/all_to_all | solution.py:182
  97.1 57.0 %all-to-all-done.1.parts_ref = bf16[2,128,512]{2,1,0:T(8,128)(2,1)S(1)} async-done(((bf16[2,128,512]{2,1,0:T(8,128)(2,1)}), bf16[2,128,512]{2,1,0:T(8,128)(2,1)S(1)}, u32[]{:S(2)}, u32[]{:S(2)}) %all-to-all-start.1) | async-done | bytes 262176 | tf_op jit(solution)/shard_map/all_to_all | solution.py:182
  154.1 0.7 amplitudes.2
  154.8 14.2 %all_to_all.25 = bf16[4,128,512]{2,1,0:T(8,128)(2,1)S(1)} all-to-all(bf16[4,128,512]{2,1,0:T(8,128)(2,1)S(1)} %amplitudes.2), channel_id=1, replica_groups={{0,1,2,3},{4,5,6,7},{8,9,10,11},{12,13,14,15},{16,17,18,19},{20,21,22,2..., dimensions={0} | all-to-all | bytes 1048576 | tf_op jit(solution)/shard_map/all_to_all | solution.py:182
  169.1 2.8 %copy-done.2 = bf16[512,6144]{1,0:T(8,128)(2,1)S(1)} copy-done((bf16[512,6144]{1,0:T(8,128)(2,1)S(1)}, bf16[512,6144]{1,0:T(8,128)(2,1)}, u32[]{:S(2)}) %copy-start.2) | copy-done | bytes 6291480
  171.9 4.7 %first_density.1.refs_2_ = bf16[512,6144]{1,0:T(8,128)(2,1)S(1)} custom-call(bf16[512,512]{1,0:T(8,128)(2,1)S(1)} %bitcast.13, bf16[512,6144]{1,0:T(8,128)(2,1)S(1)} %copy-done.2), custom_call_target="tpu_custom_call" | custom-call | flops 3221225472 | bytes 12582912 | tf_op jit(solution)/shard_map/first_density/pallas_call | solution.py:118
  176.6 2.7 %copy-done.3 = bf16[512,6144]{1,0:T(8,128)(2,1)} copy-done((bf16[512,6144]{1,0:T(8,128)(2,1)}, bf16[512,6144]{1,0:T(8,128)(2,1)S(1)}, u32[]{:S(2)}) %copy-start.3) | copy-done | bytes 6291480
  179.3 6.8 %products.4 = bf16[512,384]{1,0:T(8,128)(2,1)S(1)} custom-call(bf16[512,6144]{1,0:T(8,128)(2,1)S(1)} %bitcast.10, bf16[384,6144]{1,0:T(8,128)(2,1)} %collective-permute-done.3.refs_0_), custom_call_target="tpu_custom_call" | custom-call | flops 2415919104 | bytes 11010048 | tf_op jit(solution)/shard_map/products/pallas_call | solution.py:48
  186.2 2.7 %products.5 = bf16[512,128]{1,0:T(8,128)(2,1)S(1)} custom-call(bf16[512,6144]{1,0:T(8,128)(2,1)S(1)} %bitcast.11, bf16[128,6144]{1,0:T(8,128)(2,1)S(1)} %collective-permute-done.4.refs_0_.refs_1_), custom_call_target="tpu_custom_call" | custom-call | flops 805306368 | bytes 7864320 | tf_op jit(solution)/shard_map/products/pallas_call | solution.py:48
  188.8 0.8 pad_maximum_fusion
  189.7 3.5 %all-to-all-start.3 = ((bf16[8,64,512]{2,1,0:T(8,128)(2,1)}), bf16[8,64,512]{2,1,0:T(8,128)(2,1)S(1)}, u32[]{:S(2)}, u32[]{:S(2)}) async-start(bf16[8,64,512]{2,1,0:T(8,128)(2,1)} %bitcast.3), calls=%async_computation.3 | async-start | bytes 1048576 | tf_op jit(solution)/shard_map/all_to_all | solution.py:215
  193.3 10.2 %all-to-all-done.3.parts_ref = bf16[8,64,512]{2,1,0:T(8,128)(2,1)S(1)} async-done(((bf16[8,64,512]{2,1,0:T(8,128)(2,1)}), bf16[8,64,512]{2,1,0:T(8,128)(2,1)S(1)}, u32[]{:S(2)}, u32[]{:S(2)}) %all-to-all-start.3) | async-done | bytes 524320 | tf_op jit(solution)/shard_map/all_to_all | solution.py:215
  204.0 13.9 %all_to_all.26 = bf16[8,64,512]{2,1,0:T(8,128)(2,1)S(1)} all-to-all(bf16[8,64,512]{2,1,0:T(8,128)(2,1)S(1)} %amplitudes.3), channel_id=1, replica_groups=mesh['occ'=32,'aux'=8] {'aux'}, dimensions={0} | all-to-all | bytes 1048576 | tf_op jit(solution)/shard_map/all_to_all | solution.py:217
  217.9 2.8 %copy-done.4 = bf16[512,6144]{1,0:T(8,128)(2,1)S(1)} copy-done((bf16[512,6144]{1,0:T(8,128)(2,1)S(1)}, bf16[512,6144]{1,0:T(8,128)(2,1)}, u32[]{:S(2)}) %copy-start.4) | copy-done | bytes 6291480
  220.6 9.4 %last_density.1 = bf16[512,6144]{1,0:T(8,128)(2,1)} custom-call(bf16[512,512]{1,0:T(8,128)(2,1)S(1)} %bitcast.12, bf16[384,6144]{1,0:T(8,128)(2,1)} %collective-permute-done.3.refs_0_, bf16[128,6144]{1,0:T(8,128)(2,1)S(1)} %collective-permute-done.4.refs_0_.refs_1_, bf16[512,6144]{1,0:T(8,128)(2,1)S(1)} %copy-done.4), custom_call_target="tpu_custom_call" | custom-call | flops 3221225472 | bytes 18874368 | tf_op jit(solution)/shard_map/last_density/pallas_call | solution.py:153
  (31 shorter events, 1.9 us)
Async XLA Ops:
  0.0 73.5 %copy-start = (bf16[32,16,6144]{2,1,0:T(8,128)(2,1)S(1)}, bf16[32,16,6144]{2,1,0:T(8,128)(2,1)}, u32[]{:S(2)}) copy-start(bf16[32,16,6144]{2,1,0:T(8,128)(2,1)} %param.3) | copy-start | bytes 18874372
  0.0 70.7 %collective-permute-start = (bf16[512,6144]{1,0:T(8,128)(2,1)}, bf16[512,6144]{1,0:T(8,128)(2,1)S(1)}, u32[]{:S(2)}, u32[]{:S(2)}) collective-permute-start(bf16[512,6144]{1,0:T(8,128)(2,1)} %bitcast.6), channel_id=1, source_target_pairs={{0,8},{8,16},{16,24},{24,32},{32,40},{40,48},{48,56},{56,64},{64,7... | collective-permute-start | bytes 18874376 | tf_op jit(solution)/shard_map/ppermute | solution.py:179
  0.0 70.7 %collective-permute-start.1 = (f32[32]{0:T(128)}, f32[32]{0:T(128)S(1)}, u32[]{:S(2)}, u32[]{:S(2)}) collective-permute-start(f32[32]{0:T(128)} %param.4), channel_id=1, source_target_pairs={{0,8},{8,16},{16,24},{24,32},{32,40},{40,48},{48,56},{56,64},{64,7... | collective-permute-start | bytes 392 | tf_op jit(solution)/shard_map/ppermute | solution.py:179
  2.0 68.7 %collective-permute-start.2 = (f32[32]{0:T(128)}, f32[32]{0:T(128)S(1)}, u32[]{:S(2)}, u32[]{:S(2)}) collective-permute-start(f32[32]{0:T(128)} %param.4), channel_id=1, source_target_pairs={{0,16},{8,24},{16,32},{24,40},{32,48},{40,56},{48,64},{56,72},{64,... | collective-permute-start | bytes 392 | tf_op jit(solution)/shard_map/ppermute | solution.py:179
  70.7 8.1 %copy-start.1 = (bf16[512,6144]{1,0:T(8,128)(2,1)}, bf16[512,6144]{1,0:T(8,128)(2,1)S(1)}, u32[]{:S(2)}) copy-start(bf16[512,6144]{1,0:T(8,128)(2,1)S(1)} %collective-permute-done.refs_0_) | copy-start | bytes 18874372
  73.4 23.3 %copy-start.5 = (f32[32]{0:T(128)S(1)}, f32[32]{0:T(128)}, u32[]{:S(2)}) copy-start(f32[32]{0:T(128)} %param.4) | copy-start | bytes 388
  73.4 23.3 %copy-start.6 = (f32[16]{0:T(128)S(1)}, f32[16]{0:T(128)}, u32[]{:S(2)}) copy-start(f32[16]{0:T(128)} %param.5) | copy-start | bytes 196
  73.4 105.9 %collective-permute-start.3 = (bf16[384,6144]{1,0:T(8,128)(2,1)}, bf16[384,6144]{1,0:T(8,128)(2,1)}, u32[]{:S(2)}, u32[]{:S(2)}) collective-permute-start(bf16[384,6144]{1,0:T(8,128)(2,1)} %slice.6), channel_id=1, source_target_pairs={{0,8},{8,16},{16,24},{24,32},{32,40},{40,48},{48,56},{56,64},{64,7... | collective-permute-start | bytes 14155784 | tf_op jit(solution)/shard_map/ppermute | solution.py:179
  78.8 13.7 %all-to-all-start = ((bf16[4,128,512]{2,1,0:T(8,128)(2,1)}), bf16[4,128,512]{2,1,0:T(8,128)(2,1)S(1)}, u32[]{:S(2)}, u32[]{:S(2)}) async-start(bf16[4,128,512]{2,1,0:T(8,128)(2,1)} %bitcast.1), calls=%async_computation | async-start | bytes 1048576 | tf_op jit(solution)/shard_map/all_to_all | solution.py:182
  86.0 100.2 %collective-permute-start.4 = (bf16[128,6144]{1,0:T(8,128)(2,1)}, bf16[128,6144]{1,0:T(8,128)(2,1)S(1)}, u32[]{:S(2)}, u32[]{:S(2)}) collective-permute-start(bf16[128,6144]{1,0:T(8,128)(2,1)} %slice.7), channel_id=1, source_target_pairs={{0,8},{8,16},{16,24},{24,32},{32,40},{40,48},{48,56},{56,64},{64,7... | collective-permute-start | bytes 4718600 | tf_op jit(solution)/shard_map/ppermute | solution.py:179
  93.3 60.8 %all-to-all-start.1 = ((bf16[2,128,512]{2,1,0:T(8,128)(2,1)}), bf16[2,128,512]{2,1,0:T(8,128)(2,1)S(1)}, u32[]{:S(2)}, u32[]{:S(2)}) async-start(bf16[2,128,512]{2,1,0:T(8,128)(2,1)} %broadcast_in_dim.2), calls=%async_computation.1 | async-start | bytes 524288 | tf_op jit(solution)/shard_map/all_to_all | solution.py:182
  154.8 24.5 %slice-start = ((s8[6291456]{0:T(1024)(128)(4,1)}), s8[4194304]{0:T(1024)(128)(4,1)S(1)}, s32[]{:S(2)}) async-start(s8[6291456]{0:T(1024)(128)(4,1)} %bitcast.8), calls=%async_computation.5 | async-start | bytes 8388608
  169.1 2.8 %copy-start.2 = (bf16[512,6144]{1,0:T(8,128)(2,1)S(1)}, bf16[512,6144]{1,0:T(8,128)(2,1)}, u32[]{:S(2)}) copy-start(bf16[512,6144]{1,0:T(8,128)(2,1)} %copy-done.1) | copy-start | bytes 18874372
  171.9 7.4 %slice-start.1 = ((s8[6291456]{0:T(1024)(128)(4,1)}), s8[2097152]{0:T(1024)(128)(4,1)S(1)}, s32[]{:S(2)}) async-start(s8[6291456]{0:T(1024)(128)(4,1)} %bitcast.8), calls=%async_computation.6 | async-start | bytes 4194304
  176.6 2.7 %copy-start.3 = (bf16[512,6144]{1,0:T(8,128)(2,1)}, bf16[512,6144]{1,0:T(8,128)(2,1)S(1)}, u32[]{:S(2)}) copy-start(bf16[512,6144]{1,0:T(8,128)(2,1)S(1)} %first_density.1.refs_2_) | copy-start | bytes 18874372
  189.7 13.7 %all-to-all-start.3 = ((bf16[8,64,512]{2,1,0:T(8,128)(2,1)}), bf16[8,64,512]{2,1,0:T(8,128)(2,1)S(1)}, u32[]{:S(2)}, u32[]{:S(2)}) async-start(bf16[8,64,512]{2,1,0:T(8,128)(2,1)} %bitcast.3), calls=%async_computation.3 | async-start | bytes 1048576 | tf_op jit(solution)/shard_map/all_to_all | solution.py:215
  217.9 2.8 %copy-start.4 = (bf16[512,6144]{1,0:T(8,128)(2,1)S(1)}, bf16[512,6144]{1,0:T(8,128)(2,1)}, u32[]{:S(2)}) copy-start(bf16[512,6144]{1,0:T(8,128)(2,1)} %copy-done.3) | copy-start | bytes 18874372

commit v5 on v4

--- a/solution.py
+++ b/solution.py
@@ -25,8 +25,8 @@
     return arrays[0] if len(arrays) == 1 else jnp.concatenate(arrays, axis=dim)
 
 
-def product_kernel(tile, left_ref, *refs):
-    right, out_ref, total = refs[:-2], refs[-2], refs[-1]
+def product_kernel(tile, n_right, left_ref, *refs):
+    right, before, out_ref, total = refs[:n_right], refs[n_right:-2], refs[-2], refs[-1]
     total[...] = jnp.zeros_like(total)
 
     def body(step, carry):
@@ -39,16 +39,17 @@
         return carry
 
     lax.fori_loop(0, left_ref.shape[1] // tile, body, 0)
-    out_ref[...] = total[...].astype(out_ref.dtype)
-
-
-def products(left, right, tile):
+    out_ref[...] = joined([ref[...] for ref in before] + [total[...].astype(out_ref.dtype)], 1)
+
+
+def products(left, right, tile, before=()):
     rows, depth = left.shape
     cols = sum(array.shape[0] for array in right)
-    return pl.pallas_call(
-        functools.partial(product_kernel, tile),
-        out_shape=jax.ShapeDtypeStruct((rows, cols), jnp.bfloat16),
-        in_specs=[IN_VMEM] * (1 + len(right)),
+    width = cols + sum(array.shape[1] for array in before)
+    return pl.pallas_call(
+        functools.partial(product_kernel, tile, len(right)),
+        out_shape=jax.ShapeDtypeStruct((rows, width), jnp.bfloat16),
+        in_specs=[IN_VMEM] * (1 + len(right) + len(before)),
         out_specs=IN_VMEM,
         scratch_shapes=[pltpu.VMEM((rows, cols), jnp.float32)],
         compiler_params=pltpu.CompilerParams(vmem_limit_bytes=VMEM_BYTES),
@@ -56,7 +57,7 @@
             flops=2 * rows * cols * depth, bytes_accessed=2 * (rows + cols) * depth, transcendentals=0
         ),
         name="products",
-    )(left, *right)
+    )(left, *right, *before)
 
 
 def swapped(x, width):
@@ -128,35 +129,22 @@
     )(amp, *blocks)
 
 
-def last_density_kernel(tile, n_blocks, amp_ref, *refs):
-    blocks = refs[:n_blocks]
-    start_ref, out_ref, buffers, sems = refs[n_blocks:]
-    steps = start_ref.shape[1] // tile
-
-    def copy_out(slot, step):
-        columns = pl.ds(step * tile, tile)
-        return pltpu.make_async_copy(buffers.at[slot], out_ref.at[:, columns], sems.at[slot])
-
-    for step in range(steps):
-        slot = step % 2
-        if step >= 2:
-            copy_out(slot, step - 2).wait()
-        total = tile_density(amp_ref[...], blocks, step, tile) + part(start_ref, step, tile).astype(jnp.float32)
-        buffers[slot] = total.astype(buffers.dtype)
-        copy_out(slot, step).start()
-    for step in range(max(steps - 2, 0), steps):
-        copy_out(step % 2, step).wait()
+def last_density_kernel(amp_ref, *refs):
+    blocks, start_ref, out_ref = refs[:-2], refs[-2], refs[-1]
+    total = jnp.dot(amp_ref[...], joined([ref[...] for ref in blocks], 0), preferred_element_type=jnp.float32)
+    out_ref[...] = (total + start_ref[...].astype(jnp.float32)).astype(out_ref.dtype)
 
 
 def last_density(amp, blocks, start, tile):
     rows, cols = start.shape
     return pl.pallas_call(
-        functools.partial(last_density_kernel, tile, len(blocks)),
+        last_density_kernel,
         out_shape=jax.ShapeDtypeStruct((rows, cols), jnp.bfloat16),
-        in_specs=[IN_VMEM] * (2 + len(blocks)),
-        out_specs=pl.BlockSpec(memory_space=pl.ANY),
-        scratch_shapes=[pltpu.VMEM((2, rows, tile), jnp.bfloat16), pltpu.SemaphoreType.DMA((2,))],
-        compiler_params=pltpu.CompilerParams(vmem_limit_bytes=VMEM_BYTES),
+        grid=(cols // tile,),
+        in_specs=[pl.BlockSpec(amp.shape, lambda c: (0, 0))]
+        + [pl.BlockSpec((array.shape[0], tile), lambda c: (0, c)) for array in (*blocks, start)],
+        out_specs=pl.BlockSpec((rows, tile), lambda c: (0, c)),
+        compiler_params=pltpu.CompilerParams(vmem_limit_bytes=2 * VMEM_BYTES),
         cost_estimate=pl.CostEstimate(
             flops=2 * rows * rows * cols, bytes_accessed=6 * rows * cols, transcendentals=0
         ),
@@ -173,7 +161,7 @@
     y_groups = [list(range(n_y)), list(range(n_y, n_aux))]
     x_groups = [[i, i + n_y] for i in range(n_y)]
     depth_tile, tile = cols // 6, cols // 8
-    large = 3 * rows // 4
+    far_rows = [slice(0, 3 * rows // 8), slice(3 * rows // 8, 3 * rows // 4), slice(3 * rows // 4, rows)]
 
     def send(value, by=1):
         return lax.ppermute(value, "occ", [(i, (i + by) % n_occ) for i in range(n_occ)])
@@ -191,9 +179,8 @@
     energy_near, energy_far = send(occ_energy), send(occ_energy, 2)
     near = send(own)
     ready = after(near, energy_near, energy_far)
-    large_rows = ready[:large]
-    far_large = send(large_rows)
-    far_small = send(after(ready, large_rows)[large:])
+    first_rows = ready[far_rows[0]]
+    far = [send(first_rows)]
 
     row = (occ_energy[:, None] - virt_energy[None, :]).reshape(rows, 1)
     near_col = (energy_near[:, None] - virt_energy[None, :]).reshape(1, rows)
@@ -202,20 +189,21 @@
     def share(index, size):
         return lax.dynamic_slice(row, (index * size, 0), (size, 1))
 
-    near_products = products(own, [near], depth_tile)
+    near_products = products(own, [after(near, first_rows)], depth_tile)
     y_sum = total(exchanged(near_products.reshape(n_y, rows // n_y, rows), y_groups))
     near_parts = repeated(y_sum, x_groups)
+    ready = after(ready, near_parts, far[0])
+    far += [send(ready[far_rows[1]]), send(ready[far_rows[2]])]
     near_slab = amplitudes(near_parts, share(q % n_y, rows // n_y), near_col, slab, n_y)
     amp_near = exchanged(near_slab, y_groups).reshape(rows, rows)
     near_density = first_density(amp_near, [near], tile)
 
-    large_products = products(own, [after(far_large, near_density)], depth_tile)
-    small_products = products(own, [after(far_small, large_products)], depth_tile)
-    far_products = jnp.concatenate([large_products, small_products], axis=1)
+    first_products = products(own, [far[0], after(far[1], near_density)], depth_tile)
+    far_products = products(own, [after(far[2], first_products)], depth_tile, (first_products,))
     far_parts = lax.all_to_all(far_products.reshape(n_aux, rows // n_aux, rows), "aux", 0, 0)
     far_slab = amplitudes(far_parts, share(q, rows // n_aux), far_col, slab, n_aux)
     amp_far = lax.all_to_all(far_slab, "aux", 0, 0).reshape(rows, rows)
-    gamma = last_density(amp_far, [far_large, far_small], near_density, tile)
+    gamma = last_density(amp_far, far, near_density, tile)
     return gamma.reshape(occ_rows, slab, cols)
 
 

time: 231 us -> 206 us (0.89)
  waiting for transfers between devices: 138 us -> 87.9 us
  blocking collectives: 28.1 us -> 55.5 us
  starting transfers between devices: 17.5 us -> 8.94 us
  local copies, waits for them, and re-layouts: 14.8 us -> 21.7 us
    all_to_all x2 -> x0, waiting for transfers between devices: 60.9 us -> none  [exchanged(): return lax.all_to_all(value, 'aux', 0, 0, axis_index_groups=groups)]
    all_to_all x1 -> x3, blocking collectives: 14.2 us -> 42.4 us  [exchanged(): return lax.all_to_all(value, 'aux', 0, 0, axis_index_groups=groups)]
    ppermute x5 -> x6, waiting for transfers between devices: 67.2 us -> 78.2 us  [send(): lax.ppermute(value, 'occ', [(i, (i + by) % n_occ) for i in range(n_occ)])]
    all_to_all x2 -> x0, starting transfers between devices: 7.92 us -> none  [exchanged(): return lax.all_to_all(value, 'aux', 0, 0, axis_index_groups=groups)]
    unnamed x18, local copies, waits for them, and re-layouts: 8.29 us -> 13.8 us
    ppermute x5 -> x6, starting transfers between devices: 6.13 us -> 3.67 us  [send(): lax.ppermute(value, 'occ', [(i, (i + by) % n_occ) for i in range(n_occ)])]
    slice x2 -> x3, local copies, waits for them, and re-layouts: 5.41 us -> 7.59 us  [the longest x2 5.99 us: per_device(): far += [send(ready[far_rows[1]]), send(ready[far_rows[2]])]]
  transfers between devices with their start and end apart: 8 -> 7, of which waited for: 4 -> 4; matrix products, arithmetic and copies ran while one was open for 2% -> 2% of each run, Pallas kernels for 8% -> 8%
where the time goes in v5:
time: 206 us; the launch traced here: 205 us
  waiting for transfers between devices  87.9 us (43%)
  blocking collectives  55.5 us (27%)
  Pallas kernels  30.5 us (15%)
  local copies, waits for them, and re-layouts  21.7 us (11%)
  starting transfers between devices  8.94 us (4%)
    ppermute x6, waiting for transfers between devices, send(): lax.ppermute(value, 'occ', [(i, (i + by) % n_occ) for i in range(n_occ)])  78.2 us
    all_to_all x3, blocking collectives, exchanged(): return lax.all_to_all(value, 'aux', 0, 0, axis_index_groups=groups)  42.4 us
    pallas_call x3, Pallas kernels, products(): pl.pallas_call(functools.partial(product_kernel, tile, len(right)), out_s...  15.6 us
    unnamed x18, local copies, waits for them, and re-layouts  13.8 us
    all_to_all x1, blocking collectives, per_device(): amp_far = lax.all_to_all(far_slab, 'aux', 0, 0).reshape(rows, rows)  13.1 us
    all_to_all x1, waiting for transfers between devices, per_device(): lax.all_to_all(far_products.reshape(n_aux, rows // n_aux, rows), 'aux', 0...  9.7 us
    pallas_call x1, Pallas kernels, last_density(): pl.pallas_call(last_density_kernel, out_shape=jax.ShapeDtypeStruct((rows,...  8.94 us
    slice x2, local copies, waits for them, and re-layouts, per_device(): far += [send(ready[far_rows[1]]), send(ready[far_rows[2]])]  5.99 us
  transfers between devices with their start and end apart: 7, of which 4 were waited for; matrix products, arithmetic and copies ran while one was open for 2% of the time, Pallas kernels for 8%

profile of v5, /device:TPU:2, one launch (start us, length us, event | category | flops | bytes accessed | tf_op | source)
XLA Modules:
  0.0 204.8 jit_solution(10351479317487161521)
XLA Ops:
  0.0 2.0 collective-permute-start.1
  2.0 1.5 collective-permute-start.2
  3.5 67.2 %collective-permute-done.1 = f32[32]{0:T(128)S(1)} collective-permute-done((f32[32]{0:T(128)}, f32[32]{0:T(128)S(1)}, u32[]{:S(2)}, u32[]{:S(2)}) %collective-permute-start.1) | collective-permute-done | bytes 160 | tf_op jit(solution)/shard_map/ppermute | solution.py:167
  70.7 1.6 slice.9
  72.3 2.8 %copy-done = bf16[32,16,6144]{2,1,0:T(8,128)(2,1)S(1)} copy-done((bf16[32,16,6144]{2,1,0:T(8,128)(2,1)S(1)}, bf16[32,16,6144]{2,1,0:T(8,128)(2,1)}, u32[]{:S(2)}) %copy-start) | copy-done | bytes 6291480
  75.1 4.6 %products.3 = bf16[512,512]{1,0:T(8,128)(2,1)S(1)} custom-call(bf16[512,6144]{1,0:T(8,128)(2,1)S(1)} %bitcast.7, bf16[512,6144]{1,0:T(8,128)(2,1)S(1)} %collective-permute-done.refs_0_), custom_call_target="tpu_custom_call" | custom-call | flops 3221225472 | bytes 12582912 | tf_op jit(solution)/shard_map/products/pallas_call | solution.py:49
  79.7 2.7 %copy-done.1 = bf16[512,6144]{1,0:T(8,128)(2,1)} copy-done((bf16[512,6144]{1,0:T(8,128)(2,1)}, bf16[512,6144]{1,0:T(8,128)(2,1)S(1)}, u32[]{:S(2)}) %copy-start.1) | copy-done | bytes 6291480
  82.4 13.4 %all_to_all.25 = bf16[4,128,512]{2,1,0:T(8,128)(2,1)S(1)} all-to-all(bf16[4,128,512]{2,1,0:T(8,128)(2,1)S(1)} %bitcast.14), channel_id=1, replica_groups={{0,1,2,3},{4,5,6,7},{8,9,10,11},{12,13,14,15},{16,17,18,19},{20,21,22,2..., dimensions={0} | all-to-all | bytes 1048576 | tf_op jit(solution)/shard_map/all_to_all | solution.py:170
  95.9 14.8 %all_to_all.26.parts_ref = bf16[2,128,512]{2,1,0:T(8,128)(2,1)S(1)} all-to-all(bf16[2,128,512]{2,1,0:T(8,128)(2,1)S(1)} %broadcast_in_dim.2), channel_id=1, replica_groups={{0,4},{1,5},{2,6},{3,7},{8,12},{9,13},{10,14},{11,15},{16,20},{17,21},{..., dimensions={0} | all-to-all | bytes 524288 | tf_op jit(solution)/shard_map/all_to_all | solution.py:170
  110.7 3.3 %slice.11 = bf16[192,6144]{1,0:T(8,128)(2,1)} slice(bf16[512,6144]{1,0:T(8,128)(2,1)} %copy-done.1), slice={[192:384], [0:6144]} | slice | bytes 4718592 | tf_op jit(solution)/shard_map/slice | solution.py:196
  114.2 2.7 %slice.10 = bf16[128,6144]{1,0:T(8,128)(2,1)} slice(bf16[512,6144]{1,0:T(8,128)(2,1)} %copy-done.1), slice={[384:512], [0:6144]} | slice | bytes 3145728 | tf_op jit(solution)/shard_map/slice | solution.py:196
  117.2 0.7 amplitudes.2
  118.0 14.1 %all_to_all.27 = bf16[4,128,512]{2,1,0:T(8,128)(2,1)S(1)} all-to-all(bf16[4,128,512]{2,1,0:T(8,128)(2,1)S(1)} %amplitudes.2), channel_id=1, replica_groups={{0,1,2,3},{4,5,6,7},{8,9,10,11},{12,13,14,15},{16,17,18,19},{20,21,22,2..., dimensions={0} | all-to-all | bytes 1048576 | tf_op jit(solution)/shard_map/all_to_all | solution.py:170
  132.1 2.8 %copy-done.2 = bf16[512,6144]{1,0:T(8,128)(2,1)S(1)} copy-done((bf16[512,6144]{1,0:T(8,128)(2,1)S(1)}, bf16[512,6144]{1,0:T(8,128)(2,1)}, u32[]{:S(2)}) %copy-start.2) | copy-done | bytes 6291480
  134.9 4.7 %first_density.1.refs_3_ = bf16[512,6144]{1,0:T(8,128)(2,1)S(1)} custom-call(bf16[512,512]{1,0:T(8,128)(2,1)S(1)} %bitcast.13, bf16[512,6144]{1,0:T(8,128)(2,1)S(1)} %copy-done.2), custom_call_target="tpu_custom_call" | custom-call | flops 3221225472 | bytes 12582912 | tf_op jit(solution)/shard_map/first_density/pallas_call | solution.py:119
  139.6 2.7 %copy-done.3 = bf16[512,6144]{1,0:T(8,128)(2,1)} copy-done((bf16[512,6144]{1,0:T(8,128)(2,1)}, bf16[512,6144]{1,0:T(8,128)(2,1)S(1)}, u32[]{:S(2)}) %copy-start.3) | copy-done | bytes 6291480
  142.6 6.2 %products.4.refs_1_ = bf16[512,384]{1,0:T(8,128)(2,1)S(1)} custom-call(bf16[512,6144]{1,0:T(8,128)(2,1)S(1)} %bitcast.10, bf16[192,6144]{1,0:T(8,128)(2,1)S(1)} %collective-permute-done.3.refs_0_, bf16[192,6144]{1,0:T(8,128)(2,1)} %collective-permute-done.5.refs_1_), custom_call_target="tpu_custom_call" | custom-call | flops 2415919104 | bytes 11010048 | tf_op jit(solution)/shard_map/products/pallas_call | solution.py:49
  148.8 10.7 %collective-permute-done.4.refs_0_.refs_2_ = bf16[128,6144]{1,0:T(8,128)(2,1)} collective-permute-done((bf16[128,6144]{1,0:T(8,128)(2,1)}, bf16[128,6144]{1,0:T(8,128)(2,1)}, u32[]{:S(2)}, u32[]{:S(2)}) %collective-permute-start.4) | collective-permute-done | bytes 1572896 | tf_op jit(solution)/shard_map/ppermute | solution.py:167
  159.5 4.9 %products.5 = bf16[512,512]{1,0:T(8,128)(2,1)} custom-call(bf16[512,6144]{1,0:T(8,128)(2,1)S(1)} %bitcast.11, bf16[128,6144]{1,0:T(8,128)(2,1)} %collective-permute-done.4.refs_0_.refs_2_, bf16[512,384]{1,0:T(8,128)(2,1)S(1)} %products.4.refs_1_), custom_call_target="tpu_custom_call" | custom-call | flops 805306368 | bytes 7864320 | tf_op jit(solution)/shard_map/products/pallas_call | solution.py:49
  164.4 5.3 %all-to-all-start.3 = ((bf16[8,64,512]{2,1,0:T(8,128)(2,1)}), bf16[8,64,512]{2,1,0:T(8,128)(2,1)S(1)}, u32[]{:S(2)}, u32[]{:S(2)}) async-start(bf16[8,64,512]{2,1,0:T(8,128)(2,1)} %bitcast.3), calls=%async_computation.3 | async-start | bytes 1048576 | tf_op jit(solution)/shard_map/all_to_all | solution.py:203
  169.7 9.7 %all-to-all-done.3.parts_ref = bf16[8,64,512]{2,1,0:T(8,128)(2,1)S(1)} async-done(((bf16[8,64,512]{2,1,0:T(8,128)(2,1)}), bf16[8,64,512]{2,1,0:T(8,128)(2,1)S(1)}, u32[]{:S(2)}, u32[]{:S(2)}) %all-to-all-start.3) | async-done | bytes 524320 | tf_op jit(solution)/shard_map/all_to_all | solution.py:203
  180.0 13.1 %all_to_all.28 = bf16[8,64,512]{2,1,0:T(8,128)(2,1)S(1)} all-to-all(bf16[8,64,512]{2,1,0:T(8,128)(2,1)S(1)} %amplitudes.3), channel_id=1, replica_groups=mesh['occ'=32,'aux'=8] {'aux'}, dimensions={0} | all-to-all | bytes 1048576 | tf_op jit(solution)/shard_map/all_to_all | solution.py:205
  193.1 2.8 %copy-done.4 = bf16[512,6144]{1,0:T(8,128)(2,1)S(1)} copy-done((bf16[512,6144]{1,0:T(8,128)(2,1)S(1)}, bf16[512,6144]{1,0:T(8,128)(2,1)}, u32[]{:S(2)}) %copy-start.4) | copy-done | bytes 6291480
  195.9 8.9 %last_density.1 = bf16[512,6144]{1,0:T(8,128)(2,1)} custom-call(bf16[512,512]{1,0:T(8,128)(2,1)S(1)} %bitcast.12, bf16[192,6144]{1,0:T(8,128)(2,1)S(1)} %collective-permute-done.3.refs_0_, bf16[192,6144]{1,0:T(8,128)(2,1)} %collective-permute-done.5.refs_1_, bf16[128,6144]{1,0:T(8,128)(2,1)} %collective-permute-done.4.refs_0_.refs_2_, ...), custom_call_target="tpu_custom_call" | custom-call | flops 3221225472 | bytes 18874368 | tf_op jit(solution)/shard_map/last_density/pallas_call | solution.py:140
  (31 shorter events, 1.6 us)
Async XLA Ops:
  0.0 70.7 %collective-permute-start = (bf16[512,6144]{1,0:T(8,128)(2,1)}, bf16[512,6144]{1,0:T(8,128)(2,1)S(1)}, u32[]{:S(2)}, u32[]{:S(2)}) collective-permute-start(bf16[512,6144]{1,0:T(8,128)(2,1)} %bitcast.6), channel_id=1, source_target_pairs={{0,8},{8,16},{16,24},{24,32},{32,40},{40,48},{48,56},{56,64},{64,7... | collective-permute-start | bytes 18874376 | tf_op jit(solution)/shard_map/ppermute | solution.py:167
  0.0 70.7 %collective-permute-start.1 = (f32[32]{0:T(128)}, f32[32]{0:T(128)S(1)}, u32[]{:S(2)}, u32[]{:S(2)}) collective-permute-start(f32[32]{0:T(128)} %param.4), channel_id=1, source_target_pairs={{0,8},{8,16},{16,24},{24,32},{32,40},{40,48},{48,56},{56,64},{64,7... | collective-permute-start | bytes 392 | tf_op jit(solution)/shard_map/ppermute | solution.py:167
  2.0 68.7 %collective-permute-start.2 = (f32[32]{0:T(128)}, f32[32]{0:T(128)S(1)}, u32[]{:S(2)}, u32[]{:S(2)}) collective-permute-start(f32[32]{0:T(128)} %param.4), channel_id=1, source_target_pairs={{0,16},{8,24},{16,32},{24,40},{32,48},{40,56},{48,64},{56,72},{64,... | collective-permute-start | bytes 392 | tf_op jit(solution)/shard_map/ppermute | solution.py:167
  72.3 38.5 %collective-permute-start.3 = (bf16[192,6144]{1,0:T(8,128)(2,1)}, bf16[192,6144]{1,0:T(8,128)(2,1)S(1)}, u32[]{:S(2)}, u32[]{:S(2)}) collective-permute-start(bf16[192,6144]{1,0:T(8,128)(2,1)} %slice.9), channel_id=1, source_target_pairs={{0,8},{8,16},{16,24},{24,32},{32,40},{40,48},{48,56},{56,64},{64,7... | collective-permute-start | bytes 7077896 | tf_op jit(solution)/shard_map/ppermute | solution.py:167
  72.3 2.8 %copy-start = (bf16[32,16,6144]{2,1,0:T(8,128)(2,1)S(1)}, bf16[32,16,6144]{2,1,0:T(8,128)(2,1)}, u32[]{:S(2)}) copy-start(bf16[32,16,6144]{2,1,0:T(8,128)(2,1)} %param.3) | copy-start | bytes 18874372
  79.7 2.7 %copy-start.1 = (bf16[512,6144]{1,0:T(8,128)(2,1)}, bf16[512,6144]{1,0:T(8,128)(2,1)S(1)}, u32[]{:S(2)}) copy-start(bf16[512,6144]{1,0:T(8,128)(2,1)S(1)} %collective-permute-done.refs_0_) | copy-start | bytes 18874372
  114.0 2.8 %copy-start.5 = (f32[32]{0:T(128)S(1)}, f32[32]{0:T(128)}, u32[]{:S(2)}) copy-start(f32[32]{0:T(128)} %param.4) | copy-start | bytes 388
  114.0 2.8 %copy-start.6 = (f32[16]{0:T(128)S(1)}, f32[16]{0:T(128)}, u32[]{:S(2)}) copy-start(f32[16]{0:T(128)} %param.5) | copy-start | bytes 196
  114.0 28.6 %collective-permute-start.5 = (bf16[192,6144]{1,0:T(8,128)(2,1)}, bf16[192,6144]{1,0:T(8,128)(2,1)}, u32[]{:S(2)}, u32[]{:S(2)}) collective-permute-start(bf16[192,6144]{1,0:T(8,128)(2,1)} %slice.11), channel_id=1, source_target_pairs={{0,8},{8,16},{16,24},{24,32},{32,40},{40,48},{48,56},{56,64},{64,7... | collective-permute-start | bytes 7077896 | tf_op jit(solution)/shard_map/ppermute | solution.py:167
  116.9 42.6 %collective-permute-start.4 = (bf16[128,6144]{1,0:T(8,128)(2,1)}, bf16[128,6144]{1,0:T(8,128)(2,1)}, u32[]{:S(2)}, u32[]{:S(2)}) collective-permute-start(bf16[128,6144]{1,0:T(8,128)(2,1)} %slice.10), channel_id=1, source_target_pairs={{0,8},{8,16},{16,24},{24,32},{32,40},{40,48},{48,56},{56,64},{64,7... | collective-permute-start | bytes 4718600 | tf_op jit(solution)/shard_map/ppermute | solution.py:167
  118.0 24.7 %slice-start = ((s8[6291456]{0:T(1024)(128)(4,1)}), s8[4194304]{0:T(1024)(128)(4,1)S(1)}, s32[]{:S(2)}) async-start(s8[6291456]{0:T(1024)(128)(4,1)} %bitcast.8), calls=%async_computation.5 | async-start | bytes 8388608
  132.1 2.8 %copy-start.2 = (bf16[512,6144]{1,0:T(8,128)(2,1)S(1)}, bf16[512,6144]{1,0:T(8,128)(2,1)}, u32[]{:S(2)}) copy-start(bf16[512,6144]{1,0:T(8,128)(2,1)} %copy-done.1) | copy-start | bytes 18874372
  134.9 7.7 %slice-start.1 = ((s8[6291456]{0:T(1024)(128)(4,1)}), s8[2097152]{0:T(1024)(128)(4,1)S(1)}, s32[]{:S(2)}) async-start(s8[6291456]{0:T(1024)(128)(4,1)} %bitcast.8), calls=%async_computation.6 | async-start | bytes 4194304
  139.6 2.7 %copy-start.3 = (bf16[512,6144]{1,0:T(8,128)(2,1)}, bf16[512,6144]{1,0:T(8,128)(2,1)S(1)}, u32[]{:S(2)}) copy-start(bf16[512,6144]{1,0:T(8,128)(2,1)S(1)} %first_density.1.refs_3_) | copy-start | bytes 18874372
  164.4 15.1 %all-to-all-start.3 = ((bf16[8,64,512]{2,1,0:T(8,128)(2,1)}), bf16[8,64,512]{2,1,0:T(8,128)(2,1)S(1)}, u32[]{:S(2)}, u32[]{:S(2)}) async-start(bf16[8,64,512]{2,1,0:T(8,128)(2,1)} %bitcast.3), calls=%async_computation.3 | async-start | bytes 1048576 | tf_op jit(solution)/shard_map/all_to_all | solution.py:203
  193.1 2.8 %copy-start.4 = (bf16[512,6144]{1,0:T(8,128)(2,1)S(1)}, bf16[512,6144]{1,0:T(8,128)(2,1)}, u32[]{:S(2)}) copy-start(bf16[512,6144]{1,0:T(8,128)(2,1)} %copy-done.3) | copy-start | bytes 18874372

commit v6 on v5

--- a/solution.py
+++ b/solution.py
@@ -25,8 +25,8 @@
     return arrays[0] if len(arrays) == 1 else jnp.concatenate(arrays, axis=dim)
 
 
-def product_kernel(tile, n_right, left_ref, *refs):
-    right, before, out_ref, total = refs[:n_right], refs[n_right:-2], refs[-2], refs[-1]
+def product_kernel(tile, left_ref, *refs):
+    right, out_ref, total = refs[:-2], refs[-2], refs[-1]
     total[...] = jnp.zeros_like(total)
 
     def body(step, carry):
@@ -39,17 +39,16 @@
         return carry
 
     lax.fori_loop(0, left_ref.shape[1] // tile, body, 0)
-    out_ref[...] = joined([ref[...] for ref in before] + [total[...].astype(out_ref.dtype)], 1)
-
-
-def products(left, right, tile, before=()):
+    out_ref[...] = total[...].astype(out_ref.dtype)
+
+
+def products(left, right, tile):
     rows, depth = left.shape
     cols = sum(array.shape[0] for array in right)
-    width = cols + sum(array.shape[1] for array in before)
-    return pl.pallas_call(
-        functools.partial(product_kernel, tile, len(right)),
-        out_shape=jax.ShapeDtypeStruct((rows, width), jnp.bfloat16),
-        in_specs=[IN_VMEM] * (1 + len(right) + len(before)),
+    return pl.pallas_call(
+        functools.partial(product_kernel, tile),
+        out_shape=jax.ShapeDtypeStruct((rows, cols), jnp.bfloat16),
+        in_specs=[IN_VMEM] * (1 + len(right)),
         out_specs=IN_VMEM,
         scratch_shapes=[pltpu.VMEM((rows, cols), jnp.float32)],
         compiler_params=pltpu.CompilerParams(vmem_limit_bytes=VMEM_BYTES),
@@ -57,7 +56,7 @@
             flops=2 * rows * cols * depth, bytes_accessed=2 * (rows + cols) * depth, transcendentals=0
         ),
         name="products",
-    )(left, *right, *before)
+    )(left, *right)
 
 
 def swapped(x, width):
@@ -144,7 +143,7 @@
         in_specs=[pl.BlockSpec(amp.shape, lambda c: (0, 0))]
         + [pl.BlockSpec((array.shape[0], tile), lambda c: (0, c)) for array in (*blocks, start)],
         out_specs=pl.BlockSpec((rows, tile), lambda c: (0, c)),
-        compiler_params=pltpu.CompilerParams(vmem_limit_bytes=2 * VMEM_BYTES),
+        compiler_params=pltpu.CompilerParams(vmem_limit_bytes=7 * VMEM_BYTES),
         cost_estimate=pl.CostEstimate(
             flops=2 * rows * rows * cols, bytes_accessed=6 * rows * cols, transcendentals=0
         ),
@@ -161,7 +160,7 @@
     y_groups = [list(range(n_y)), list(range(n_y, n_aux))]
     x_groups = [[i, i + n_y] for i in range(n_y)]
     depth_tile, tile = cols // 6, cols // 8
-    far_rows = [slice(0, 3 * rows // 8), slice(3 * rows // 8, 3 * rows // 4), slice(3 * rows // 4, rows)]
+    second, third = 15 * rows // 32, 3 * rows // 4
 
     def send(value, by=1):
         return lax.ppermute(value, "occ", [(i, (i + by) % n_occ) for i in range(n_occ)])
@@ -179,8 +178,10 @@
     energy_near, energy_far = send(occ_energy), send(occ_energy, 2)
     near = send(own)
     ready = after(near, energy_near, energy_far)
-    first_rows = ready[far_rows[0]]
+    first_rows = ready[:second]
     far = [send(first_rows)]
+    later = after(ready, first_rows)
+    later_rows = [later[second:third], later[third:]]
 
     row = (occ_energy[:, None] - virt_energy[None, :]).reshape(rows, 1)
     near_col = (energy_near[:, None] - virt_energy[None, :]).reshape(1, rows)
@@ -189,17 +190,17 @@
     def share(index, size):
         return lax.dynamic_slice(row, (index * size, 0), (size, 1))
 
-    near_products = products(own, [after(near, first_rows)], depth_tile)
+    near_products = products(own, [after(near, *later_rows)], depth_tile)
     y_sum = total(exchanged(near_products.reshape(n_y, rows // n_y, rows), y_groups))
     near_parts = repeated(y_sum, x_groups)
-    ready = after(ready, near_parts, far[0])
-    far += [send(ready[far_rows[1]]), send(ready[far_rows[2]])]
+    far += [send(after(chunk, near_parts, far[0])) for chunk in later_rows]
     near_slab = amplitudes(near_parts, share(q % n_y, rows // n_y), near_col, slab, n_y)
     amp_near = exchanged(near_slab, y_groups).reshape(rows, rows)
     near_density = first_density(amp_near, [near], tile)
 
     first_products = products(own, [far[0], after(far[1], near_density)], depth_tile)
-    far_products = products(own, [after(far[2], first_products)], depth_tile, (first_products,))
+    last_products = products(own, [after(far[2], first_products)], depth_tile)
+    far_products = jnp.concatenate([first_products, last_products], axis=1)
     far_parts = lax.all_to_all(far_products.reshape(n_aux, rows // n_aux, rows), "aux", 0, 0)
     far_slab = amplitudes(far_parts, share(q, rows // n_aux), far_col, slab, n_aux)
     amp_far = lax.all_to_all(far_slab, "aux", 0, 0).reshape(rows, rows)

time: 206 us -> 203 us (0.985)
  local copies, waits for them, and re-layouts: 21.7 us -> 13.7 us
  blocking collectives: 55.5 us -> 61.1 us
  waiting for transfers between devices: 87.9 us -> 84.4 us
    unnamed x18, local copies, waits for them, and re-layouts: 13.8 us -> 7.69 us
    all_to_all x3, blocking collectives: 42.4 us -> 47.9 us  [exchanged(): return lax.all_to_all(value, 'aux', 0, 0, axis_index_groups=groups)]
    ppermute x6, waiting for transfers between devices: 78.2 us -> 74.7 us  [send(): lax.ppermute(value, 'occ', [(i, (i + by) % n_occ) for i in range(n_occ)])]
    slice x3, local copies, waits for them, and re-layouts: 7.59 us -> 4.74 us  [the longest x2 2.65 us: per_device(): later_rows = [later[second:third], later[third:]]]
    pallas_call x1, Pallas kernels: 8.94 us -> 11.4 us  [last_density(): pl.pallas_call(last_density_kernel, out_shape=jax.ShapeDtypeStruct((rows,...]
  transfers between devices with their start and end apart: 7 -> 7, of which waited for: 4 -> 3; matrix products, arithmetic and copies ran while one was open for 2% -> 2% of each run, Pallas kernels for 8% -> 8%
where the time goes in v6:
time: 203 us; the launch traced here: 202 us
  waiting for transfers between devices  84.4 us (42%)
  blocking collectives  61.1 us (30%)
  Pallas kernels  32 us (16%)
  local copies, waits for them, and re-layouts  13.7 us (7%)
  starting transfers between devices  8.94 us (4%)
    ppermute x6, waiting for transfers between devices, send(): lax.ppermute(value, 'occ', [(i, (i + by) % n_occ) for i in range(n_occ)])  74.7 us
    all_to_all x3, blocking collectives, exchanged(): return lax.all_to_all(value, 'aux', 0, 0, axis_index_groups=groups)  47.9 us
    pallas_call x3, Pallas kernels, products(): pl.pallas_call(functools.partial(product_kernel, tile), out_shape=jax.Sha...  14.6 us
    all_to_all x1, blocking collectives, per_device(): amp_far = lax.all_to_all(far_slab, 'aux', 0, 0).reshape(rows, rows)  13.2 us
    pallas_call x1, Pallas kernels, last_density(): pl.pallas_call(last_density_kernel, out_shape=jax.ShapeDtypeStruct((rows,...  11.4 us
    all_to_all x1, waiting for transfers between devices, per_device(): lax.all_to_all(far_products.reshape(n_aux, rows // n_aux, rows), 'aux', 0...  9.7 us
    unnamed x18, local copies, waits for them, and re-layouts  7.69 us
    all_to_all x1, starting transfers between devices, per_device(): lax.all_to_all(far_products.reshape(n_aux, rows // n_aux, rows), 'aux', 0...  5.31 us
  transfers between devices with their start and end apart: 7, of which 3 were waited for; matrix products, arithmetic and copies ran while one was open for 2% of the time, Pallas kernels for 8%

profile of v6, /device:TPU:2, one launch (start us, length us, event | category | flops | bytes accessed | tf_op | source)
XLA Modules:
  0.0 202.0 jit_solution(1575136195448915169)
XLA Ops:
  0.0 2.0 collective-permute-start.1
  2.0 1.5 collective-permute-start.2
  3.5 67.2 %collective-permute-done.1 = f32[32]{0:T(128)S(1)} collective-permute-done((f32[32]{0:T(128)}, f32[32]{0:T(128)S(1)}, u32[]{:S(2)}, u32[]{:S(2)}) %collective-permute-start.1) | collective-permute-done | bytes 160 | tf_op jit(solution)/shard_map/ppermute | solution.py:166
  70.7 2.1 %slice.9 = bf16[240,6144]{1,0:T(8,128)(2,1)} slice(bf16[512,6144]{1,0:T(8,128)(2,1)S(1)} %collective-permute-done.refs_0_), slice={[0:240], [0:6144]} | slice | bytes 5898240 | tf_op jit(solution)/shard_map/slice | solution.py:181
  72.8 1.3 slice.11
  74.1 1.3 slice.10
  75.8 1.9 copy-done
  77.7 4.6 %products.3 = bf16[512,512]{1,0:T(8,128)(2,1)S(1)} custom-call(bf16[512,6144]{1,0:T(8,128)(2,1)S(1)} %bitcast.7, bf16[512,6144]{1,0:T(8,128)(2,1)S(1)} %collective-permute-done.refs_0_), custom_call_target="tpu_custom_call" | custom-call | flops 3221225472 | bytes 12582912 | tf_op jit(solution)/shard_map/products/pallas_call | solution.py:48
  82.3 14.6 %all_to_all.25 = bf16[4,128,512]{2,1,0:T(8,128)(2,1)S(1)} all-to-all(bf16[4,128,512]{2,1,0:T(8,128)(2,1)S(1)} %bitcast.13), channel_id=1, replica_groups={{0,1,2,3},{4,5,6,7},{8,9,10,11},{12,13,14,15},{16,17,18,19},{20,21,22,2..., dimensions={0} | all-to-all | bytes 1048576 | tf_op jit(solution)/shard_map/all_to_all | solution.py:169
  96.9 0.7 reduce_sum.12
  97.6 0.9 broadcast_in_dim.2
  98.5 19.1 %all_to_all.26.parts_ref = bf16[2,128,512]{2,1,0:T(8,128)(2,1)S(1)} all-to-all(bf16[2,128,512]{2,1,0:T(8,128)(2,1)S(1)} %broadcast_in_dim.2), channel_id=1, replica_groups={{0,4},{1,5},{2,6},{3,7},{8,12},{9,13},{10,14},{11,15},{16,20},{17,21},{..., dimensions={0} | all-to-all | bytes 524288 | tf_op jit(solution)/shard_map/all_to_all | solution.py:169
  118.8 14.2 %all_to_all.27 = bf16[4,128,512]{2,1,0:T(8,128)(2,1)S(1)} all-to-all(bf16[4,128,512]{2,1,0:T(8,128)(2,1)S(1)} %amplitudes.2), channel_id=1, replica_groups={{0,1,2,3},{4,5,6,7},{8,9,10,11},{12,13,14,15},{16,17,18,19},{20,21,22,2..., dimensions={0} | all-to-all | bytes 1048576 | tf_op jit(solution)/shard_map/all_to_all | solution.py:169
  133.0 2.8 %copy-done.2 = bf16[512,6144]{1,0:T(8,128)(2,1)S(1)} copy-done((bf16[512,6144]{1,0:T(8,128)(2,1)S(1)}, bf16[512,6144]{1,0:T(8,128)(2,1)}, u32[]{:S(2)}) %copy-start.2) | copy-done | bytes 6291480
  135.8 4.7 %first_density.1.refs_3_ = bf16[512,6144]{1,0:T(8,128)(2,1)S(1)} custom-call(bf16[512,512]{1,0:T(8,128)(2,1)S(1)} %bitcast.12, bf16[512,6144]{1,0:T(8,128)(2,1)S(1)} %copy-done.2), custom_call_target="tpu_custom_call" | custom-call | flops 3221225472 | bytes 12582912 | tf_op jit(solution)/shard_map/first_density/pallas_call | solution.py:118
  140.6 2.7 %copy-done.3 = bf16[512,6144]{1,0:T(8,128)(2,1)} copy-done((bf16[512,6144]{1,0:T(8,128)(2,1)}, bf16[512,6144]{1,0:T(8,128)(2,1)S(1)}, u32[]{:S(2)}) %copy-start.3) | copy-done | bytes 6291480
  143.2 6.0 %products.4 = bf16[512,384]{1,0:T(8,128)(2,1)S(1)} custom-call(bf16[512,6144]{1,0:T(8,128)(2,1)S(1)} %bitcast.10, bf16[240,6144]{1,0:T(8,128)(2,1)S(1)} %collective-permute-done.3.refs_0_, bf16[144,6144]{1,0:T(8,128)(2,1)} %collective-permute-done.4.refs_1_), custom_call_target="tpu_custom_call" | custom-call | flops 2415919104 | bytes 11010048 | tf_op jit(solution)/shard_map/products/pallas_call | solution.py:48
  149.2 7.5 %collective-permute-done.5.refs_0_.refs_2_ = bf16[128,6144]{1,0:T(8,128)(2,1)} collective-permute-done((bf16[128,6144]{1,0:T(8,128)(2,1)}, bf16[128,6144]{1,0:T(8,128)(2,1)}, u32[]{:S(2)}, u32[]{:S(2)}) %collective-permute-start.5) | collective-permute-done | bytes 1572896 | tf_op jit(solution)/shard_map/ppermute | solution.py:166
  156.7 4.1 %products.5 = bf16[512,128]{1,0:T(8,128)(2,1)S(1)} custom-call(bf16[512,6144]{1,0:T(8,128)(2,1)S(1)} %bitcast.11, bf16[128,6144]{1,0:T(8,128)(2,1)} %collective-permute-done.5.refs_0_.refs_2_), custom_call_target="tpu_custom_call" | custom-call | flops 805306368 | bytes 7864320 | tf_op jit(solution)/shard_map/products/pallas_call | solution.py:48
  160.8 0.8 pad_maximum_fusion
  161.6 5.3 %all-to-all-start.3 = ((bf16[8,64,512]{2,1,0:T(8,128)(2,1)}), bf16[8,64,512]{2,1,0:T(8,128)(2,1)S(1)}, u32[]{:S(2)}, u32[]{:S(2)}) async-start(bf16[8,64,512]{2,1,0:T(8,128)(2,1)} %bitcast.3), calls=%async_computation.3 | async-start | bytes 1048576 | tf_op jit(solution)/shard_map/all_to_all | solution.py:204
  167.0 9.7 %all-to-all-done.3.parts_ref = bf16[8,64,512]{2,1,0:T(8,128)(2,1)S(1)} async-done(((bf16[8,64,512]{2,1,0:T(8,128)(2,1)}), bf16[8,64,512]{2,1,0:T(8,128)(2,1)S(1)}, u32[]{:S(2)}, u32[]{:S(2)}) %all-to-all-start.3) | async-done | bytes 524320 | tf_op jit(solution)/shard_map/all_to_all | solution.py:204
  177.3 13.2 %all_to_all.28 = bf16[8,64,512]{2,1,0:T(8,128)(2,1)} all-to-all(bf16[8,64,512]{2,1,0:T(8,128)(2,1)S(1)} %amplitudes.3), channel_id=1, replica_groups=mesh['occ'=32,'aux'=8] {'aux'}, dimensions={0} | all-to-all | bytes 1048576 | tf_op jit(solution)/shard_map/all_to_all | solution.py:206
  190.5 11.4 %last_density.1 = bf16[512,6144]{1,0:T(8,128)(2,1)} custom-call(bf16[512,512]{1,0:T(8,128)(2,1)} %bitcast.14, bf16[240,6144]{1,0:T(8,128)(2,1)} %copy-done.4, bf16[144,6144]{1,0:T(8,128)(2,1)} %collective-permute-done.4.refs_1_, bf16[128,6144]{1,0:T(8,128)(2,1)} %collective-permute-done.5.refs_0_.refs_2_, bf16[512,6144]{1,0:T(8,128)(2,1)} %copy-done.3), custom_call_target="tpu_custom_call" | custom-call | flops 3221225472 | bytes 18874368 | tf_op jit(solution)/shard_map/last_density/pallas_call | solution.py:139
  (32 shorter events, 2.2 us)
Async XLA Ops:
  0.0 70.7 %collective-permute-start = (bf16[512,6144]{1,0:T(8,128)(2,1)}, bf16[512,6144]{1,0:T(8,128)(2,1)S(1)}, u32[]{:S(2)}, u32[]{:S(2)}) collective-permute-start(bf16[512,6144]{1,0:T(8,128)(2,1)} %bitcast.6), channel_id=1, source_target_pairs={{0,8},{8,16},{16,24},{24,32},{32,40},{40,48},{48,56},{56,64},{64,7... | collective-permute-start | bytes 18874376 | tf_op jit(solution)/shard_map/ppermute | solution.py:166
  0.0 70.7 %collective-permute-start.1 = (f32[32]{0:T(128)}, f32[32]{0:T(128)S(1)}, u32[]{:S(2)}, u32[]{:S(2)}) collective-permute-start(f32[32]{0:T(128)} %param.4), channel_id=1, source_target_pairs={{0,8},{8,16},{16,24},{24,32},{32,40},{40,48},{48,56},{56,64},{64,7... | collective-permute-start | bytes 392 | tf_op jit(solution)/shard_map/ppermute | solution.py:166
  2.0 68.7 %collective-permute-start.2 = (f32[32]{0:T(128)}, f32[32]{0:T(128)S(1)}, u32[]{:S(2)}, u32[]{:S(2)}) collective-permute-start(f32[32]{0:T(128)} %param.4), channel_id=1, source_target_pairs={{0,16},{8,24},{16,32},{24,40},{32,48},{40,56},{48,64},{56,72},{64,... | collective-permute-start | bytes 392 | tf_op jit(solution)/shard_map/ppermute | solution.py:166
  70.7 5.1 %copy-start.1 = (bf16[512,6144]{1,0:T(8,128)(2,1)}, bf16[512,6144]{1,0:T(8,128)(2,1)S(1)}, u32[]{:S(2)}) copy-start(bf16[512,6144]{1,0:T(8,128)(2,1)S(1)} %collective-permute-done.refs_0_) | copy-start | bytes 18874372
  72.8 4.9 %copy-start = (bf16[32,16,6144]{2,1,0:T(8,128)(2,1)S(1)}, bf16[32,16,6144]{2,1,0:T(8,128)(2,1)}, u32[]{:S(2)}) copy-start(bf16[32,16,6144]{2,1,0:T(8,128)(2,1)} %param.3) | copy-start | bytes 18874372
  72.8 44.8 %collective-permute-start.3 = (bf16[240,6144]{1,0:T(8,128)(2,1)}, bf16[240,6144]{1,0:T(8,128)(2,1)S(1)}, u32[]{:S(2)}, u32[]{:S(2)}) collective-permute-start(bf16[240,6144]{1,0:T(8,128)(2,1)} %slice.9), channel_id=1, source_target_pairs={{0,8},{8,16},{16,24},{24,32},{32,40},{40,48},{48,56},{56,64},{64,7... | collective-permute-start | bytes 8847368 | tf_op jit(solution)/shard_map/ppermute | solution.py:166
  77.7 40.0 %copy-start.5 = (f32[32]{0:T(128)S(1)}, f32[32]{0:T(128)}, u32[]{:S(2)}) copy-start(f32[32]{0:T(128)} %param.4) | copy-start | bytes 388
  77.7 40.0 %copy-start.6 = (f32[16]{0:T(128)S(1)}, f32[16]{0:T(128)}, u32[]{:S(2)}) copy-start(f32[16]{0:T(128)} %param.5) | copy-start | bytes 196
  117.6 25.6 %copy-start.4 = (bf16[240,6144]{1,0:T(8,128)(2,1)}, bf16[240,6144]{1,0:T(8,128)(2,1)S(1)}, u32[]{:S(2)}) copy-start(bf16[240,6144]{1,0:T(8,128)(2,1)S(1)} %collective-permute-done.3.refs_0_) | copy-start | bytes 8847364
  117.6 25.6 %collective-permute-start.4 = (bf16[144,6144]{1,0:T(8,128)(2,1)}, bf16[144,6144]{1,0:T(8,128)(2,1)}, u32[]{:S(2)}, u32[]{:S(2)}) collective-permute-start(bf16[144,6144]{1,0:T(8,128)(2,1)} %slice.10), channel_id=1, source_target_pairs={{0,8},{8,16},{16,24},{24,32},{32,40},{40,48},{48,56},{56,64},{64,7... | collective-permute-start | bytes 5308424 | tf_op jit(solution)/shard_map/ppermute | solution.py:166
  117.6 39.1 %collective-permute-start.5 = (bf16[128,6144]{1,0:T(8,128)(2,1)}, bf16[128,6144]{1,0:T(8,128)(2,1)}, u32[]{:S(2)}, u32[]{:S(2)}) collective-permute-start(bf16[128,6144]{1,0:T(8,128)(2,1)} %slice.11), channel_id=1, source_target_pairs={{0,8},{8,16},{16,24},{24,32},{32,40},{40,48},{48,56},{56,64},{64,7... | collective-permute-start | bytes 4718600 | tf_op jit(solution)/shard_map/ppermute | solution.py:166
  118.8 24.4 %slice-start = ((s8[6291456]{0:T(1024)(128)(4,1)}), s8[4194304]{0:T(1024)(128)(4,1)S(1)}, s32[]{:S(2)}) async-start(s8[6291456]{0:T(1024)(128)(4,1)} %bitcast.8), calls=%async_computation.5 | async-start | bytes 8388608
  133.0 2.8 %copy-start.2 = (bf16[512,6144]{1,0:T(8,128)(2,1)S(1)}, bf16[512,6144]{1,0:T(8,128)(2,1)}, u32[]{:S(2)}) copy-start(bf16[512,6144]{1,0:T(8,128)(2,1)} %copy-done.1) | copy-start | bytes 18874372
  135.8 7.4 %slice-start.1 = ((s8[6291456]{0:T(1024)(128)(4,1)}), s8[2097152]{0:T(1024)(128)(4,1)S(1)}, s32[]{:S(2)}) async-start(s8[6291456]{0:T(1024)(128)(4,1)} %bitcast.8), calls=%async_computation.6 | async-start | bytes 4194304
  140.5 2.7 %copy-start.3 = (bf16[512,6144]{1,0:T(8,128)(2,1)}, bf16[512,6144]{1,0:T(8,128)(2,1)S(1)}, u32[]{:S(2)}) copy-start(bf16[512,6144]{1,0:T(8,128)(2,1)S(1)} %first_density.1.refs_3_) | copy-start | bytes 18874372
  161.6 15.1 %all-to-all-start.3 = ((bf16[8,64,512]{2,1,0:T(8,128)(2,1)}), bf16[8,64,512]{2,1,0:T(8,128)(2,1)S(1)}, u32[]{:S(2)}, u32[]{:S(2)}) async-start(bf16[8,64,512]{2,1,0:T(8,128)(2,1)} %bitcast.3), calls=%async_computation.3 | async-start | bytes 1048576 | tf_op jit(solution)/shard_map/all_to_all | solution.py:204

commit v7 on v6

--- a/solution.py
+++ b/solution.py
@@ -25,38 +25,49 @@
     return arrays[0] if len(arrays) == 1 else jnp.concatenate(arrays, axis=dim)
 
 
-def product_kernel(tile, left_ref, *refs):
-    right, out_ref, total = refs[:-2], refs[-2], refs[-1]
-    total[...] = jnp.zeros_like(total)
-
-    def body(step, carry):
-        total[...] += lax.dot_general(
-            part(left_ref, step, tile),
-            joined([part(ref, step, tile) for ref in right], 0),
+def product_kernel(tile, n_sources, *refs):
+    sources, out_ref = refs[:n_sources], refs[n_sources]
+    buffers, total, sems = refs[n_sources + 1:-2], refs[-2], refs[-1]
+    steps = buffers[0].shape[1] // tile
+
+    def copy_in(at, step):
+        columns = pl.ds(step * tile, tile)
+        return pltpu.make_async_copy(sources[at].at[:, columns], buffers[at].at[:, columns], sems.at[at, step])
+
+    for step in range(steps):
+        for at in range(n_sources):
+            copy_in(at, step).start()
+    for step in range(steps):
+        for at in range(n_sources):
+            copy_in(at, step).wait()
+        columns = pl.ds(step * tile, tile)
+        term = lax.dot_general(
+            buffers[0][:, columns],
+            joined([ref[:, columns] for ref in buffers[1:]], 0),
             (((1,), (1,)), ((), ())),
             preferred_element_type=jnp.float32,
         )
-        return carry
-
-    lax.fori_loop(0, left_ref.shape[1] // tile, body, 0)
+        total[...] = term if step == 0 else total[...] + term
     out_ref[...] = total[...].astype(out_ref.dtype)
 
 
 def products(left, right, tile):
     rows, depth = left.shape
     cols = sum(array.shape[0] for array in right)
-    return pl.pallas_call(
-        functools.partial(product_kernel, tile),
+    sources = (left, *right)
+    return pl.pallas_call(
+        functools.partial(product_kernel, tile, len(sources)),
         out_shape=jax.ShapeDtypeStruct((rows, cols), jnp.bfloat16),
-        in_specs=[IN_VMEM] * (1 + len(right)),
+        in_specs=[pl.BlockSpec(memory_space=pl.ANY)] * len(sources),
         out_specs=IN_VMEM,
-        scratch_shapes=[pltpu.VMEM((rows, cols), jnp.float32)],
-        compiler_params=pltpu.CompilerParams(vmem_limit_bytes=VMEM_BYTES),
+        scratch_shapes=[pltpu.VMEM(array.shape, jnp.bfloat16) for array in sources]
+        + [pltpu.VMEM((rows, cols), jnp.float32), pltpu.SemaphoreType.DMA((len(sources), depth // tile))],
+        compiler_params=pltpu.CompilerParams(vmem_limit_bytes=3 * VMEM_BYTES),
         cost_estimate=pl.CostEstimate(
             flops=2 * rows * cols * depth, bytes_accessed=2 * (rows + cols) * depth, transcendentals=0
         ),
         name="products",
-    )(left, *right)
+    )(*sources)
 
 
 def swapped(x, width):
@@ -128,27 +139,64 @@
     )(amp, *blocks)
 
 
-def last_density_kernel(amp_ref, *refs):
-    blocks, start_ref, out_ref = refs[:-2], refs[-2], refs[-1]
-    total = jnp.dot(amp_ref[...], joined([ref[...] for ref in blocks], 0), preferred_element_type=jnp.float32)
-    out_ref[...] = (total + start_ref[...].astype(jnp.float32)).astype(out_ref.dtype)
+def last_density_kernel(tile, n_blocks, *refs):
+    sources, out_ref = refs[:n_blocks + 2], refs[n_blocks + 2]
+    buffers, out_buffer = refs[n_blocks + 3:2 * n_blocks + 5], refs[2 * n_blocks + 5]
+    amp_sem, in_sems, out_sems = refs[2 * n_blocks + 6:]
+    amp, blocks, start = buffers[0], buffers[1:-1], buffers[-1]
+    steps = start.shape[1] // tile
+
+    def columns(step):
+        return pl.ds(step * tile, tile)
+
+    def copy_in(at, step):
+        return pltpu.make_async_copy(
+            sources[at].at[:, columns(step)], buffers[at].at[:, columns(step)], in_sems.at[at - 1, step]
+        )
+
+    def copy_out(step):
+        return pltpu.make_async_copy(out_buffer.at[:, columns(step)], out_ref.at[:, columns(step)], out_sems.at[step])
+
+    copy_amp = pltpu.make_async_copy(sources[0], amp, amp_sem)
+    copy_amp.start()
+    for step in range(steps):
+        for at in range(1, n_blocks + 2):
+            copy_in(at, step).start()
+    copy_amp.wait()
+    for step in range(steps):
+        for at in range(1, n_blocks + 2):
+            copy_in(at, step).wait()
+        total = jnp.dot(
+            amp[...], joined([ref[:, columns(step)] for ref in blocks], 0), preferred_element_type=jnp.float32
+        )
+        out_buffer[:, columns(step)] = (total + start[:, columns(step)].astype(jnp.float32)).astype(out_buffer.dtype)
+        copy_out(step).start()
+    for step in range(steps):
+        copy_out(step).wait()
 
 
 def last_density(amp, blocks, start, tile):
     rows, cols = start.shape
-    return pl.pallas_call(
-        last_density_kernel,
+    sources = (amp, *blocks, start)
+    in_hbm = pl.BlockSpec(memory_space=pl.ANY)
+    return pl.pallas_call(
+        functools.partial(last_density_kernel, tile, len(blocks)),
         out_shape=jax.ShapeDtypeStruct((rows, cols), jnp.bfloat16),
-        grid=(cols // tile,),
-        in_specs=[pl.BlockSpec(amp.shape, lambda c: (0, 0))]
-        + [pl.BlockSpec((array.shape[0], tile), lambda c: (0, c)) for array in (*blocks, start)],
-        out_specs=pl.BlockSpec((rows, tile), lambda c: (0, c)),
+        in_specs=[in_hbm] * len(sources),
+        out_specs=in_hbm,
+        scratch_shapes=[pltpu.VMEM(array.shape, jnp.bfloat16) for array in sources]
+        + [
+            pltpu.VMEM((rows, cols), jnp.bfloat16),
+            pltpu.SemaphoreType.DMA,
+            pltpu.SemaphoreType.DMA((len(blocks) + 1, cols // tile)),
+            pltpu.SemaphoreType.DMA((cols // tile,)),
+        ],
         compiler_params=pltpu.CompilerParams(vmem_limit_bytes=7 * VMEM_BYTES),
         cost_estimate=pl.CostEstimate(
             flops=2 * rows * rows * cols, bytes_accessed=6 * rows * cols, transcendentals=0
         ),
         name="last_density",
-    )(amp, *blocks, start)
+    )(*sources)
 
 
 def per_device(b_factor, occ_energy, virt_energy):

time: 203 us -> 205 us (level)
  Pallas kernels: 32 us -> 35.6 us
  blocking collectives: 61.1 us -> 58.6 us
    pallas_call x4, Pallas kernels: 26 us -> 29.6 us  [the longest x3 18.1 us: products(): pl.pallas_call(functools.partial(product_kernel, tile, len(sources)), out...]
    all_to_all x3, blocking collectives: 47.9 us -> 45.4 us  [exchanged(): return lax.all_to_all(value, 'aux', 0, 0, axis_index_groups=groups)]
  transfers between devices with their start and end apart: 7 -> 7, of which waited for: 3 -> 3; matrix products, arithmetic and copies ran while one was open for 2% -> 2% of each run, Pallas kernels for 8% -> 9%
where the time goes in v7:
time: 205 us; the launch traced here: 203 us
  waiting for transfers between devices  84.6 us (41%)
  blocking collectives  58.6 us (29%)
  Pallas kernels  35.6 us (17%)
  local copies, waits for them, and re-layouts  13.7 us (7%)
  starting transfers between devices  8.94 us (4%)
    ppermute x6, waiting for transfers between devices, send(): lax.ppermute(value, 'occ', [(i, (i + by) % n_occ) for i in range(n_occ)])  74.9 us
    all_to_all x3, blocking collectives, exchanged(): return lax.all_to_all(value, 'aux', 0, 0, axis_index_groups=groups)  45.4 us
    pallas_call x3, Pallas kernels, products(): pl.pallas_call(functools.partial(product_kernel, tile, len(sources)), out...  18.1 us
    all_to_all x1, blocking collectives, per_device(): amp_far = lax.all_to_all(far_slab, 'aux', 0, 0).reshape(rows, rows)  13.2 us
    pallas_call x1, Pallas kernels, last_density(): pl.pallas_call(functools.partial(last_density_kernel, tile, len(blocks)),...  11.5 us
    all_to_all x1, waiting for transfers between devices, per_device(): lax.all_to_all(far_products.reshape(n_aux, rows // n_aux, rows), 'aux', 0...  9.7 us
    unnamed x18, local copies, waits for them, and re-layouts  7.69 us
    all_to_all x1, starting transfers between devices, per_device(): lax.all_to_all(far_products.reshape(n_aux, rows // n_aux, rows), 'aux', 0...  5.31 us
  transfers between devices with their start and end apart: 7, of which 3 were waited for; matrix products, arithmetic and copies ran while one was open for 2% of the time, Pallas kernels for 9%

profile of v7, /device:TPU:2, one launch (start us, length us, event | category | flops | bytes accessed | tf_op | source)
XLA Modules:
  0.0 203.4 jit_solution(397187268370726061)
XLA Ops:
  0.0 2.0 collective-permute-start.1
  2.0 1.5 collective-permute-start.2
  3.5 67.2 %collective-permute-done.1 = f32[32]{0:T(128)S(1)} collective-permute-done((f32[32]{0:T(128)}, f32[32]{0:T(128)S(1)}, u32[]{:S(2)}, u32[]{:S(2)}) %collective-permute-start.1) | collective-permute-done | bytes 160 | tf_op jit(solution)/shard_map/ppermute | solution.py:214
  70.7 2.1 %slice.9 = bf16[240,6144]{1,0:T(8,128)(2,1)} slice(bf16[512,6144]{1,0:T(8,128)(2,1)S(1)} %collective-permute-done.refs_1_.refs_0_), slice={[0:240], [0:6144]} | slice | bytes 5898240 | tf_op jit(solution)/shard_map/slice | solution.py:229
  72.8 1.3 slice.11
  74.1 1.3 slice.10
  75.8 1.9 copy-done
  77.7 7.0 %products.3 = bf16[512,512]{1,0:T(8,128)(2,1)S(1)} custom-call(bf16[512,6144]{1,0:T(8,128)(2,1)S(1)} %bitcast.7, bf16[512,6144]{1,0:T(8,128)(2,1)S(1)} %collective-permute-done.refs_1_.refs_0_), custom_call_target="tpu_custom_call" | custom-call | flops 3221225472 | bytes 12582912 | tf_op jit(solution)/shard_map/products/pallas_call | solution.py:58
  84.7 14.6 %all_to_all.25 = bf16[4,128,512]{2,1,0:T(8,128)(2,1)S(1)} all-to-all(bf16[4,128,512]{2,1,0:T(8,128)(2,1)S(1)} %bitcast.13), channel_id=1, replica_groups={{0,1,2,3},{4,5,6,7},{8,9,10,11},{12,13,14,15},{16,17,18,19},{20,21,22,2..., dimensions={0} | all-to-all | bytes 1048576 | tf_op jit(solution)/shard_map/all_to_all | solution.py:217
  99.3 0.7 reduce_sum.12
  100.0 0.9 broadcast_in_dim.2
  100.9 16.7 %all_to_all.26.parts_ref = bf16[2,128,512]{2,1,0:T(8,128)(2,1)S(1)} all-to-all(bf16[2,128,512]{2,1,0:T(8,128)(2,1)S(1)} %broadcast_in_dim.2), channel_id=1, replica_groups={{0,4},{1,5},{2,6},{3,7},{8,12},{9,13},{10,14},{11,15},{16,20},{17,21},{..., dimensions={0} | all-to-all | bytes 524288 | tf_op jit(solution)/shard_map/all_to_all | solution.py:217
  118.8 14.2 %all_to_all.27 = bf16[4,128,512]{2,1,0:T(8,128)(2,1)S(1)} all-to-all(bf16[4,128,512]{2,1,0:T(8,128)(2,1)S(1)} %amplitudes.2), channel_id=1, replica_groups={{0,1,2,3},{4,5,6,7},{8,9,10,11},{12,13,14,15},{16,17,18,19},{20,21,22,2..., dimensions={0} | all-to-all | bytes 1048576 | tf_op jit(solution)/shard_map/all_to_all | solution.py:217
  133.0 2.8 %copy-done.2 = bf16[512,6144]{1,0:T(8,128)(2,1)S(1)} copy-done((bf16[512,6144]{1,0:T(8,128)(2,1)S(1)}, bf16[512,6144]{1,0:T(8,128)(2,1)}, u32[]{:S(2)}) %copy-start.2) | copy-done | bytes 6291480
  135.8 4.7 %first_density.1.refs_4_ = bf16[512,6144]{1,0:T(8,128)(2,1)S(1)} custom-call(bf16[512,512]{1,0:T(8,128)(2,1)S(1)} %bitcast.12, bf16[512,6144]{1,0:T(8,128)(2,1)S(1)} %copy-done.2), custom_call_target="tpu_custom_call" | custom-call | flops 3221225472 | bytes 12582912 | tf_op jit(solution)/shard_map/first_density/pallas_call | solution.py:129
  140.6 2.7 %copy-done.3 = bf16[512,6144]{1,0:T(8,128)(2,1)} copy-done((bf16[512,6144]{1,0:T(8,128)(2,1)}, bf16[512,6144]{1,0:T(8,128)(2,1)S(1)}, u32[]{:S(2)}) %copy-start.3) | copy-done | bytes 6291480
  143.2 5.8 %products.4 = bf16[512,384]{1,0:T(8,128)(2,1)S(1)} custom-call(bf16[512,6144]{1,0:T(8,128)(2,1)S(1)} %bitcast.10, bf16[240,6144]{1,0:T(8,128)(2,1)S(1)} %collective-permute-done.3.refs_1_, bf16[144,6144]{1,0:T(8,128)(2,1)} %collective-permute-done.4.refs_2_), custom_call_target="tpu_custom_call" | custom-call | flops 2415919104 | bytes 11010048 | tf_op jit(solution)/shard_map/products/pallas_call | solution.py:58
  149.1 7.7 %collective-permute-done.5.refs_1_.refs_3_ = bf16[128,6144]{1,0:T(8,128)(2,1)} collective-permute-done((bf16[128,6144]{1,0:T(8,128)(2,1)}, bf16[128,6144]{1,0:T(8,128)(2,1)}, u32[]{:S(2)}, u32[]{:S(2)}) %collective-permute-start.5) | collective-permute-done | bytes 1572896 | tf_op jit(solution)/shard_map/ppermute | solution.py:214
  156.7 5.3 %products.5 = bf16[512,128]{1,0:T(8,128)(2,1)S(1)} custom-call(bf16[512,6144]{1,0:T(8,128)(2,1)S(1)} %bitcast.11, bf16[128,6144]{1,0:T(8,128)(2,1)} %collective-permute-done.5.refs_1_.refs_3_), custom_call_target="tpu_custom_call" | custom-call | flops 805306368 | bytes 7864320 | tf_op jit(solution)/shard_map/products/pallas_call | solution.py:58
  162.1 0.8 pad_maximum_fusion
  162.9 5.3 %all-to-all-start.3 = ((bf16[8,64,512]{2,1,0:T(8,128)(2,1)}), bf16[8,64,512]{2,1,0:T(8,128)(2,1)S(1)}, u32[]{:S(2)}, u32[]{:S(2)}) async-start(bf16[8,64,512]{2,1,0:T(8,128)(2,1)} %bitcast.3), calls=%async_computation.3 | async-start | bytes 1048576 | tf_op jit(solution)/shard_map/all_to_all | solution.py:252
  168.3 9.7 %all-to-all-done.3.parts_ref = bf16[8,64,512]{2,1,0:T(8,128)(2,1)S(1)} async-done(((bf16[8,64,512]{2,1,0:T(8,128)(2,1)}), bf16[8,64,512]{2,1,0:T(8,128)(2,1)S(1)}, u32[]{:S(2)}, u32[]{:S(2)}) %all-to-all-start.3) | async-done | bytes 524320 | tf_op jit(solution)/shard_map/all_to_all | solution.py:252
  178.6 13.2 %all_to_all.28 = bf16[8,64,512]{2,1,0:T(8,128)(2,1)} all-to-all(bf16[8,64,512]{2,1,0:T(8,128)(2,1)S(1)} %amplitudes.3), channel_id=1, replica_groups=mesh['occ'=32,'aux'=8] {'aux'}, dimensions={0} | all-to-all | bytes 1048576 | tf_op jit(solution)/shard_map/all_to_all | solution.py:254
  191.8 11.5 %last_density.1 = bf16[512,6144]{1,0:T(8,128)(2,1)} custom-call(bf16[512,512]{1,0:T(8,128)(2,1)} %bitcast.14, bf16[240,6144]{1,0:T(8,128)(2,1)} %copy-done.4, bf16[144,6144]{1,0:T(8,128)(2,1)} %collective-permute-done.4.refs_2_, bf16[128,6144]{1,0:T(8,128)(2,1)} %collective-permute-done.5.refs_1_.refs_3_, bf16[512,6144]{1,0:T(8,128)(2,1)} %copy-done.3), custom_call_target="tpu_custom_call" | custom-call | flops 3221225472 | bytes 18874368 | tf_op jit(solution)/shard_map/last_density/pallas_call | solution.py:182
  (32 shorter events, 2.2 us)
Async XLA Ops:
  0.0 70.7 %collective-permute-start = (bf16[512,6144]{1,0:T(8,128)(2,1)}, bf16[512,6144]{1,0:T(8,128)(2,1)S(1)}, u32[]{:S(2)}, u32[]{:S(2)}) collective-permute-start(bf16[512,6144]{1,0:T(8,128)(2,1)} %bitcast.6), channel_id=1, source_target_pairs={{0,8},{8,16},{16,24},{24,32},{32,40},{40,48},{48,56},{56,64},{64,7... | collective-permute-start | bytes 18874376 | tf_op jit(solution)/shard_map/ppermute | solution.py:214
  0.0 70.7 %collective-permute-start.1 = (f32[32]{0:T(128)}, f32[32]{0:T(128)S(1)}, u32[]{:S(2)}, u32[]{:S(2)}) collective-permute-start(f32[32]{0:T(128)} %param.4), channel_id=1, source_target_pairs={{0,8},{8,16},{16,24},{24,32},{32,40},{40,48},{48,56},{56,64},{64,7... | collective-permute-start | bytes 392 | tf_op jit(solution)/shard_map/ppermute | solution.py:214
  2.0 68.7 %collective-permute-start.2 = (f32[32]{0:T(128)}, f32[32]{0:T(128)S(1)}, u32[]{:S(2)}, u32[]{:S(2)}) collective-permute-start(f32[32]{0:T(128)} %param.4), channel_id=1, source_target_pairs={{0,16},{8,24},{16,32},{24,40},{32,48},{40,56},{48,64},{56,72},{64,... | collective-permute-start | bytes 392 | tf_op jit(solution)/shard_map/ppermute | solution.py:214
  70.7 5.1 %copy-start.1 = (bf16[512,6144]{1,0:T(8,128)(2,1)}, bf16[512,6144]{1,0:T(8,128)(2,1)S(1)}, u32[]{:S(2)}) copy-start(bf16[512,6144]{1,0:T(8,128)(2,1)S(1)} %collective-permute-done.refs_1_.refs_0_) | copy-start | bytes 18874372
  72.8 4.9 %copy-start = (bf16[32,16,6144]{2,1,0:T(8,128)(2,1)S(1)}, bf16[32,16,6144]{2,1,0:T(8,128)(2,1)}, u32[]{:S(2)}) copy-start(bf16[32,16,6144]{2,1,0:T(8,128)(2,1)} %param.3) | copy-start | bytes 18874372
  72.8 44.8 %collective-permute-start.3 = (bf16[240,6144]{1,0:T(8,128)(2,1)}, bf16[240,6144]{1,0:T(8,128)(2,1)S(1)}, u32[]{:S(2)}, u32[]{:S(2)}) collective-permute-start(bf16[240,6144]{1,0:T(8,128)(2,1)} %slice.9), channel_id=1, source_target_pairs={{0,8},{8,16},{16,24},{24,32},{32,40},{40,48},{48,56},{56,64},{64,7... | collective-permute-start | bytes 8847368 | tf_op jit(solution)/shard_map/ppermute | solution.py:214
  77.7 40.0 %copy-start.5 = (f32[32]{0:T(128)S(1)}, f32[32]{0:T(128)}, u32[]{:S(2)}) copy-start(f32[32]{0:T(128)} %param.4) | copy-start | bytes 388
  77.7 40.0 %copy-start.6 = (f32[16]{0:T(128)S(1)}, f32[16]{0:T(128)}, u32[]{:S(2)}) copy-start(f32[16]{0:T(128)} %param.5) | copy-start | bytes 196
  117.6 25.6 %copy-start.4 = (bf16[240,6144]{1,0:T(8,128)(2,1)}, bf16[240,6144]{1,0:T(8,128)(2,1)S(1)}, u32[]{:S(2)}) copy-start(bf16[240,6144]{1,0:T(8,128)(2,1)S(1)} %collective-permute-done.3.refs_1_) | copy-start | bytes 8847364
  117.6 25.6 %collective-permute-start.4 = (bf16[144,6144]{1,0:T(8,128)(2,1)}, bf16[144,6144]{1,0:T(8,128)(2,1)}, u32[]{:S(2)}, u32[]{:S(2)}) collective-permute-start(bf16[144,6144]{1,0:T(8,128)(2,1)} %slice.10), channel_id=1, source_target_pairs={{0,8},{8,16},{16,24},{24,32},{32,40},{40,48},{48,56},{56,64},{64,7... | collective-permute-start | bytes 5308424 | tf_op jit(solution)/shard_map/ppermute | solution.py:214
  117.6 39.1 %collective-permute-start.5 = (bf16[128,6144]{1,0:T(8,128)(2,1)}, bf16[128,6144]{1,0:T(8,128)(2,1)}, u32[]{:S(2)}, u32[]{:S(2)}) collective-permute-start(bf16[128,6144]{1,0:T(8,128)(2,1)} %slice.11), channel_id=1, source_target_pairs={{0,8},{8,16},{16,24},{24,32},{32,40},{40,48},{48,56},{56,64},{64,7... | collective-permute-start | bytes 4718600 | tf_op jit(solution)/shard_map/ppermute | solution.py:214
  118.8 24.4 %slice-start = ((s8[6291456]{0:T(1024)(128)(4,1)}), s8[4194304]{0:T(1024)(128)(4,1)S(1)}, s32[]{:S(2)}) async-start(s8[6291456]{0:T(1024)(128)(4,1)} %bitcast.8), calls=%async_computation.5 | async-start | bytes 8388608
  133.0 2.8 %copy-start.2 = (bf16[512,6144]{1,0:T(8,128)(2,1)S(1)}, bf16[512,6144]{1,0:T(8,128)(2,1)}, u32[]{:S(2)}) copy-start(bf16[512,6144]{1,0:T(8,128)(2,1)} %copy-done.1) | copy-start | bytes 18874372
  135.8 7.4 %slice-start.1 = ((s8[6291456]{0:T(1024)(128)(4,1)}), s8[2097152]{0:T(1024)(128)(4,1)S(1)}, s32[]{:S(2)}) async-start(s8[6291456]{0:T(1024)(128)(4,1)} %bitcast.8), calls=%async_computation.6 | async-start | bytes 4194304
  140.5 2.7 %copy-start.3 = (bf16[512,6144]{1,0:T(8,128)(2,1)}, bf16[512,6144]{1,0:T(8,128)(2,1)S(1)}, u32[]{:S(2)}) copy-start(bf16[512,6144]{1,0:T(8,128)(2,1)S(1)} %first_density.1.refs_4_) | copy-start | bytes 18874372
  162.9 15.1 %all-to-all-start.3 = ((bf16[8,64,512]{2,1,0:T(8,128)(2,1)}), bf16[8,64,512]{2,1,0:T(8,128)(2,1)S(1)}, u32[]{:S(2)}, u32[]{:S(2)}) async-start(bf16[8,64,512]{2,1,0:T(8,128)(2,1)} %bitcast.3), calls=%async_computation.3 | async-start | bytes 1048576 | tf_op jit(solution)/shard_map/all_to_all | solution.py:252
